TPU v7x, 256 devices: a whole 4x4x8 slice. The times are simulated.
256 devices in a mesh: aux: 8 (over z), pair: 32 (over x, y, core).
Axes of the slice: x: 4, y: 4, z: 8, core: 2. Of those that a mesh axis runs over, the one named last changes fastest.
Arguments:
- dfints: bfloat16 [8192, 256, 128], P('aux', 'pair'), may hold values from -0.625 to 0.625
- projectors: bfloat16 [4352, 128, 128], P('pair'), may hold values from -0.5 to 0.5
- pairs: int32 [4352, 2], P('pair'), may hold values from 0 to 255, as said below
- pno_energy: float32 [4352, 64], P('pair'), may hold values from 0.3 to 3
- occ_energy: float32 [256], replicated, may hold values from -1.2 to -0.3
Outputs:
- amplitudes: float32 [4352, 4096], P('pair', 'aux')
Inputs may be any that keep to these rules, and one draw needn't show every extreme that they name: `pairs`: orbital o is owned by device o // 8 of pair. In each device's aligned block of 136 rows, i is always owned by that device; rows k < 128 name as j one and the same orbital for all k with equal k // 4, owned by device k // 4; the other 8 rows name a j owned by the device itself, and the block's last row names its device's last orbital as j.
All inputs are finite; a program needn't handle non-finite values.
Results may differ from a plain program's by a relative error of at most 0.003.
Values may be sent and summed in bfloat16 or wider, within the bound.
No kernel may reach another device: no remote copies, remote signals or barrier semaphores. Data moves between devices by JAX's collectives and lax.ppermute only.
A program may use at most 192 MiB of HBM per device.

v0:
```python
import functools

import jax
import jax.numpy as jnp
from jax import lax
from jax.experimental import pallas as pl
from jax.experimental.pallas import tpu as pltpu
from jax.sharding import PartitionSpec as P

GROUP = 4
SIDE = 4
CORES = 2
RELS = (0, 1, -1, 2)
TARGETS = tuple((shift, core) for shift in RELS for core in range(CORES))
SMEM = pl.BlockSpec(memory_space=pltpu.SMEM)
EXTRA = 16
SLOTS = 6
VMEM = pl.BlockSpec(memory_space=pltpu.VMEM)
ANY = pl.BlockSpec(memory_space=pl.ANY)
NEAR = [(dx, dy, c) for dx in RELS for dy in RELS for c in range(CORES) if 2 not in (dx, dy)]
FAR = [(dx, dy, c) for dx in RELS for dy in RELS for c in range(CORES) if 2 in (dx, dy)]


def params(mib=12):
    return pltpu.CompilerParams(vmem_limit_bytes=mib * 1024 * 1024)


def back(shift):
    return shift if shift in (0, 2) else -shift


def my_place():
    me = lax.axis_index("pair")
    return me // (CORES * SIDE), me // CORES % SIDE, me % CORES


def group_of(place, dx, dy, core):
    x, y, c = place[0] + dx, place[1] + dy, place[2] + core
    return (((x + SIDE) % SIDE) * SIDE + (y + SIDE) % SIDE) * CORES + c % CORES


def by_orbital_kernel(blocks_ref, wanted_ref, other_ref, first_ref, second_ref, wide_ref):
    aux_rows, orbs, domain = blocks_ref.shape
    rows = wide_ref.shape[0] // orbs
    half = aux_rows // 2
    line = lax.broadcasted_iota(jnp.int32, wanted_ref.shape, 0)
    requests = jnp.where(
        line == 0, wanted_ref[...].astype(jnp.float32), other_ref[...].astype(jnp.float32)
    ).astype(jnp.bfloat16)
    for out_ref, start in ((first_ref, 0), (second_ref, half)):
        for at in range(0, half, rows):
            wide_ref[...] = (
                blocks_ref[pl.ds(start + at, rows)].astype(jnp.float32).reshape(rows * orbs, domain)
            )
            for orb in range(orbs):
                out_ref[orb, pl.ds(at, rows), :] = wide_ref[
                    pl.ds(orb, rows, stride=orbs), :
                ].astype(jnp.bfloat16)
        for orb in range(orbs):
            out_ref[orb, pl.ds(half, EXTRA), :] = requests


def by_orbital(dfints, wanted, other):
    aux_rows, orbs, domain = dfints.shape
    shape = jax.ShapeDtypeStruct((orbs, aux_rows // 2 + EXTRA, domain), dfints.dtype)
    return pl.pallas_call(
        by_orbital_kernel,
        in_specs=[VMEM] * 3,
        out_specs=[VMEM, VMEM],
        out_shape=[shape, shape],
        scratch_shapes=[pltpu.VMEM((128 * orbs, domain), jnp.float32)],
        compiler_params=params(),
        name="by_orbital",
    )(dfints, wanted, other)


def cut_kernel(first_less, first_more, second_less, second_more, _, *out_refs):
    half = out_refs[0].shape[0]
    for n, (less_ref, more_ref) in enumerate(((first_less, first_more), (second_less, second_more))):
        out_refs[2 * n][...] = less_ref[:half]
        out_refs[2 * n + 1][...] = more_ref[half:]


def cut(less, more, behind):
    orbs, rows, domain = less[0].shape
    shape = jax.ShapeDtypeStruct((orbs // 2, rows, domain), less[0].dtype)
    return pl.pallas_call(
        cut_kernel,
        in_specs=[VMEM] * 4 + [ANY],
        out_specs=[VMEM] * 4,
        out_shape=[shape] * 4,
        compiler_params=params(),
        name="cut",
    )(less[0], more[0], less[1], more[1], behind)


def choose_kernel(work, *refs):
    gathered, refs = (refs[:5], refs[5:10]), refs[10:]
    out_refs, (seen_ref, asked_ref, sem) = refs[: len(work)], refs[len(work) :]
    place = my_place()
    half = gathered[0][3].shape[0]
    rows = gathered[0][0].shape[1] - EXTRA
    for along in range(2):
        own_ref, less_ref, more_ref, low_ref, _ = gathered[1 - along]
        for n, shift in enumerate(RELS):
            ref = {0: own_ref, 1: more_ref, -1: less_ref, 2: low_ref}[shift]
            lines = ref[0, pl.ds(rows, EXTRA), :].astype(jnp.float32)[:8]
            seen_ref[along * SIDE + n] = lines.astype(jnp.int32)
    copy = pltpu.make_async_copy(seen_ref, asked_ref, sem)
    copy.start()
    copy.wait()
    for out_ref, (along, shift, core) in zip(out_refs, work):
        own_ref, less_ref, more_ref, low_ref, high_ref = gathered[along]
        table = along * SIDE + RELS.index(shift)
        for r, rel in enumerate(RELS):
            owner = group_of(place, *((rel, 0) if along == 0 else (0, rel)), 0)
            asked = asked_ref[table, core, owner]
            if rel != 2:
                source = {0: own_ref, -1: less_ref, 1: more_ref}[rel]
                out_ref[r] = source[asked, pl.ds(0, rows), :]
                continue

            @pl.when(asked < half)
            def _():
                out_ref[r] = low_ref[jnp.minimum(asked, half - 1), pl.ds(0, rows), :]

            @pl.when(asked >= half)
            def _():
                out_ref[r] = high_ref[jnp.maximum(asked - half, 0), pl.ds(0, rows), :]


def choose(work, gathered):
    own = gathered[0][0]
    _, rows, domain = own.shape
    shape = jax.ShapeDtypeStruct((len(RELS), rows - EXTRA, domain), own.dtype)
    tables = (2 * SIDE, 8, domain)
    return pl.pallas_call(
        functools.partial(choose_kernel, work),
        in_specs=[VMEM] * 10,
        out_specs=[VMEM] * len(work),
        out_shape=[shape] * len(work),
        scratch_shapes=[
            pltpu.VMEM(tables, jnp.int32),
            pltpu.SMEM(tables, jnp.int32),
            pltpu.SemaphoreType.DMA(()),
        ],
        compiler_params=params(),
        name="choose",
    )(*gathered[0], *gathered[1])


def right_coeffs(projectors_ref, start, count):
    width = projectors_ref.shape[2] // 2
    return jnp.concatenate([projectors_ref[start + k][:, width:] for k in range(count)], axis=1)


def merge(even, odd):
    lane = lax.broadcasted_iota(jnp.int32, even.shape, 1)
    return jnp.where(lane < even.shape[1] // 2, even, odd)


def put(out_ref, at, blocks, base_ref=None, base_at=0):
    pieces = out_ref.shape[0]
    rows = blocks[0].shape[0] // pieces
    for piece in range(pieces):
        part = jnp.concatenate([one[piece * rows : (piece + 1) * rows] for one in blocks], axis=0)
        if base_ref is not None:
            part = part + base_ref[piece, base_at]
        out_ref[piece, at] = part.astype(out_ref.dtype)


def left_kernel(
    left_index, right_index, first_ref, second_ref, projectors_ref, out_ref, own_ref,
    made, out_sem
):
    groups = projectors_ref.shape[0] // GROUP
    batch, _, wide, half = made.shape[1:]
    width = wide // GROUP
    steps = groups // batch
    halves = (first_ref, second_ref)

    def copy_out(s, slot):
        return pltpu.make_async_copy(
            made.at[slot], out_ref.at[pl.ds(s * batch, batch)], out_sem.at[slot]
        )

    def step(s, _):
        slot = s % 2

        @pl.when(s >= 2)
        def _():
            copy_out(0, slot).wait()

        for k in range(batch * GROUP):
            pair = s * batch * GROUP + k
            lefts = projectors_ref[pair].T[:width]
            orb = left_index[pair]
            for n, part_ref in enumerate(halves):
                made[slot, k // GROUP, n, pl.ds(k % GROUP * width, width), :] = lax.dot_general(
                    lefts,
                    part_ref[orb, pl.ds(0, half), :],
                    (((1,), (1,)), ((), ())),
                    preferred_element_type=jnp.float32,
                ).astype(jnp.bfloat16)
        copy_out(s, slot).start()
        return 0

    lax.fori_loop(0, steps, step, 0)
    slot = (steps - 1) % 2
    own = own_ref.shape[1]
    for n in range(own):
        blocks = []
        at = batch - own + n
        for pair in range(0, GROUP, 2):
            rights = right_coeffs(projectors_ref, (groups - own + n) * GROUP + pair, 2)
            totals = []
            for k in (pair, pair + 1):
                orb = right_index[(groups - own + n) * GROUP + k]
                total = 0.0
                for m, part_ref in enumerate(halves):
                    right = jnp.dot(
                        part_ref[orb, pl.ds(0, half), :], rights, preferred_element_type=jnp.float32
                    ).astype(jnp.bfloat16)
                    total += jnp.dot(
                        made[slot, at, m, pl.ds(k * width, width), :],
                        right,
                        preferred_element_type=jnp.float32,
                    )
                totals.append(total)
            blocks.append(merge(*totals))
        put(own_ref, n, blocks)
    for one in range(2):
        copy_out(0, one).wait()


def left_of(left_index, right_index, first, second, projectors, pieces):
    half = first.shape[1] - EXTRA
    pair_rows, _, both = projectors.shape
    groups = pair_rows // GROUP
    own = groups - len(NEAR) - len(FAR)
    batch = 2
    wide = GROUP * both // 2
    return pl.pallas_call(
        left_kernel,
        in_specs=[SMEM] * 2 + [VMEM] * 3,
        out_specs=[ANY, VMEM],
        out_shape=[
            jax.ShapeDtypeStruct((pair_rows, 2, wide, half), jnp.bfloat16),
            sums_shape(own, pieces, both, jnp.bfloat16),
        ],
        scratch_shapes=[
            pltpu.VMEM((2, batch, 2, wide, half), jnp.bfloat16),
            pltpu.SemaphoreType.DMA((2,)),
        ],
        compiler_params=params(),
        name="left",
    )(left_index, right_index, first, second, projectors)


def sums_shape(count, pieces, both, dtype):
    return jax.ShapeDtypeStruct((pieces, count, both // pieces, both), dtype)


def entry_of(along, shift, core, rel):
    return (rel, back(shift), core) if along == 0 else (back(shift), rel, core)


def parts_of(work):
    return {
        (entry_of(along, shift, core, rel), along): (n, r)
        for n, (along, shift, core) in enumerate(work)
        for r, rel in enumerate(RELS)
    }


def add_up(work, targets, left_ref, projectors_ref, block_refs, lefts, sem):
    slots, _, wide, _ = lefts.shape
    width = wide // GROUP
    place = my_place()
    parts = parts_of(work)
    todo = []
    for groups, out_ref, start, base_ref in targets:
        for at, entry in enumerate(groups):
            alongs = [along for along in range(2) if (entry, along) in parts]
            if alongs:
                base = base_ref if len(alongs) == 1 else None
                todo.append((entry, alongs, out_ref, start + at, base, at))

    def copy_in(n):
        entry, alongs = todo[n][:2]
        group, slot = group_of(place, *entry), n % slots
        if len(alongs) == 2:
            return pltpu.make_async_copy(left_ref.at[group], lefts.at[slot], sem.at[slot])
        along = alongs[0]
        return pltpu.make_async_copy(
            left_ref.at[group, along], lefts.at[slot, along], sem.at[slot]
        )

    for n in range(slots - 1):
        copy_in(n).start()
    for n, (entry, alongs, out_ref, at, base_ref, base_at) in enumerate(todo):
        slot = n % slots
        if n + slots - 1 < len(todo):
            copy_in(n + slots - 1).start()
        copy_in(n).wait()
        rights = right_coeffs(projectors_ref, group_of(place, *entry) * GROUP, GROUP)
        mixed = 0.0
        for along in alongs:
            number, r = parts[entry, along]
            right = jnp.dot(
                block_refs[number][r], rights, preferred_element_type=jnp.float32
            ).astype(jnp.bfloat16)
            mixed += jnp.dot(lefts[slot, along], right, preferred_element_type=jnp.float32)
        blocks = []
        for k in range(0, GROUP, 2):
            columns = slice(k * width, (k + 2) * width)
            blocks.append(
                merge(
                    mixed[k * width : (k + 1) * width, columns],
                    mixed[(k + 1) * width : (k + 2) * width, columns],
                )
            )
        put(out_ref, at, blocks, base_ref, base_at)


def near_kernel(work, left_ref, projectors_ref, own_ref, *refs):
    near_ref, far_ref, lefts, sem = refs[len(work) :]
    near_ref[:, len(NEAR) :] = own_ref[...]
    targets = [(NEAR, near_ref, 0, None), (FAR, far_ref, 0, None)]
    add_up(work, targets, left_ref, projectors_ref, refs[: len(work)], lefts, sem)


def far_kernel(work, left_ref, projectors_ref, near_ref, begun_ref, *refs):
    out_ref, lefts, sem = refs[len(work) :]
    count = near_ref.shape[1]
    out_ref[:, :count] = near_ref[...]
    targets = [(FAR, out_ref, count, begun_ref)]
    add_up(work, targets, left_ref, projectors_ref, refs[: len(work)], lefts, sem)


def left_slots(left):
    return [
        pltpu.VMEM((SLOTS,) + left.shape[1:], left.dtype),
        pltpu.SemaphoreType.DMA((SLOTS,)),
    ]


def near_exchange(work, left, projectors, own, blocks):
    pieces, own_rows, _, both = own.shape
    return pl.pallas_call(
        functools.partial(near_kernel, work),
        in_specs=[ANY] + [VMEM] * (2 + len(work)),
        out_specs=[VMEM, VMEM],
        out_shape=[
            sums_shape(len(NEAR) + own_rows, pieces, both, own.dtype),
            sums_shape(len(FAR), pieces, both, jnp.float32),
        ],
        scratch_shapes=left_slots(left),
        compiler_params=params(),
        name="near_exchange",
    )(left, projectors, own, *blocks)


def far_exchange(work, left, projectors, near, begun, blocks):
    pieces, near_rows, _, both = near.shape
    return pl.pallas_call(
        functools.partial(far_kernel, work),
        in_specs=[ANY] + [VMEM] * (3 + len(work)),
        out_specs=VMEM,
        out_shape=sums_shape(near_rows + len(FAR), pieces, both, near.dtype),
        scratch_shapes=left_slots(left),
        compiler_params=params(),
        name="far_exchange",
    )(left, projectors, near, begun, *blocks)


def finish_kernel(arrived_ref, denom_ref, out_ref, share_ref, rows_ref):
    width = arrived_ref.shape[3] // 2
    parts = share_ref.shape[1]
    lane = lax.broadcasted_iota(jnp.int32, (1, 2 * width), 1)
    total = arrived_ref[0].astype(jnp.float32)
    for piece in range(1, arrived_ref.shape[0]):
        total += arrived_ref[piece].astype(jnp.float32)
    share_ref[...] = total.reshape(share_ref.shape)
    for part in range(0, parts, 2):
        even, odd = share_ref[:, part, :], share_ref[:, part + 1, :]
        columns = pl.ds(part * width, 2 * width)
        rows_ref[0, :, columns] = jnp.where(lane < width, even, pltpu.roll(odd, width, 1))
        rows_ref[1, :, columns] = jnp.where(lane < width, pltpu.roll(even, width, 1), odd)
    shared = len(NEAR) + len(FAR)
    own = arrived_ref.shape[1] - shared
    place = my_place()
    groups = [group_of(place, *entry) for entry in NEAR]
    groups += [shared + n for n in range(own)]
    groups += [group_of(place, *entry) for entry in FAR]
    for n, group in enumerate(groups):
        for k in range(GROUP):
            row = pl.ds(group * GROUP + k, 1)
            out_ref[row, :] = (
                -rows_ref[k % 2, pl.ds(2 * n + k // 2, 1), :] / denom_ref[row, :]
            )


def finish(arrived, denom):
    pieces, _, _, both = arrived.shape
    parts = both // 2 // pieces
    pair_rows = denom.shape[0]
    return pl.pallas_call(
        finish_kernel,
        in_specs=[VMEM] * 2,
        out_specs=VMEM,
        out_shape=jax.ShapeDtypeStruct(denom.shape, jnp.float32),
        scratch_shapes=[
            pltpu.VMEM((pair_rows // 2, parts, both), jnp.float32),
            pltpu.VMEM((2, pair_rows // 2, parts * both // 2), jnp.float32),
        ],
        compiler_params=params(),
        name="finish",
    )(arrived, denom)


def denominators_kernel(first_index, second_index, occ_ref, energy_ref, out_ref, base_ref):
    pair_rows, width = energy_ref.shape
    parts = out_ref.shape[1] // width
    energy = energy_ref[...]
    lane = lax.broadcasted_iota(jnp.int32, energy.shape, 1)
    wide = lax.broadcasted_iota(jnp.int32, (pair_rows, 2 * width), 1)
    twice = jnp.concatenate([energy, energy], axis=1)
    start = lax.axis_index("aux") * parts
    for part in range(0, parts, 2):
        even, odd = [
            jnp.sum(jnp.where(lane == start + part + n, energy, 0.0), axis=1, keepdims=True)
            for n in range(2)
        ]
        base_ref[:, pl.ds(part * width, 2 * width)] = twice + jnp.where(wide < width, even, odd)

    def step(pair, _):
        occupied = occ_ref[first_index[pair]] + occ_ref[second_index[pair]]
        row = pl.ds(pair, 1)
        out_ref[row, :] = base_ref[row, :] - occupied
        return 0

    lax.fori_loop(0, pair_rows, step, 0, unroll=8)


def denominators(first_index, second_index, occ_energy, pno_energy, pieces):
    pair_rows, width = pno_energy.shape
    shape = (pair_rows, width // pieces * width)
    return pl.pallas_call(
        denominators_kernel,
        in_specs=[SMEM] * 3 + [VMEM],
        out_specs=VMEM,
        out_shape=jax.ShapeDtypeStruct(shape, jnp.float32),
        scratch_shapes=[pltpu.VMEM(shape, jnp.float32)],
        compiler_params=params(4),
        name="denominators",
    )(first_index, second_index, occ_energy, pno_energy)


def after(array, other):
    return pl.pallas_call(
        lambda *_: None,
        in_specs=[ANY, ANY],
        out_specs=ANY,
        out_shape=jax.ShapeDtypeStruct(array.shape, array.dtype),
        input_output_aliases={0: 0},
        compiler_params=params(1),
        name="after",
    )(array, other)


def moved(array, dx, dy, core):
    def at(x, y, c):
        return ((x % SIDE) * SIDE + y % SIDE) * CORES + c % CORES

    return lax.ppermute(
        array,
        "pair",
        [
            (at(x, y, c), at(x + dx, y + dy, c + core))
            for x in range(SIDE)
            for y in range(SIDE)
            for c in range(CORES)
        ],
    )


def step_along(along, array, shift, core=0):
    return moved(array, *((shift, 0) if along == 0 else (0, shift)), core)


def on_device(dfints, projectors, pairs, pno_energy, occ_energy):
    orb_count, domain = dfints.shape[1:]
    ranks = lax.axis_size("pair")
    pieces = lax.axis_size("aux")
    left_local = pairs[:, 0] % orb_count
    right_local = pairs[:, 1] % orb_count
    wanted = right_local[: ranks * GROUP : GROUP].astype(dfints.dtype)
    wanted = jnp.broadcast_to(jnp.pad(wanted, (0, domain - ranks))[None], (EXTRA, domain))
    halves = by_orbital(dfints, wanted, moved(wanted, 0, 0, 1))

    denom = denominators(pairs[:, 0], pairs[:, 1], occ_energy, pno_energy, pieces)
    less = [step_along(along, own, 1) for along, own in enumerate(halves)]
    more = [step_along(along, own, -1) for along, own in enumerate(halves)]
    left, own = left_of(left_local, right_local, *halves, projectors, pieces)
    pieces_on = cut(less, more, own)
    low = [step_along(along, pieces_on[2 * along], 1) for along in range(2)]
    high = [step_along(along, pieces_on[2 * along + 1], -1) for along in range(2)]
    gathered = list(zip(halves, less, more, low, high))

    def work_of(*shifts):
        return tuple((along, shift, core) for shift, core in shifts for along in range(2))

    near_work = work_of((1, 0), (-1, 0), (0, 0), (0, 1), (1, 1), (-1, 1))
    far_work = work_of((2, 0), (2, 1))
    chosen = dict(zip(near_work + far_work, choose(near_work + far_work, gathered)))
    follows = {(1, 1): (1, 0), (-1, 1): (-1, 0), (2, 0): (1, 1), (2, 1): (-1, 1)}
    arrived = {}
    for along, shift, core in near_work + far_work:
        one = chosen[along, shift, core]
        if (shift, core) in follows:
            one = after(one, arrived[(along, *follows[shift, core])])
        if (shift, core) != (0, 0):
            one = step_along(1 - along, one, shift, core)
        arrived[along, shift, core] = one
    near, begun = near_exchange(near_work, left, projectors, own, [arrived[one] for one in near_work])
    sums = far_exchange(
        far_work, left, projectors, near, begun, [arrived[one] for one in far_work]
    )
    sums = lax.all_to_all(sums, "aux", split_axis=0, concat_axis=0, tiled=True)
    return finish(sums, denom)


def solution(mesh):
    in_specs = (
        P("aux", "pair", None),
        P("pair", None, None),
        P("pair", None),
        P("pair", None),
        P(),
    )
    out_specs = P("pair", "aux")
    return jax.shard_map(
        on_device, mesh=mesh, in_specs=in_specs, out_specs=out_specs, check_vma=False
    )
```

profile of v0, /device:TPU:1, one launch (start us, length us, event | category | flops | bytes accessed | tf_op | source)
XLA Modules:
  0.0 161.6 jit_solution(16961994392827364685)
XLA Ops:
  0.9 3.3 %collective-permute-start = (bf16[16,128]{1,0:T(8,128)(2,1)S(1)}, bf16[16,128]{1,0:T(8,128)(2,1)S(1)}, u32[]{:S(2)}, u32[]{:S(2)}) collective-permute-start(bf16[16,128]{1,0:T(8,128)(2,1)S(1)} %broadcast_in_dim.2.wanted_ref), channel_id=1, source_target_pairs={{0,1},{1,0},{2,3},{3,2},{4,5},{5,4},{6,7},{7,6},{8,9},{9,8},{10,11... | collective-permute-start | bytes 12296 | tf_op jit(solution)/shard_map/ppermute | solution.py:476
  7.7 2.7 %collective-permute-start.2 = (bf16[8,528,128]{2,1,0:T(8,128)(2,1)S(1)}, bf16[8,528,128]{2,1,0:T(8,128)(2,1)S(1)}, u32[]{:S(2)}, u32[]{:S(2)}) collective-permute-start(bf16[8,528,128]{2,1,0:T(8,128)(2,1)S(1)} %get-tuple-element.31.first_ref.refs_0_), channel_id=1, source_target_pairs={{0,24},{1,25},{2,26},{3,27},{4,28},{5,29},{6,30},{7,31},{8,0},{9,1... | collective-permute-start | bytes 3244040 | tf_op jit(solution)/shard_map/ppermute | solution.py:476
  10.3 2.7 %collective-permute-start.4 = (bf16[8,528,128]{2,1,0:T(8,128)(2,1)S(1)}, bf16[8,528,128]{2,1,0:T(8,128)(2,1)S(1)}, u32[]{:S(2)}, u32[]{:S(2)}) collective-permute-start(bf16[8,528,128]{2,1,0:T(8,128)(2,1)S(1)} %get-tuple-element.32.second_ref.refs_5_), channel_id=1, source_target_pairs={{0,6},{1,7},{2,0},{3,1},{4,2},{5,3},{6,4},{7,5},{8,14},{9,15},{10,... | collective-permute-start | bytes 3244040 | tf_op jit(solution)/shard_map/ppermute | solution.py:476
  13.0 2.3 %copy-done = bf16[136,128,128]{2,1,0:T(8,128)(2,1)S(1)} copy-done((bf16[136,128,128]{2,1,0:T(8,128)(2,1)S(1)}, bf16[136,128,128]{2,1,0:T(8,128)(2,1)}, u32[]{:S(2)}) %copy-start) | copy-done | bytes 4456472
  15.3 18.4 %left.1 = (bf16[136,2,256,512]{3,2,1,0:T(8,128)(2,1)}, bf16[8,2,16,128]{3,2,1,0:T(8,128)(2,1)S(1)}) custom-call(s32[136]{0:T(256)S(1)} %and_select_fusion.1.left_index, s32[136]{0:T(256)S(1)} %get-tuple-element.58.right_index, bf16[8,528,128]{2,1,0:T(8,128)(2,1)S(1)} %get-tuple-element.31.first_ref.refs_0_, ...), custom_call_target="tpu_custom_call" | custom-call | tf_op jit(solution)/shard_map/left/pallas_call | solution.py:243
  34.0 2.0 %collective-permute-done.3.second_less.refs_6_ = bf16[8,528,128]{2,1,0:T(8,128)(2,1)S(1)} collective-permute-done((bf16[8,528,128]{2,1,0:T(8,128)(2,1)S(1)}, bf16[8,528,128]{2,1,0:T(8,128)(2,1)S(1)}, u32[]{:S(2)}, u32[]{:S(2)}) %collective-permute-start.3) | collective-permute-done | bytes 1081376 | tf_op jit(solution)/shard_map/ppermute | solution.py:476
  36.2 2.7 %collective-permute-start.6 = (bf16[4,528,128]{2,1,0:T(8,128)(2,1)S(1)}, bf16[4,528,128]{2,1,0:T(8,128)(2,1)S(1)}, u32[]{:S(2)}, u32[]{:S(2)}) collective-permute-start(bf16[4,528,128]{2,1,0:T(8,128)(2,1)S(1)} %get-tuple-element.36), channel_id=1, source_target_pairs={{0,24},{1,25},{2,26},{3,27},{4,28},{5,29},{6,30},{7,31},{8,0},{9,1... | collective-permute-start | bytes 1622024 | tf_op jit(solution)/shard_map/ppermute | solution.py:476
  38.9 2.7 %collective-permute-start.8 = (bf16[4,528,128]{2,1,0:T(8,128)(2,1)S(1)}, bf16[4,528,128]{2,1,0:T(8,128)(2,1)S(1)}, u32[]{:S(2)}, u32[]{:S(2)}) collective-permute-start(bf16[4,528,128]{2,1,0:T(8,128)(2,1)S(1)} %get-tuple-element.38), channel_id=1, source_target_pairs={{0,6},{1,7},{2,0},{3,1},{4,2},{5,3},{6,4},{7,5},{8,14},{9,15},{10,... | collective-permute-start | bytes 1622024 | tf_op jit(solution)/shard_map/ppermute | solution.py:476
  41.6 7.8 %collective-permute-done.5.refs_3_ = bf16[4,528,128]{2,1,0:T(8,128)(2,1)S(1)} collective-permute-done((bf16[4,528,128]{2,1,0:T(8,128)(2,1)S(1)}, bf16[4,528,128]{2,1,0:T(8,128)(2,1)S(1)}, u32[]{:S(2)}, u32[]{:S(2)}) %collective-permute-start.5) | collective-permute-done | bytes 540704 | tf_op jit(solution)/shard_map/ppermute | solution.py:476
  49.4 2.1 %collective-permute-done.7.refs_8_ = bf16[4,528,128]{2,1,0:T(8,128)(2,1)S(1)} collective-permute-done((bf16[4,528,128]{2,1,0:T(8,128)(2,1)S(1)}, bf16[4,528,128]{2,1,0:T(8,128)(2,1)S(1)}, u32[]{:S(2)}, u32[]{:S(2)}) %collective-permute-start.7) | collective-permute-done | bytes 540704 | tf_op jit(solution)/shard_map/ppermute | solution.py:476
  51.5 1.9 %choose.1 = (bf16[4,512,128]{2,1,0:T(8,128)(2,1)S(1)}, bf16[4,512,128]{2,1,0:T(8,128)(2,1)S(1)}, bf16[4,512,128]{2,1,0:T(8,128)(2,1)S(1)}, bf16[4,512,128]{2,1,0...) custom-call(bf16[8,528,128]{2,1,0:T(8,128)(2,1)S(1)} %get-tuple-elem, ...), custom_call_target="tpu_custom_call" | custom-call | tf_op jit(solution)/shard_map/choose/pallas_call | solution.py:137
  53.8 2.5 %collective-permute-start.11 = (bf16[4,512,128]{2,1,0:T(8,128)(2,1)S(1)}, bf16[4,512,128]{2,1,0:T(8,128)(2,1)S(1)}, u32[]{:S(2)}, u32[]{:S(2)}) collective-permute-start(bf16[4,512,128]{2,1,0:T(8,128)(2,1)S(1)} %get-tuple-element.41), channel_id=1, source_target_pairs={{0,6},{1,7},{2,0},{3,1},{4,2},{5,3},{6,4},{7,5},{8,14},{9,15},{10,... | collective-permute-start | bytes 1572872 | tf_op jit(solution)/shard_map/ppermute | solution.py:476
  56.2 2.6 %collective-permute-start.12 = (bf16[4,512,128]{2,1,0:T(8,128)(2,1)S(1)}, bf16[4,512,128]{2,1,0:T(8,128)(2,1)S(1)}, u32[]{:S(2)}, u32[]{:S(2)}) collective-permute-start(bf16[4,512,128]{2,1,0:T(8,128)(2,1)S(1)} %get-tuple-element.42), channel_id=1, source_target_pairs={{0,24},{1,25},{2,26},{3,27},{4,28},{5,29},{6,30},{7,31},{8,0},{9,1... | collective-permute-start | bytes 1572872 | tf_op jit(solution)/shard_map/ppermute | solution.py:476
  58.8 6.0 %collective-permute-done.9.__1_.refs_0_ = bf16[4,512,128]{2,1,0:T(8,128)(2,1)S(1)} collective-permute-done((bf16[4,512,128]{2,1,0:T(8,128)(2,1)S(1)}, bf16[4,512,128]{2,1,0:T(8,128)(2,1)S(1)}, u32[]{:S(2)}, u32[]{:S(2)}) %collective-permute-start.9) | collective-permute-done | bytes 524320 | tf_op jit(solution)/shard_map/ppermute | solution.py:476
  64.8 3.1 %collective-permute-start.15 = (bf16[4,512,128]{2,1,0:T(8,128)(2,1)S(1)}, bf16[4,512,128]{2,1,0:T(8,128)(2,1)S(1)}, u32[]{:S(2)}, u32[]{:S(2)}) collective-permute-start(bf16[4,512,128]{2,1,0:T(8,128)(2,1)S(1)} %after.8), channel_id=1, source_target_pairs={{0,3},{1,2},{2,5},{3,4},{4,7},{5,6},{6,1},{7,0},{8,11},{9,10},{10,... | collective-permute-start | bytes 1572872 | tf_op jit(solution)/shard_map/ppermute | solution.py:476
  68.2 3.5 %collective-permute-start.17 = (bf16[4,512,128]{2,1,0:T(8,128)(2,1)S(1)}, bf16[4,512,128]{2,1,0:T(8,128)(2,1)S(1)}, u32[]{:S(2)}, u32[]{:S(2)}) collective-permute-start(bf16[4,512,128]{2,1,0:T(8,128)(2,1)S(1)} %after.10), channel_id=1, source_target_pairs={{0,7},{1,6},{2,1},{3,0},{4,3},{5,2},{6,5},{7,4},{8,15},{9,14},{10,... | collective-permute-start | bytes 1572872 | tf_op jit(solution)/shard_map/ppermute | solution.py:476
  71.7 2.9 %collective-permute-start.18 = (bf16[4,512,128]{2,1,0:T(8,128)(2,1)S(1)}, bf16[4,512,128]{2,1,0:T(8,128)(2,1)S(1)}, u32[]{:S(2)}, u32[]{:S(2)}) collective-permute-start(bf16[4,512,128]{2,1,0:T(8,128)(2,1)S(1)} %after.11), channel_id=1, source_target_pairs={{0,25},{1,24},{2,27},{3,26},{4,29},{5,28},{6,31},{7,30},{8,1},{9,0... | collective-permute-start | bytes 1572872 | tf_op jit(solution)/shard_map/ppermute | solution.py:476
  75.0 6.6 %collective-permute-done.15.refs_8_.__1_ = bf16[4,512,128]{2,1,0:T(8,128)(2,1)S(1)} collective-permute-done((bf16[4,512,128]{2,1,0:T(8,128)(2,1)S(1)}, bf16[4,512,128]{2,1,0:T(8,128)(2,1)S(1)}, u32[]{:S(2)}, u32[]{:S(2)}) %collective-permute-start.15) | collective-permute-done | bytes 524320 | tf_op jit(solution)/shard_map/ppermute | solution.py:476
  83.3 3.2 %collective-permute-start.19 = (bf16[4,512,128]{2,1,0:T(8,128)(2,1)S(1)}, bf16[4,512,128]{2,1,0:T(8,128)(2,1)S(1)}, u32[]{:S(2)}, u32[]{:S(2)}) collective-permute-start(bf16[4,512,128]{2,1,0:T(8,128)(2,1)S(1)} %after.12), channel_id=1, source_target_pairs={{0,4},{1,5},{2,6},{3,7},{4,0},{5,1},{6,2},{7,3},{8,12},{9,13},{10,... | collective-permute-start | bytes 1572872 | tf_op jit(solution)/shard_map/ppermute | solution.py:476
  87.5 3.6 %collective-permute-start.22 = (bf16[4,512,128]{2,1,0:T(8,128)(2,1)S(1)}, bf16[4,512,128]{2,1,0:T(8,128)(2,1)S(1)}, u32[]{:S(2)}, u32[]{:S(2)}) collective-permute-start(bf16[4,512,128]{2,1,0:T(8,128)(2,1)S(1)} %after.15), channel_id=1, source_target_pairs={{0,17},{1,16},{2,19},{3,18},{4,21},{5,20},{6,23},{7,22},{8,25},{9,... | collective-permute-start | bytes 1572872 | tf_op jit(solution)/shard_map/ppermute | solution.py:476
  91.2 21.6 %near_exchange.1 = (bf16[8,20,16,128]{3,2,1,0:T(8,128)(2,1)S(1)}, f32[8,14,16,128]{3,2,1,0:T(8,128)S(1)}) custom-call(bf16[136,2,256,512]{3,2,1,0:T(8,128)(2,1)} %get-tuple-element.33.left_ref, bf16[136,128,128]{2,1,0:T(8,128)(2,1)S(1)} %bitcast.3, bf16[8,2,16,128]{3,2,1,0:T(8,128)(2,1)S(1)} %get-tuple-element.34._.own_ref, ...), custom_call_target="tpu_custom_call" | custom-call | tf_op jit(solution)/shard_map/near_exchange/pallas_call | solution.py:350
  112.8 10.0 %far_exchange.1 = bf16[8,34,16,128]{3,2,1,0:T(8,128)(2,1)} custom-call(bf16[136,2,256,512]{3,2,1,0:T(8,128)(2,1)} %get-tuple-element.33.left_ref, bf16[136,128,128]{2,1,0:T(8,128)(2,1)S(1)} %bitcast.3, bf16[8,20,16,128]{3,2,1,0:T(8,128)(2,1)S(1)} %get-tuple-element.51.near_ref, f32[8,14,16,128]{3,2,1,0:T(8,128)S(1)} %get-tuple-element.52.begun_ref, ...), custom_call_target="tpu_custom_call" | custom-call | tf_op jit(solution)/shard_map/far_exchange/pallas_call | solution.py:366
  122.9 6.8 %all-to-all-start = ((bf16[8,34,16,128]{3,2,1,0:T(8,128)(2,1)}), bf16[8,34,16,128]{3,2,1,0:T(8,128)(2,1)S(1)}, u32[]{:S(2)}, u32[]{:S(2)}) async-start(bf16[8,34,16,128]{3,2,1,0:T(8,128)(2,1)} %far_exchange.1), calls=%async_computation | async-start | bytes 2228224 | tf_op jit(solution)/shard_map/all_to_all | solution.py:530
  131.1 29.2 %all-to-all-done.arrived_ref = bf16[8,34,16,128]{3,2,1,0:T(8,128)(2,1)S(1)} async-done(((bf16[8,34,16,128]{3,2,1,0:T(8,128)(2,1)}), bf16[8,34,16,128]{3,2,1,0:T(8,128)(2,1)S(1)}, u32[]{:S(2)}, u32[]{:S(2)}) %all-to-all-start) | async-done | bytes 1114144 | tf_op jit(solution)/shard_map/all_to_all | solution.py:530
  (60 shorter events, 11.3 us)
Async XLA Ops:
  0.9 4.2 %collective-permute-start = (bf16[16,128]{1,0:T(8,128)(2,1)S(1)}, bf16[16,128]{1,0:T(8,128)(2,1)S(1)}, u32[]{:S(2)}, u32[]{:S(2)}) collective-permute-start(bf16[16,128]{1,0:T(8,128)(2,1)S(1)} %broadcast_in_dim.2.wanted_ref), channel_id=1, source_target_pairs={{0,1},{1,0},{2,3},{3,2},{4,5},{5,4},{6,7},{7,6},{8,9},{9,8},{10,11... | collective-permute-start | bytes 12296 | tf_op jit(solution)/shard_map/ppermute | solution.py:476
  7.6 26.4 %collective-permute-start.1 = (bf16[8,528,128]{2,1,0:T(8,128)(2,1)S(1)}, bf16[8,528,128]{2,1,0:T(8,128)(2,1)S(1)}, u32[]{:S(2)}, u32[]{:S(2)}) collective-permute-start(bf16[8,528,128]{2,1,0:T(8,128)(2,1)S(1)} %get-tuple-element.31.first_ref.refs_0_), channel_id=1, source_target_pairs={{0,8},{1,9},{2,10},{3,11},{4,12},{5,13},{6,14},{7,15},{8,16},{9,17... | collective-permute-start | bytes 3244040 | tf_op jit(solution)/shard_map/ppermute | solution.py:476
  7.7 26.3 %collective-permute-start.2 = (bf16[8,528,128]{2,1,0:T(8,128)(2,1)S(1)}, bf16[8,528,128]{2,1,0:T(8,128)(2,1)S(1)}, u32[]{:S(2)}, u32[]{:S(2)}) collective-permute-start(bf16[8,528,128]{2,1,0:T(8,128)(2,1)S(1)} %get-tuple-element.31.first_ref.refs_0_), channel_id=1, source_target_pairs={{0,24},{1,25},{2,26},{3,27},{4,28},{5,29},{6,30},{7,31},{8,0},{9,1... | collective-permute-start | bytes 3244040 | tf_op jit(solution)/shard_map/ppermute | solution.py:476
  10.3 25.7 %collective-permute-start.3 = (bf16[8,528,128]{2,1,0:T(8,128)(2,1)S(1)}, bf16[8,528,128]{2,1,0:T(8,128)(2,1)S(1)}, u32[]{:S(2)}, u32[]{:S(2)}) collective-permute-start(bf16[8,528,128]{2,1,0:T(8,128)(2,1)S(1)} %get-tuple-element.32.second_ref.refs_5_), channel_id=1, source_target_pairs={{0,2},{1,3},{2,4},{3,5},{4,6},{5,7},{6,0},{7,1},{8,10},{9,11},{10,... | collective-permute-start | bytes 3244040 | tf_op jit(solution)/shard_map/ppermute | solution.py:476
  10.3 25.7 %collective-permute-start.4 = (bf16[8,528,128]{2,1,0:T(8,128)(2,1)S(1)}, bf16[8,528,128]{2,1,0:T(8,128)(2,1)S(1)}, u32[]{:S(2)}, u32[]{:S(2)}) collective-permute-start(bf16[8,528,128]{2,1,0:T(8,128)(2,1)S(1)} %get-tuple-element.32.second_ref.refs_5_), channel_id=1, source_target_pairs={{0,6},{1,7},{2,0},{3,1},{4,2},{5,3},{6,4},{7,5},{8,14},{9,15},{10,... | collective-permute-start | bytes 3244040 | tf_op jit(solution)/shard_map/ppermute | solution.py:476
  36.2 13.2 %collective-permute-start.5 = (bf16[4,528,128]{2,1,0:T(8,128)(2,1)S(1)}, bf16[4,528,128]{2,1,0:T(8,128)(2,1)S(1)}, u32[]{:S(2)}, u32[]{:S(2)}) collective-permute-start(bf16[4,528,128]{2,1,0:T(8,128)(2,1)S(1)} %get-tuple-element.35), channel_id=1, source_target_pairs={{0,8},{1,9},{2,10},{3,11},{4,12},{5,13},{6,14},{7,15},{8,16},{9,17... | collective-permute-start | bytes 1622024 | tf_op jit(solution)/shard_map/ppermute | solution.py:476
  36.2 13.2 %collective-permute-start.6 = (bf16[4,528,128]{2,1,0:T(8,128)(2,1)S(1)}, bf16[4,528,128]{2,1,0:T(8,128)(2,1)S(1)}, u32[]{:S(2)}, u32[]{:S(2)}) collective-permute-start(bf16[4,528,128]{2,1,0:T(8,128)(2,1)S(1)} %get-tuple-element.36), channel_id=1, source_target_pairs={{0,24},{1,25},{2,26},{3,27},{4,28},{5,29},{6,30},{7,31},{8,0},{9,1... | collective-permute-start | bytes 1622024 | tf_op jit(solution)/shard_map/ppermute | solution.py:476
  38.9 12.6 %collective-permute-start.7 = (bf16[4,528,128]{2,1,0:T(8,128)(2,1)S(1)}, bf16[4,528,128]{2,1,0:T(8,128)(2,1)S(1)}, u32[]{:S(2)}, u32[]{:S(2)}) collective-permute-start(bf16[4,528,128]{2,1,0:T(8,128)(2,1)S(1)} %get-tuple-element.37), channel_id=1, source_target_pairs={{0,2},{1,3},{2,4},{3,5},{4,6},{5,7},{6,0},{7,1},{8,10},{9,11},{10,... | collective-permute-start | bytes 1622024 | tf_op jit(solution)/shard_map/ppermute | solution.py:476
  38.9 12.6 %collective-permute-start.8 = (bf16[4,528,128]{2,1,0:T(8,128)(2,1)S(1)}, bf16[4,528,128]{2,1,0:T(8,128)(2,1)S(1)}, u32[]{:S(2)}, u32[]{:S(2)}) collective-permute-start(bf16[4,528,128]{2,1,0:T(8,128)(2,1)S(1)} %get-tuple-element.38), channel_id=1, source_target_pairs={{0,6},{1,7},{2,0},{3,1},{4,2},{5,3},{6,4},{7,5},{8,14},{9,15},{10,... | collective-permute-start | bytes 1622024 | tf_op jit(solution)/shard_map/ppermute | solution.py:476
  53.4 11.4 %collective-permute-start.9 = (bf16[4,512,128]{2,1,0:T(8,128)(2,1)S(1)}, bf16[4,512,128]{2,1,0:T(8,128)(2,1)S(1)}, u32[]{:S(2)}, u32[]{:S(2)}) collective-permute-start(bf16[4,512,128]{2,1,0:T(8,128)(2,1)S(1)} %get-tuple-element.39), channel_id=1, source_target_pairs={{0,2},{1,3},{2,4},{3,5},{4,6},{5,7},{6,0},{7,1},{8,10},{9,11},{10,... | collective-permute-start | bytes 1572872 | tf_op jit(solution)/shard_map/ppermute | solution.py:476
  53.7 14.2 %collective-permute-start.10 = (bf16[4,512,128]{2,1,0:T(8,128)(2,1)S(1)}, bf16[4,512,128]{2,1,0:T(8,128)(2,1)S(1)}, u32[]{:S(2)}, u32[]{:S(2)}) collective-permute-start(bf16[4,512,128]{2,1,0:T(8,128)(2,1)S(1)} %get-tuple-element.40), channel_id=1, source_target_pairs={{0,8},{1,9},{2,10},{3,11},{4,12},{5,13},{6,14},{7,15},{8,16},{9,17... | collective-permute-start | bytes 1572872 | tf_op jit(solution)/shard_map/ppermute | solution.py:476
  53.8 14.4 %collective-permute-start.11 = (bf16[4,512,128]{2,1,0:T(8,128)(2,1)S(1)}, bf16[4,512,128]{2,1,0:T(8,128)(2,1)S(1)}, u32[]{:S(2)}, u32[]{:S(2)}) collective-permute-start(bf16[4,512,128]{2,1,0:T(8,128)(2,1)S(1)} %get-tuple-element.41), channel_id=1, source_target_pairs={{0,6},{1,7},{2,0},{3,1},{4,2},{5,3},{6,4},{7,5},{8,14},{9,15},{10,... | collective-permute-start | bytes 1572872 | tf_op jit(solution)/shard_map/ppermute | solution.py:476
  56.2 15.5 %collective-permute-start.12 = (bf16[4,512,128]{2,1,0:T(8,128)(2,1)S(1)}, bf16[4,512,128]{2,1,0:T(8,128)(2,1)S(1)}, u32[]{:S(2)}, u32[]{:S(2)}) collective-permute-start(bf16[4,512,128]{2,1,0:T(8,128)(2,1)S(1)} %get-tuple-element.42), channel_id=1, source_target_pairs={{0,24},{1,25},{2,26},{3,27},{4,28},{5,29},{6,30},{7,31},{8,0},{9,1... | collective-permute-start | bytes 1572872 | tf_op jit(solution)/shard_map/ppermute | solution.py:476
  64.8 16.8 %collective-permute-start.15 = (bf16[4,512,128]{2,1,0:T(8,128)(2,1)S(1)}, bf16[4,512,128]{2,1,0:T(8,128)(2,1)S(1)}, u32[]{:S(2)}, u32[]{:S(2)}) collective-permute-start(bf16[4,512,128]{2,1,0:T(8,128)(2,1)S(1)} %after.8), channel_id=1, source_target_pairs={{0,3},{1,2},{2,5},{3,4},{4,7},{5,6},{6,1},{7,0},{8,11},{9,10},{10,... | collective-permute-start | bytes 1572872 | tf_op jit(solution)/shard_map/ppermute | solution.py:476
  68.0 15.3 %collective-permute-start.16 = (bf16[4,512,128]{2,1,0:T(8,128)(2,1)S(1)}, bf16[4,512,128]{2,1,0:T(8,128)(2,1)S(1)}, u32[]{:S(2)}, u32[]{:S(2)}) collective-permute-start(bf16[4,512,128]{2,1,0:T(8,128)(2,1)S(1)} %after.9), channel_id=1, source_target_pairs={{0,9},{1,8},{2,11},{3,10},{4,13},{5,12},{6,15},{7,14},{8,17},{9,16... | collective-permute-start | bytes 1572872 | tf_op jit(solution)/shard_map/ppermute | solution.py:476
  68.2 18.3 %collective-permute-start.17 = (bf16[4,512,128]{2,1,0:T(8,128)(2,1)S(1)}, bf16[4,512,128]{2,1,0:T(8,128)(2,1)S(1)}, u32[]{:S(2)}, u32[]{:S(2)}) collective-permute-start(bf16[4,512,128]{2,1,0:T(8,128)(2,1)S(1)} %after.10), channel_id=1, source_target_pairs={{0,7},{1,6},{2,1},{3,0},{4,3},{5,2},{6,5},{7,4},{8,15},{9,14},{10,... | collective-permute-start | bytes 1572872 | tf_op jit(solution)/shard_map/ppermute | solution.py:476
  71.7 14.8 %collective-permute-start.18 = (bf16[4,512,128]{2,1,0:T(8,128)(2,1)S(1)}, bf16[4,512,128]{2,1,0:T(8,128)(2,1)S(1)}, u32[]{:S(2)}, u32[]{:S(2)}) collective-permute-start(bf16[4,512,128]{2,1,0:T(8,128)(2,1)S(1)} %after.11), channel_id=1, source_target_pairs={{0,25},{1,24},{2,27},{3,26},{4,29},{5,28},{6,31},{7,30},{8,1},{9,0... | collective-permute-start | bytes 1572872 | tf_op jit(solution)/shard_map/ppermute | solution.py:476
  74.6 13.0 %collective-permute-start.13 = (bf16[4,512,128]{2,1,0:T(8,128)(2,1)S(1)}, bf16[4,512,128]{2,1,0:T(8,128)(2,1)S(1)}, u32[]{:S(2)}, u32[]{:S(2)}) collective-permute-start(bf16[4,512,128]{2,1,0:T(8,128)(2,1)S(1)} %get-tuple-element.45), channel_id=1, source_target_pairs={{0,1},{1,0},{2,3},{3,2},{4,5},{5,4},{6,7},{7,6},{8,9},{9,8},{10,11... | collective-permute-start | bytes 1572872 | tf_op jit(solution)/shard_map/ppermute | solution.py:476
  81.7 9.5 %collective-permute-start.14 = (bf16[4,512,128]{2,1,0:T(8,128)(2,1)S(1)}, bf16[4,512,128]{2,1,0:T(8,128)(2,1)S(1)}, u32[]{:S(2)}, u32[]{:S(2)}) collective-permute-start(bf16[4,512,128]{2,1,0:T(8,128)(2,1)S(1)} %get-tuple-element.46), channel_id=1, source_target_pairs={{0,1},{1,0},{2,3},{3,2},{4,5},{5,4},{6,7},{7,6},{8,9},{9,8},{10,11... | collective-permute-start | bytes 1572872 | tf_op jit(solution)/shard_map/ppermute | solution.py:476
  83.3 29.5 %collective-permute-start.19 = (bf16[4,512,128]{2,1,0:T(8,128)(2,1)S(1)}, bf16[4,512,128]{2,1,0:T(8,128)(2,1)S(1)}, u32[]{:S(2)}, u32[]{:S(2)}) collective-permute-start(bf16[4,512,128]{2,1,0:T(8,128)(2,1)S(1)} %after.12), channel_id=1, source_target_pairs={{0,4},{1,5},{2,6},{3,7},{4,0},{5,1},{6,2},{7,3},{8,12},{9,13},{10,... | collective-permute-start | bytes 1572872 | tf_op jit(solution)/shard_map/ppermute | solution.py:476
  86.5 26.3 %collective-permute-start.20 = (bf16[4,512,128]{2,1,0:T(8,128)(2,1)S(1)}, bf16[4,512,128]{2,1,0:T(8,128)(2,1)S(1)}, u32[]{:S(2)}, u32[]{:S(2)}) collective-permute-start(bf16[4,512,128]{2,1,0:T(8,128)(2,1)S(1)} %after.13), channel_id=1, source_target_pairs={{0,16},{1,17},{2,18},{3,19},{4,20},{5,21},{6,22},{7,23},{8,24},{9,... | collective-permute-start | bytes 1572872 | tf_op jit(solution)/shard_map/ppermute | solution.py:476
  86.5 26.3 %collective-permute-start.21 = (bf16[4,512,128]{2,1,0:T(8,128)(2,1)S(1)}, bf16[4,512,128]{2,1,0:T(8,128)(2,1)S(1)}, u32[]{:S(2)}, u32[]{:S(2)}) collective-permute-start(bf16[4,512,128]{2,1,0:T(8,128)(2,1)S(1)} %after.14), channel_id=1, source_target_pairs={{0,5},{1,4},{2,7},{3,6},{4,1},{5,0},{6,3},{7,2},{8,13},{9,12},{10,... | collective-permute-start | bytes 1572872 | tf_op jit(solution)/shard_map/ppermute | solution.py:476
  87.5 25.3 %collective-permute-start.22 = (bf16[4,512,128]{2,1,0:T(8,128)(2,1)S(1)}, bf16[4,512,128]{2,1,0:T(8,128)(2,1)S(1)}, u32[]{:S(2)}, u32[]{:S(2)}) collective-permute-start(bf16[4,512,128]{2,1,0:T(8,128)(2,1)S(1)} %after.15), channel_id=1, source_target_pairs={{0,17},{1,16},{2,19},{3,18},{4,21},{5,20},{6,23},{7,22},{8,25},{9,... | collective-permute-start | bytes 1572872 | tf_op jit(solution)/shard_map/ppermute | solution.py:476
  122.9 37.4 %all-to-all-start = ((bf16[8,34,16,128]{3,2,1,0:T(8,128)(2,1)}), bf16[8,34,16,128]{3,2,1,0:T(8,128)(2,1)S(1)}, u32[]{:S(2)}, u32[]{:S(2)}) async-start(bf16[8,34,16,128]{3,2,1,0:T(8,128)(2,1)} %far_exchange.1), calls=%async_computation | async-start | bytes 2228224 | tf_op jit(solution)/shard_map/all_to_all | solution.py:530
  (6 other events, 80.4 us)
where the time goes:
time: 162 us
  Pallas kernels  55.5 us (34%)
  waiting for transfers between devices  55 us (34%)
  starting transfers between devices  46 us (28%)
  local copies, waits for them, and re-layouts  4.86 us (3%)
    ppermute x23, starting transfers between devices, moved(): lax.ppermute(array, 'pair', [(at(x, y, c), at(x + dx, y + dy, c + core))...  39.3 us
    all_to_all x1, waiting for transfers between devices, on_device(): sums = lax.all_to_all(sums, 'aux', split_axis=0, concat_axis=0, tiled=True)  29.2 us
    ppermute x23, waiting for transfers between devices, moved(): lax.ppermute(array, 'pair', [(at(x, y, c), at(x + dx, y + dy, c + core))...  25.8 us
    pallas_call x1, Pallas kernels, near_exchange(): pl.pallas_call(functools.partial(near_kernel, work), in_specs=[ANY] + [VM...  21.6 us
    pallas_call x1, Pallas kernels, left_of(): pl.pallas_call(left_kernel, in_specs=[SMEM] * 2 + [VMEM] * 3, out_specs=[...  18.4 us
    pallas_call x1, Pallas kernels, far_exchange(): pl.pallas_call(functools.partial(far_kernel, work), in_specs=[ANY] + [VME...  10 us
    all_to_all x1, starting transfers between devices, on_device(): sums = lax.all_to_all(sums, 'aux', split_axis=0, concat_axis=0, tiled=True)  6.77 us
    unnamed x13, local copies, waits for them, and re-layouts  3.96 us
  transfers between devices with their start and end apart: 24, of which 8 were waited for; matrix products, arithmetic and copies ran while one was open for 0% of the time, Pallas kernels for 26%

commit v1 on v0

--- a/solution.py
+++ b/solution.py
@@ -14,14 +14,14 @@
 TARGETS = tuple((shift, core) for shift in RELS for core in range(CORES))
 SMEM = pl.BlockSpec(memory_space=pltpu.SMEM)
 EXTRA = 16
-SLOTS = 6
+BATCH = 6
 VMEM = pl.BlockSpec(memory_space=pltpu.VMEM)
 ANY = pl.BlockSpec(memory_space=pl.ANY)
 NEAR = [(dx, dy, c) for dx in RELS for dy in RELS for c in range(CORES) if 2 not in (dx, dy)]
 FAR = [(dx, dy, c) for dx in RELS for dy in RELS for c in range(CORES) if 2 in (dx, dy)]
 
 
-def params(mib=12):
+def params(mib=20):
     return pltpu.CompilerParams(vmem_limit_bytes=mib * 1024 * 1024)
 
 
@@ -296,21 +296,32 @@
             left_ref.at[group, along], lefts.at[slot, along], sem.at[slot]
         )
 
-    for n in range(slots - 1):
+    rights = {}
+    batch = slots // 2
+    for n in range(min(batch, len(todo))):
         copy_in(n).start()
     for n, (entry, alongs, out_ref, at, base_ref, base_at) in enumerate(todo):
         slot = n % slots
-        if n + slots - 1 < len(todo):
-            copy_in(n + slots - 1).start()
-        copy_in(n).wait()
-        rights = right_coeffs(projectors_ref, group_of(place, *entry) * GROUP, GROUP)
+        if n % batch == 0:
+            for later in range(n + batch, min(n + 2 * batch, len(todo))):
+                copy_in(later).start()
+            here = range(n, min(n + batch, len(todo)))
+            for now in here:
+                coeffs = right_coeffs(
+                    projectors_ref, group_of(place, *todo[now][0]) * GROUP, GROUP
+                )
+                for along in todo[now][1]:
+                    number, r = parts[todo[now][0], along]
+                    rights[now, along] = jnp.dot(
+                        block_refs[number][r], coeffs, preferred_element_type=jnp.float32
+                    ).astype(jnp.bfloat16)
+            for now in here:
+                copy_in(now).wait()
         mixed = 0.0
         for along in alongs:
-            number, r = parts[entry, along]
-            right = jnp.dot(
-                block_refs[number][r], rights, preferred_element_type=jnp.float32
-            ).astype(jnp.bfloat16)
-            mixed += jnp.dot(lefts[slot, along], right, preferred_element_type=jnp.float32)
+            mixed += jnp.dot(
+                lefts[slot, along], rights.pop((n, along)), preferred_element_type=jnp.float32
+            )
         blocks = []
         for k in range(0, GROUP, 2):
             columns = slice(k * width, (k + 2) * width)
@@ -330,18 +341,16 @@
     add_up(work, targets, left_ref, projectors_ref, refs[: len(work)], lefts, sem)
 
 
-def far_kernel(work, left_ref, projectors_ref, near_ref, begun_ref, *refs):
+def far_kernel(work, left_ref, projectors_ref, begun_ref, *refs):
     out_ref, lefts, sem = refs[len(work) :]
-    count = near_ref.shape[1]
-    out_ref[:, :count] = near_ref[...]
-    targets = [(FAR, out_ref, count, begun_ref)]
+    targets = [(FAR, out_ref, 0, begun_ref)]
     add_up(work, targets, left_ref, projectors_ref, refs[: len(work)], lefts, sem)
 
 
 def left_slots(left):
     return [
-        pltpu.VMEM((SLOTS,) + left.shape[1:], left.dtype),
-        pltpu.SemaphoreType.DMA((SLOTS,)),
+        pltpu.VMEM((2 * BATCH,) + left.shape[1:], left.dtype),
+        pltpu.SemaphoreType.DMA((2 * BATCH,)),
     ]
 
 
@@ -361,34 +370,38 @@
     )(left, projectors, own, *blocks)
 
 
-def far_exchange(work, left, projectors, near, begun, blocks):
-    pieces, near_rows, _, both = near.shape
+def far_exchange(work, left, projectors, begun, blocks):
+    pieces, _, _, both = begun.shape
     return pl.pallas_call(
         functools.partial(far_kernel, work),
-        in_specs=[ANY] + [VMEM] * (3 + len(work)),
+        in_specs=[ANY] + [VMEM] * (2 + len(work)),
         out_specs=VMEM,
-        out_shape=sums_shape(near_rows + len(FAR), pieces, both, near.dtype),
+        out_shape=sums_shape(len(FAR), pieces, both, jnp.bfloat16),
         scratch_shapes=left_slots(left),
         compiler_params=params(),
         name="far_exchange",
-    )(left, projectors, near, begun, *blocks)
-
-
-def finish_kernel(arrived_ref, denom_ref, out_ref, share_ref, rows_ref):
-    width = arrived_ref.shape[3] // 2
+    )(left, projectors, begun, *blocks)
+
+
+def finish_kernel(near_ref, far_ref, denom_ref, out_ref, share_ref, rows_ref):
+    width = near_ref.shape[3] // 2
     parts = share_ref.shape[1]
     lane = lax.broadcasted_iota(jnp.int32, (1, 2 * width), 1)
-    total = arrived_ref[0].astype(jnp.float32)
-    for piece in range(1, arrived_ref.shape[0]):
-        total += arrived_ref[piece].astype(jnp.float32)
-    share_ref[...] = total.reshape(share_ref.shape)
+    start = 0
+    for arrived_ref in (near_ref, far_ref):
+        total = arrived_ref[0].astype(jnp.float32)
+        for piece in range(1, arrived_ref.shape[0]):
+            total += arrived_ref[piece].astype(jnp.float32)
+        count = 2 * arrived_ref.shape[1]
+        share_ref[pl.ds(start, count)] = total.reshape((count,) + share_ref.shape[1:])
+        start += count
     for part in range(0, parts, 2):
         even, odd = share_ref[:, part, :], share_ref[:, part + 1, :]
         columns = pl.ds(part * width, 2 * width)
         rows_ref[0, :, columns] = jnp.where(lane < width, even, pltpu.roll(odd, width, 1))
         rows_ref[1, :, columns] = jnp.where(lane < width, pltpu.roll(even, width, 1), odd)
     shared = len(NEAR) + len(FAR)
-    own = arrived_ref.shape[1] - shared
+    own = near_ref.shape[1] - len(NEAR)
     place = my_place()
     groups = [group_of(place, *entry) for entry in NEAR]
     groups += [shared + n for n in range(own)]
@@ -401,13 +414,13 @@
             )
 
 
-def finish(arrived, denom):
-    pieces, _, _, both = arrived.shape
+def finish(near, far, denom):
+    pieces, _, _, both = near.shape
     parts = both // 2 // pieces
     pair_rows = denom.shape[0]
     return pl.pallas_call(
         finish_kernel,
-        in_specs=[VMEM] * 2,
+        in_specs=[VMEM] * 3,
         out_specs=VMEM,
         out_shape=jax.ShapeDtypeStruct(denom.shape, jnp.float32),
         scratch_shapes=[
@@ -416,7 +429,7 @@
         ],
         compiler_params=params(),
         name="finish",
-    )(arrived, denom)
+    )(near, far, denom)
 
 
 def denominators_kernel(first_index, second_index, occ_ref, energy_ref, out_ref, base_ref):
@@ -457,16 +470,16 @@
     )(first_index, second_index, occ_energy, pno_energy)
 
 
-def after(array, other):
+def after(array, *others):
     return pl.pallas_call(
         lambda *_: None,
-        in_specs=[ANY, ANY],
+        in_specs=[ANY] * (1 + len(others)),
         out_specs=ANY,
         out_shape=jax.ShapeDtypeStruct(array.shape, array.dtype),
         input_output_aliases={0: 0},
         compiler_params=params(1),
         name="after",
-    )(array, other)
+    )(array, *others)
 
 
 def moved(array, dx, dy, core):
@@ -524,11 +537,11 @@
             one = step_along(1 - along, one, shift, core)
         arrived[along, shift, core] = one
     near, begun = near_exchange(near_work, left, projectors, own, [arrived[one] for one in near_work])
-    sums = far_exchange(
-        far_work, left, projectors, near, begun, [arrived[one] for one in far_work]
-    )
-    sums = lax.all_to_all(sums, "aux", split_axis=0, concat_axis=0, tiled=True)
-    return finish(sums, denom)
+    near = after(near, arrived[0, 2, 0], arrived[1, 2, 0])
+    near = lax.all_to_all(near, "aux", split_axis=0, concat_axis=0, tiled=True)
+    far = far_exchange(far_work, left, projectors, begun, [arrived[one] for one in far_work])
+    far = lax.all_to_all(after(far, near), "aux", split_axis=0, concat_axis=0, tiled=True)
+    return finish(near, far, denom)
 
 
 def solution(mesh):

time: 162 us -> 169 us (1.043)
  the two profiles are of different devices: /device:TPU:1 before, /device:TPU:11 now
where the time goes in v1:
time: 169 us
  waiting for transfers between devices  71.1 us (42%)
  starting transfers between devices  48.6 us (29%)
  Pallas kernels  38.7 us (23%)
  local copies, waits for them, and re-layouts  9.91 us (6%)
    ppermute x23, waiting for transfers between devices, moved(): lax.ppermute(array, 'pair', [(at(x, y, c), at(x + dx, y + dy, c + core))...  56.1 us
    ppermute x23, starting transfers between devices, moved(): lax.ppermute(array, 'pair', [(at(x, y, c), at(x + dx, y + dy, c + core))...  34 us
    pallas_call x1, Pallas kernels, left_of(): pl.pallas_call(left_kernel, in_specs=[SMEM] * 2 + [VMEM] * 3, out_specs=[...  18.4 us
    all_to_all x1, waiting for transfers between devices, on_device(): lax.all_to_all(after(far, near), 'aux', split_axis=0, concat_axis=0, tile...  15.1 us
    pallas_call x1, Pallas kernels, near_exchange(): pl.pallas_call(functools.partial(near_kernel, work), in_specs=[ANY] + [VM...  9.98 us
    unnamed x25, local copies, waits for them, and re-layouts  9.01 us
    all_to_all x1, starting transfers between devices, on_device(): near = lax.all_to_all(near, 'aux', split_axis=0, concat_axis=0, tiled=True)  7.57 us
    all_to_all x1, starting transfers between devices, on_device(): lax.all_to_all(after(far, near), 'aux', split_axis=0, concat_axis=0, tile...  6.97 us
  transfers between devices with their start and end apart: 25, of which 16 were waited for; matrix products, arithmetic and copies ran while one was open for 0% of the time, Pallas kernels for 20%

profile of v1, /device:TPU:11, one launch (start us, length us, event | category | flops | bytes accessed | tf_op | source)
XLA Modules:
  0.0 168.5 jit_solution(15055296449652556125)
XLA Ops:
  2.5 1.6 copy-done.2
  8.0 2.3 %copy-done = bf16[136,128,128]{2,1,0:T(8,128)(2,1)S(1)} copy-done((bf16[136,128,128]{2,1,0:T(8,128)(2,1)S(1)}, bf16[136,128,128]{2,1,0:T(8,128)(2,1)}, u32[]{:S(2)}) %copy-start) | copy-done | bytes 4456472
  10.3 18.4 %left.1 = (bf16[136,2,256,512]{3,2,1,0:T(8,128)(2,1)}, bf16[8,2,16,128]{3,2,1,0:T(8,128)(2,1)S(1)}) custom-call(s32[136]{0:T(256)S(1)} %and_select_fusion.1.left_index, s32[136]{0:T(256)S(1)} %get-tuple-element.58.right_index, bf16[8,528,128]{2,1,0:T(8,128)(2,1)S(1)} %get-tuple-element.31.first_ref.refs_0_, ...), custom_call_target="tpu_custom_call" | custom-call | tf_op jit(solution)/shard_map/left/pallas_call | solution.py:243
  28.7 1.5 collective-permute-done.1.first_less.refs_1_
  33.8 1.4 collective-permute-start.7
  35.9 8.0 %collective-permute-done.5.refs_3_ = bf16[4,528,128]{2,1,0:T(8,128)(2,1)S(1)} collective-permute-done((bf16[4,528,128]{2,1,0:T(8,128)(2,1)S(1)}, bf16[4,528,128]{2,1,0:T(8,128)(2,1)S(1)}, u32[]{:S(2)}, u32[]{:S(2)}) %collective-permute-start.5) | collective-permute-done | bytes 540704 | tf_op jit(solution)/shard_map/ppermute | solution.py:489
  44.8 1.5 collective-permute-done.7.refs_8_
  47.6 1.9 %choose.1 = (bf16[4,512,128]{2,1,0:T(8,128)(2,1)S(1)}, bf16[4,512,128]{2,1,0:T(8,128)(2,1)S(1)}, bf16[4,512,128]{2,1,0:T(8,128)(2,1)S(1)}, bf16[4,512,128]{2,1,0...) custom-call(bf16[8,528,128]{2,1,0:T(8,128)(2,1)S(1)} %get-tuple-elem, ...), custom_call_target="tpu_custom_call" | custom-call | tf_op jit(solution)/shard_map/choose/pallas_call | solution.py:137
  51.1 2.3 %collective-permute-start.12 = (bf16[4,512,128]{2,1,0:T(8,128)(2,1)S(1)}, bf16[4,512,128]{2,1,0:T(8,128)(2,1)S(1)}, u32[]{:S(2)}, u32[]{:S(2)}) collective-permute-start(bf16[4,512,128]{2,1,0:T(8,128)(2,1)S(1)} %get-tuple-element.42), channel_id=1, source_target_pairs={{0,24},{1,25},{2,26},{3,27},{4,28},{5,29},{6,30},{7,31},{8,0},{9,1... | collective-permute-start | bytes 1572872 | tf_op jit(solution)/shard_map/ppermute | solution.py:489
  53.5 6.2 %collective-permute-done.9.__1_.refs_0_ = bf16[4,512,128]{2,1,0:T(8,128)(2,1)S(1)} collective-permute-done((bf16[4,512,128]{2,1,0:T(8,128)(2,1)S(1)}, bf16[4,512,128]{2,1,0:T(8,128)(2,1)S(1)}, u32[]{:S(2)}, u32[]{:S(2)}) %collective-permute-start.9) | collective-permute-done | bytes 524320 | tf_op jit(solution)/shard_map/ppermute | solution.py:489
  59.7 5.3 %collective-permute-start.15 = (bf16[4,512,128]{2,1,0:T(8,128)(2,1)S(1)}, bf16[4,512,128]{2,1,0:T(8,128)(2,1)S(1)}, u32[]{:S(2)}, u32[]{:S(2)}) collective-permute-start(bf16[4,512,128]{2,1,0:T(8,128)(2,1)S(1)} %after.10), channel_id=1, source_target_pairs={{0,3},{1,2},{2,5},{3,4},{4,7},{5,6},{6,1},{7,0},{8,11},{9,10},{10,... | collective-permute-start | bytes 1572872 | tf_op jit(solution)/shard_map/ppermute | solution.py:489
  66.1 2.2 %collective-permute-start.17 = (bf16[4,512,128]{2,1,0:T(8,128)(2,1)S(1)}, bf16[4,512,128]{2,1,0:T(8,128)(2,1)S(1)}, u32[]{:S(2)}, u32[]{:S(2)}) collective-permute-start(bf16[4,512,128]{2,1,0:T(8,128)(2,1)S(1)} %after.12), channel_id=1, source_target_pairs={{0,7},{1,6},{2,1},{3,0},{4,3},{5,2},{6,5},{7,4},{8,15},{9,14},{10,... | collective-permute-start | bytes 1572872 | tf_op jit(solution)/shard_map/ppermute | solution.py:489
  68.2 9.5 %collective-permute-done.15.refs_8_.__1_ = bf16[4,512,128]{2,1,0:T(8,128)(2,1)S(1)} collective-permute-done((bf16[4,512,128]{2,1,0:T(8,128)(2,1)S(1)}, bf16[4,512,128]{2,1,0:T(8,128)(2,1)S(1)}, u32[]{:S(2)}, u32[]{:S(2)}) %collective-permute-start.15) | collective-permute-done | bytes 524320 | tf_op jit(solution)/shard_map/ppermute | solution.py:489
  79.8 3.0 %collective-permute-start.19 = (bf16[4,512,128]{2,1,0:T(8,128)(2,1)S(1)}, bf16[4,512,128]{2,1,0:T(8,128)(2,1)S(1)}, u32[]{:S(2)}, u32[]{:S(2)}) collective-permute-start(bf16[4,512,128]{2,1,0:T(8,128)(2,1)S(1)} %after.14), channel_id=1, source_target_pairs={{0,4},{1,5},{2,6},{3,7},{4,0},{5,1},{6,2},{7,3},{8,12},{9,13},{10,... | collective-permute-start | bytes 1572872 | tf_op jit(solution)/shard_map/ppermute | solution.py:489
  83.3 7.4 %collective-permute-done.18.refs_11_.__1_ = bf16[4,512,128]{2,1,0:T(8,128)(2,1)S(1)} collective-permute-done((bf16[4,512,128]{2,1,0:T(8,128)(2,1)S(1)}, bf16[4,512,128]{2,1,0:T(8,128)(2,1)S(1)}, u32[]{:S(2)}, u32[]{:S(2)}) %collective-permute-start.18) | collective-permute-done | bytes 524320 | tf_op jit(solution)/shard_map/ppermute | solution.py:489
  90.7 10.0 %near_exchange.1 = (bf16[8,20,16,128]{3,2,1,0:T(8,128)(2,1)}, f32[8,14,16,128]{3,2,1,0:T(8,128)S(1)}) custom-call(bf16[136,2,256,512]{3,2,1,0:T(8,128)(2,1)} %get-tuple-element.33.left_ref, bf16[136,128,128]{2,1,0:T(8,128)(2,1)S(1)} %bitcast.3, bf16[8,2,16,128]{3,2,1,0:T(8,128)(2,1)S(1)} %get-tuple-element.34._.own_ref, ...), custom_call_target="tpu_custom_call" | custom-call | tf_op jit(solution)/shard_map/near_exchange/pallas_call | solution.py:359
  102.3 7.6 %all-to-all-start = ((bf16[8,20,16,128]{3,2,1,0:T(8,128)(2,1)}), bf16[8,20,16,128]{3,2,1,0:T(8,128)(2,1)S(1)}, u32[]{:S(2)}, u32[]{:S(2)}) async-start(bf16[8,20,16,128]{3,2,1,0:T(8,128)(2,1)} %after.16), calls=%async_computation | async-start | bytes 1310720 | tf_op jit(solution)/shard_map/all_to_all | solution.py:541
  111.7 9.2 %collective-permute-start.21 = (bf16[4,512,128]{2,1,0:T(8,128)(2,1)}, bf16[4,512,128]{2,1,0:T(8,128)(2,1)S(1)}, u32[]{:S(2)}, u32[]{:S(2)}) collective-permute-start(bf16[4,512,128]{2,1,0:T(8,128)(2,1)} %copy-done.7), channel_id=1, source_target_pairs={{0,5},{1,4},{2,7},{3,6},{4,1},{5,0},{6,3},{7,2},{8,13},{9,12},{10,... | collective-permute-start | bytes 1572872 | tf_op jit(solution)/shard_map/ppermute | solution.py:489
  121.0 12.3 %collective-permute-done.21.refs_2_ = bf16[4,512,128]{2,1,0:T(8,128)(2,1)S(1)} collective-permute-done((bf16[4,512,128]{2,1,0:T(8,128)(2,1)}, bf16[4,512,128]{2,1,0:T(8,128)(2,1)S(1)}, u32[]{:S(2)}, u32[]{:S(2)}) %collective-permute-start.21) | collective-permute-done | bytes 524320 | tf_op jit(solution)/shard_map/ppermute | solution.py:489
  133.3 3.4 %collective-permute-done.22.refs_3_ = bf16[4,512,128]{2,1,0:T(8,128)(2,1)S(1)} collective-permute-done((bf16[4,512,128]{2,1,0:T(8,128)(2,1)S(1)}, bf16[4,512,128]{2,1,0:T(8,128)(2,1)S(1)}, u32[]{:S(2)}, u32[]{:S(2)}) %collective-permute-start.22) | collective-permute-done | bytes 524320 | tf_op jit(solution)/shard_map/ppermute | solution.py:489
  136.6 2.3 %copy-done.1 = bf16[136,128,128]{2,1,0:T(8,128)(2,1)S(1)} copy-done((bf16[136,128,128]{2,1,0:T(8,128)(2,1)S(1)}, bf16[136,128,128]{2,1,0:T(8,128)(2,1)}, u32[]{:S(2)}) %copy-start.1) | copy-done | bytes 4456472
  138.9 4.8 %far_exchange.1.__0_ = bf16[8,14,16,128]{3,2,1,0:T(8,128)(2,1)} custom-call(bf16[136,2,256,512]{3,2,1,0:T(8,128)(2,1)} %get-tuple-element.33.left_ref, bf16[136,128,128]{2,1,0:T(8,128)(2,1)S(1)} %copy-done.1, f32[8,14,16,128]{3,2,1,0:T(8,128)S(1)} %copy-done.4, bf16[4,512,128]{2,1,0:T(8,128)(2,1)S(1)} %collective-permute-done.19.__1_.refs_0_, ...), custom_call_target="tpu_custom_call" | custom-call | tf_op jit(solution)/shard_map/far_exchange/pallas_call | solution.py:375
  143.8 7.0 %all-to-all-start.1 = ((bf16[8,14,16,128]{3,2,1,0:T(8,128)(2,1)}), bf16[8,14,16,128]{3,2,1,0:T(8,128)(2,1)S(1)}, u32[]{:S(2)}, u32[]{:S(2)}) async-start(bf16[8,14,16,128]{3,2,1,0:T(8,128)(2,1)} %after.19), calls=%async_computation.1 | async-start | bytes 917504 | tf_op jit(solution)/shard_map/all_to_all | solution.py:543
  152.2 15.1 %all-to-all-done.1.far_ref = bf16[8,14,16,128]{3,2,1,0:T(8,128)(2,1)S(1)} async-done(((bf16[8,14,16,128]{3,2,1,0:T(8,128)(2,1)}), bf16[8,14,16,128]{3,2,1,0:T(8,128)(2,1)S(1)}, u32[]{:S(2)}, u32[]{:S(2)}) %all-to-all-start.1) | async-done | bytes 458784 | tf_op jit(solution)/shard_map/all_to_all | solution.py:543
  (76 shorter events, 24.3 us)
Async XLA Ops:
  5.0 25.2 %collective-permute-start.1 = (bf16[8,528,128]{2,1,0:T(8,128)(2,1)S(1)}, bf16[8,528,128]{2,1,0:T(8,128)(2,1)S(1)}, u32[]{:S(2)}, u32[]{:S(2)}) collective-permute-start(bf16[8,528,128]{2,1,0:T(8,128)(2,1)S(1)} %get-tuple-element.31.first_ref.refs_0_), channel_id=1, source_target_pairs={{0,8},{1,9},{2,10},{3,11},{4,12},{5,13},{6,14},{7,15},{8,16},{9,17... | collective-permute-start | bytes 3244040 | tf_op jit(solution)/shard_map/ppermute | solution.py:489
  6.3 24.8 %collective-permute-start.2 = (bf16[8,528,128]{2,1,0:T(8,128)(2,1)S(1)}, bf16[8,528,128]{2,1,0:T(8,128)(2,1)S(1)}, u32[]{:S(2)}, u32[]{:S(2)}) collective-permute-start(bf16[8,528,128]{2,1,0:T(8,128)(2,1)S(1)} %get-tuple-element.31.first_ref.refs_0_), channel_id=1, source_target_pairs={{0,24},{1,25},{2,26},{3,27},{4,28},{5,29},{6,30},{7,31},{8,0},{9,1... | collective-permute-start | bytes 3244040 | tf_op jit(solution)/shard_map/ppermute | solution.py:489
  6.6 24.5 %collective-permute-start.3 = (bf16[8,528,128]{2,1,0:T(8,128)(2,1)S(1)}, bf16[8,528,128]{2,1,0:T(8,128)(2,1)S(1)}, u32[]{:S(2)}, u32[]{:S(2)}) collective-permute-start(bf16[8,528,128]{2,1,0:T(8,128)(2,1)S(1)} %get-tuple-element.32.second_ref.refs_5_), channel_id=1, source_target_pairs={{0,2},{1,3},{2,4},{3,5},{4,6},{5,7},{6,0},{7,1},{8,10},{9,11},{10,... | collective-permute-start | bytes 3244040 | tf_op jit(solution)/shard_map/ppermute | solution.py:489
  7.9 24.2 %collective-permute-start.4 = (bf16[8,528,128]{2,1,0:T(8,128)(2,1)S(1)}, bf16[8,528,128]{2,1,0:T(8,128)(2,1)S(1)}, u32[]{:S(2)}, u32[]{:S(2)}) collective-permute-start(bf16[8,528,128]{2,1,0:T(8,128)(2,1)S(1)} %get-tuple-element.32.second_ref.refs_5_), channel_id=1, source_target_pairs={{0,6},{1,7},{2,0},{3,1},{4,2},{5,3},{6,4},{7,5},{8,14},{9,15},{10,... | collective-permute-start | bytes 3244040 | tf_op jit(solution)/shard_map/ppermute | solution.py:489
  32.2 11.8 %collective-permute-start.5 = (bf16[4,528,128]{2,1,0:T(8,128)(2,1)S(1)}, bf16[4,528,128]{2,1,0:T(8,128)(2,1)S(1)}, u32[]{:S(2)}, u32[]{:S(2)}) collective-permute-start(bf16[4,528,128]{2,1,0:T(8,128)(2,1)S(1)} %get-tuple-element.35), channel_id=1, source_target_pairs={{0,8},{1,9},{2,10},{3,11},{4,12},{5,13},{6,14},{7,15},{8,16},{9,17... | collective-permute-start | bytes 1622024 | tf_op jit(solution)/shard_map/ppermute | solution.py:489
  33.5 11.4 %collective-permute-start.6 = (bf16[4,528,128]{2,1,0:T(8,128)(2,1)S(1)}, bf16[4,528,128]{2,1,0:T(8,128)(2,1)S(1)}, u32[]{:S(2)}, u32[]{:S(2)}) collective-permute-start(bf16[4,528,128]{2,1,0:T(8,128)(2,1)S(1)} %get-tuple-element.36), channel_id=1, source_target_pairs={{0,24},{1,25},{2,26},{3,27},{4,28},{5,29},{6,30},{7,31},{8,0},{9,1... | collective-permute-start | bytes 1622024 | tf_op jit(solution)/shard_map/ppermute | solution.py:489
  33.8 12.5 %collective-permute-start.7 = (bf16[4,528,128]{2,1,0:T(8,128)(2,1)S(1)}, bf16[4,528,128]{2,1,0:T(8,128)(2,1)S(1)}, u32[]{:S(2)}, u32[]{:S(2)}) collective-permute-start(bf16[4,528,128]{2,1,0:T(8,128)(2,1)S(1)} %get-tuple-element.37), channel_id=1, source_target_pairs={{0,2},{1,3},{2,4},{3,5},{4,6},{5,7},{6,0},{7,1},{8,10},{9,11},{10,... | collective-permute-start | bytes 1622024 | tf_op jit(solution)/shard_map/ppermute | solution.py:489
  35.2 12.4 %collective-permute-start.8 = (bf16[4,528,128]{2,1,0:T(8,128)(2,1)S(1)}, bf16[4,528,128]{2,1,0:T(8,128)(2,1)S(1)}, u32[]{:S(2)}, u32[]{:S(2)}) collective-permute-start(bf16[4,528,128]{2,1,0:T(8,128)(2,1)S(1)} %get-tuple-element.38), channel_id=1, source_target_pairs={{0,6},{1,7},{2,0},{3,1},{4,2},{5,3},{6,4},{7,5},{8,14},{9,15},{10,... | collective-permute-start | bytes 1622024 | tf_op jit(solution)/shard_map/ppermute | solution.py:489
  49.5 10.2 %collective-permute-start.9 = (bf16[4,512,128]{2,1,0:T(8,128)(2,1)S(1)}, bf16[4,512,128]{2,1,0:T(8,128)(2,1)S(1)}, u32[]{:S(2)}, u32[]{:S(2)}) collective-permute-start(bf16[4,512,128]{2,1,0:T(8,128)(2,1)S(1)} %get-tuple-element.39), channel_id=1, source_target_pairs={{0,2},{1,3},{2,4},{3,5},{4,6},{5,7},{6,0},{7,1},{8,10},{9,11},{10,... | collective-permute-start | bytes 1572872 | tf_op jit(solution)/shard_map/ppermute | solution.py:489
  50.8 14.2 %collective-permute-start.10 = (bf16[4,512,128]{2,1,0:T(8,128)(2,1)S(1)}, bf16[4,512,128]{2,1,0:T(8,128)(2,1)S(1)}, u32[]{:S(2)}, u32[]{:S(2)}) collective-permute-start(bf16[4,512,128]{2,1,0:T(8,128)(2,1)S(1)} %get-tuple-element.40), channel_id=1, source_target_pairs={{0,8},{1,9},{2,10},{3,11},{4,12},{5,13},{6,14},{7,15},{8,16},{9,17... | collective-permute-start | bytes 1572872 | tf_op jit(solution)/shard_map/ppermute | solution.py:489
  50.8 15.2 %collective-permute-start.11 = (bf16[4,512,128]{2,1,0:T(8,128)(2,1)S(1)}, bf16[4,512,128]{2,1,0:T(8,128)(2,1)S(1)}, u32[]{:S(2)}, u32[]{:S(2)}) collective-permute-start(bf16[4,512,128]{2,1,0:T(8,128)(2,1)S(1)} %get-tuple-element.41), channel_id=1, source_target_pairs={{0,6},{1,7},{2,0},{3,1},{4,2},{5,3},{6,4},{7,5},{8,14},{9,15},{10,... | collective-permute-start | bytes 1572872 | tf_op jit(solution)/shard_map/ppermute | solution.py:489
  51.1 14.9 %collective-permute-start.12 = (bf16[4,512,128]{2,1,0:T(8,128)(2,1)S(1)}, bf16[4,512,128]{2,1,0:T(8,128)(2,1)S(1)}, u32[]{:S(2)}, u32[]{:S(2)}) collective-permute-start(bf16[4,512,128]{2,1,0:T(8,128)(2,1)S(1)} %get-tuple-element.42), channel_id=1, source_target_pairs={{0,24},{1,25},{2,26},{3,27},{4,28},{5,29},{6,30},{7,31},{8,0},{9,1... | collective-permute-start | bytes 1572872 | tf_op jit(solution)/shard_map/ppermute | solution.py:489
  59.7 18.1 %collective-permute-start.15 = (bf16[4,512,128]{2,1,0:T(8,128)(2,1)S(1)}, bf16[4,512,128]{2,1,0:T(8,128)(2,1)S(1)}, u32[]{:S(2)}, u32[]{:S(2)}) collective-permute-start(bf16[4,512,128]{2,1,0:T(8,128)(2,1)S(1)} %after.10), channel_id=1, source_target_pairs={{0,3},{1,2},{2,5},{3,4},{4,7},{5,6},{6,1},{7,0},{8,11},{9,10},{10,... | collective-permute-start | bytes 1572872 | tf_op jit(solution)/shard_map/ppermute | solution.py:489
  65.0 14.8 %collective-permute-start.16 = (bf16[4,512,128]{2,1,0:T(8,128)(2,1)S(1)}, bf16[4,512,128]{2,1,0:T(8,128)(2,1)S(1)}, u32[]{:S(2)}, u32[]{:S(2)}) collective-permute-start(bf16[4,512,128]{2,1,0:T(8,128)(2,1)S(1)} %after.11), channel_id=1, source_target_pairs={{0,9},{1,8},{2,11},{3,10},{4,13},{5,12},{6,15},{7,14},{8,17},{9,16... | collective-permute-start | bytes 1572872 | tf_op jit(solution)/shard_map/ppermute | solution.py:489
  65.0 17.8 %collective-permute-start.13 = (bf16[4,512,128]{2,1,0:T(8,128)(2,1)S(1)}, bf16[4,512,128]{2,1,0:T(8,128)(2,1)S(1)}, u32[]{:S(2)}, u32[]{:S(2)}) collective-permute-start(bf16[4,512,128]{2,1,0:T(8,128)(2,1)S(1)} %get-tuple-element.45), channel_id=1, source_target_pairs={{0,1},{1,0},{2,3},{3,2},{4,5},{5,4},{6,7},{7,6},{8,9},{9,8},{10,11... | collective-permute-start | bytes 1572872 | tf_op jit(solution)/shard_map/ppermute | solution.py:489
  66.0 17.3 %collective-permute-start.14 = (bf16[4,512,128]{2,1,0:T(8,128)(2,1)S(1)}, bf16[4,512,128]{2,1,0:T(8,128)(2,1)S(1)}, u32[]{:S(2)}, u32[]{:S(2)}) collective-permute-start(bf16[4,512,128]{2,1,0:T(8,128)(2,1)S(1)} %get-tuple-element.46), channel_id=1, source_target_pairs={{0,1},{1,0},{2,3},{3,2},{4,5},{5,4},{6,7},{7,6},{8,9},{9,8},{10,11... | collective-permute-start | bytes 1572872 | tf_op jit(solution)/shard_map/ppermute | solution.py:489
  66.1 17.2 %collective-permute-start.17 = (bf16[4,512,128]{2,1,0:T(8,128)(2,1)S(1)}, bf16[4,512,128]{2,1,0:T(8,128)(2,1)S(1)}, u32[]{:S(2)}, u32[]{:S(2)}) collective-permute-start(bf16[4,512,128]{2,1,0:T(8,128)(2,1)S(1)} %after.12), channel_id=1, source_target_pairs={{0,7},{1,6},{2,1},{3,0},{4,3},{5,2},{6,5},{7,4},{8,15},{9,14},{10,... | collective-permute-start | bytes 1572872 | tf_op jit(solution)/shard_map/ppermute | solution.py:489
  77.8 13.0 %collective-permute-start.18 = (bf16[4,512,128]{2,1,0:T(8,128)(2,1)S(1)}, bf16[4,512,128]{2,1,0:T(8,128)(2,1)S(1)}, u32[]{:S(2)}, u32[]{:S(2)}) collective-permute-start(bf16[4,512,128]{2,1,0:T(8,128)(2,1)S(1)} %after.13), channel_id=1, source_target_pairs={{0,25},{1,24},{2,27},{3,26},{4,29},{5,28},{6,31},{7,30},{8,1},{9,0... | collective-permute-start | bytes 1572872 | tf_op jit(solution)/shard_map/ppermute | solution.py:489
  79.8 21.9 %collective-permute-start.19 = (bf16[4,512,128]{2,1,0:T(8,128)(2,1)S(1)}, bf16[4,512,128]{2,1,0:T(8,128)(2,1)S(1)}, u32[]{:S(2)}, u32[]{:S(2)}) collective-permute-start(bf16[4,512,128]{2,1,0:T(8,128)(2,1)S(1)} %after.14), channel_id=1, source_target_pairs={{0,4},{1,5},{2,6},{3,7},{4,0},{5,1},{6,2},{7,3},{8,12},{9,13},{10,... | collective-permute-start | bytes 1572872 | tf_op jit(solution)/shard_map/ppermute | solution.py:489
  82.8 19.4 %collective-permute-start.20 = (bf16[4,512,128]{2,1,0:T(8,128)(2,1)S(1)}, bf16[4,512,128]{2,1,0:T(8,128)(2,1)S(1)}, u32[]{:S(2)}, u32[]{:S(2)}) collective-permute-start(bf16[4,512,128]{2,1,0:T(8,128)(2,1)S(1)} %after.15), channel_id=1, source_target_pairs={{0,16},{1,17},{2,18},{3,19},{4,20},{5,21},{6,22},{7,23},{8,24},{9,... | collective-permute-start | bytes 1572872 | tf_op jit(solution)/shard_map/ppermute | solution.py:489
  102.3 41.5 %all-to-all-start = ((bf16[8,20,16,128]{3,2,1,0:T(8,128)(2,1)}), bf16[8,20,16,128]{3,2,1,0:T(8,128)(2,1)S(1)}, u32[]{:S(2)}, u32[]{:S(2)}) async-start(bf16[8,20,16,128]{3,2,1,0:T(8,128)(2,1)} %after.16), calls=%async_computation | async-start | bytes 1310720 | tf_op jit(solution)/shard_map/all_to_all | solution.py:541
  111.7 21.6 %collective-permute-start.21 = (bf16[4,512,128]{2,1,0:T(8,128)(2,1)}, bf16[4,512,128]{2,1,0:T(8,128)(2,1)S(1)}, u32[]{:S(2)}, u32[]{:S(2)}) collective-permute-start(bf16[4,512,128]{2,1,0:T(8,128)(2,1)} %copy-done.7), channel_id=1, source_target_pairs={{0,5},{1,4},{2,7},{3,6},{4,1},{5,0},{6,3},{7,2},{8,13},{9,12},{10,... | collective-permute-start | bytes 1572872 | tf_op jit(solution)/shard_map/ppermute | solution.py:489
  121.0 15.7 %collective-permute-start.22 = (bf16[4,512,128]{2,1,0:T(8,128)(2,1)S(1)}, bf16[4,512,128]{2,1,0:T(8,128)(2,1)S(1)}, u32[]{:S(2)}, u32[]{:S(2)}) collective-permute-start(bf16[4,512,128]{2,1,0:T(8,128)(2,1)S(1)} %after.18), channel_id=1, source_target_pairs={{0,17},{1,16},{2,19},{3,18},{4,21},{5,20},{6,23},{7,22},{8,25},{9,... | collective-permute-start | bytes 1572872 | tf_op jit(solution)/shard_map/ppermute | solution.py:489
  143.8 23.5 %all-to-all-start.1 = ((bf16[8,14,16,128]{3,2,1,0:T(8,128)(2,1)}), bf16[8,14,16,128]{3,2,1,0:T(8,128)(2,1)S(1)}, u32[]{:S(2)}, u32[]{:S(2)}) async-start(bf16[8,14,16,128]{3,2,1,0:T(8,128)(2,1)} %after.19), calls=%async_computation.1 | async-start | bytes 917504 | tf_op jit(solution)/shard_map/all_to_all | solution.py:543
  (13 other events, 139.2 us)

commit v2 on v1

--- a/solution.py
+++ b/solution.py
@@ -17,8 +17,9 @@
 BATCH = 6
 VMEM = pl.BlockSpec(memory_space=pltpu.VMEM)
 ANY = pl.BlockSpec(memory_space=pl.ANY)
-NEAR = [(dx, dy, c) for dx in RELS for dy in RELS for c in range(CORES) if 2 not in (dx, dy)]
-FAR = [(dx, dy, c) for dx in RELS for dy in RELS for c in range(CORES) if 2 in (dx, dy)]
+ENTRIES = [(dx, dy, c) for c in range(CORES) for dx in RELS for dy in RELS]
+LATE = [entry for entry in ENTRIES if entry[2] == 1 and {1, -1} & set(entry[:2])]
+EARLY = [entry for entry in ENTRIES if entry not in LATE]
 
 
 def params(mib=20):
@@ -159,13 +160,13 @@
     return jnp.where(lane < even.shape[1] // 2, even, odd)
 
 
-def put(out_ref, at, blocks, base_ref=None, base_at=0):
+def put(out_ref, at, blocks, base_ref=None):
     pieces = out_ref.shape[0]
     rows = blocks[0].shape[0] // pieces
     for piece in range(pieces):
         part = jnp.concatenate([one[piece * rows : (piece + 1) * rows] for one in blocks], axis=0)
         if base_ref is not None:
-            part = part + base_ref[piece, base_at]
+            part = part + base_ref[piece, at]
         out_ref[piece, at] = part.astype(out_ref.dtype)
 
 
@@ -174,8 +175,10 @@
     made, out_sem
 ):
     groups = projectors_ref.shape[0] // GROUP
-    batch, _, wide, half = made.shape[1:]
-    width = wide // GROUP
+    batch, _, _, half = made.shape[1:]
+    width = projectors_ref.shape[2] // 2
+    wide = GROUP * width
+    domain = projectors_ref.shape[1]
     steps = groups // batch
     halves = (first_ref, second_ref)
 
@@ -202,6 +205,11 @@
                     (((1,), (1,)), ((), ())),
                     preferred_element_type=jnp.float32,
                 ).astype(jnp.bfloat16)
+        for n in range(batch):
+            rights = right_coeffs(projectors_ref, (s * batch + n) * GROUP, GROUP)
+            made[slot, n, 0, pl.ds(wide, domain // 2), :] = jnp.concatenate(
+                [rights[: domain // 2], rights[domain // 2 :]], axis=1
+            )
         copy_out(s, slot).start()
         return 0
 
@@ -235,21 +243,21 @@
 
 def left_of(left_index, right_index, first, second, projectors, pieces):
     half = first.shape[1] - EXTRA
-    pair_rows, _, both = projectors.shape
+    pair_rows, domain, both = projectors.shape
     groups = pair_rows // GROUP
-    own = groups - len(NEAR) - len(FAR)
+    own = groups - len(ENTRIES)
     batch = 2
-    wide = GROUP * both // 2
+    rows = GROUP * both // 2 + domain // 2
     return pl.pallas_call(
         left_kernel,
         in_specs=[SMEM] * 2 + [VMEM] * 3,
         out_specs=[ANY, VMEM],
         out_shape=[
-            jax.ShapeDtypeStruct((pair_rows, 2, wide, half), jnp.bfloat16),
-            sums_shape(own, pieces, both, jnp.bfloat16),
+            jax.ShapeDtypeStruct((pair_rows, 2, rows, half), jnp.bfloat16),
+            sums_shape(own, pieces, both, jnp.float32),
         ],
         scratch_shapes=[
-            pltpu.VMEM((2, batch, 2, wide, half), jnp.bfloat16),
+            pltpu.VMEM((2, batch, 2, rows, half), jnp.bfloat16),
             pltpu.SemaphoreType.DMA((2,)),
         ],
         compiler_params=params(),
@@ -273,50 +281,65 @@
     }
 
 
-def add_up(work, targets, left_ref, projectors_ref, block_refs, lefts, sem):
+def exchange_kernel(work, before, sets, own, left_ref, *refs):
+    block_refs, refs = refs[: len(work)], refs[len(work) :]
+    base_refs, refs = (refs[: len(sets)], refs[len(sets) :]) if before else (refs[:1], refs[1:])
+    out_refs, (lefts, coeffs, sem) = refs[: len(sets)], refs[len(sets) :]
     slots, _, wide, _ = lefts.shape
     width = wide // GROUP
     place = my_place()
     parts = parts_of(work)
     todo = []
-    for groups, out_ref, start, base_ref in targets:
+    for n, (groups, out_ref) in enumerate(zip(sets, out_refs)):
+        base_ref = base_refs[n] if before else None
+        if groups is EARLY:
+            rest = pl.ds(len(groups), own)
+            out_ref[:, rest] = base_ref[:, rest] if before else base_refs[0][...]
         for at, entry in enumerate(groups):
             alongs = [along for along in range(2) if (entry, along) in parts]
+            old = base_ref if entry in before else None
             if alongs:
-                base = base_ref if len(alongs) == 1 else None
-                todo.append((entry, alongs, out_ref, start + at, base, at))
-
-    def copy_in(n):
+                todo.append((entry, alongs, out_ref, at, old))
+            elif old is not None:
+                out_ref[:, at] = old[:, at].astype(out_ref.dtype)
+
+    def left_copy(n):
         entry, alongs = todo[n][:2]
-        group, slot = group_of(place, *entry), n % slots
-        if len(alongs) == 2:
-            return pltpu.make_async_copy(left_ref.at[group], lefts.at[slot], sem.at[slot])
-        along = alongs[0]
+        group, slot, rows = group_of(place, *entry), n % slots, pl.ds(0, wide)
+        along = slice(None) if len(alongs) == 2 else alongs[0]
         return pltpu.make_async_copy(
-            left_ref.at[group, along], lefts.at[slot, along], sem.at[slot]
+            left_ref.at[group, along, rows], lefts.at[slot, along], sem.at[slot, 0]
         )
+
+    def coeffs_copy(n):
+        group, slot = group_of(place, *todo[n][0]), n % slots
+        rows = pl.ds(wide, coeffs.shape[1])
+        return pltpu.make_async_copy(left_ref.at[group, 0, rows], coeffs.at[slot], sem.at[slot, 1])
 
     rights = {}
     batch = slots // 2
     for n in range(min(batch, len(todo))):
-        copy_in(n).start()
-    for n, (entry, alongs, out_ref, at, base_ref, base_at) in enumerate(todo):
+        coeffs_copy(n).start()
+        left_copy(n).start()
+    for n, (entry, alongs, out_ref, at, old) in enumerate(todo):
         slot = n % slots
         if n % batch == 0:
             for later in range(n + batch, min(n + 2 * batch, len(todo))):
-                copy_in(later).start()
+                coeffs_copy(later).start()
+                left_copy(later).start()
             here = range(n, min(n + batch, len(todo)))
             for now in here:
-                coeffs = right_coeffs(
-                    projectors_ref, group_of(place, *todo[now][0]) * GROUP, GROUP
-                )
+                coeffs_copy(now).wait()
+            for now in here:
+                both = coeffs[now % slots]
+                right = jnp.concatenate([both[:, :wide], both[:, wide:]], axis=0)
                 for along in todo[now][1]:
                     number, r = parts[todo[now][0], along]
                     rights[now, along] = jnp.dot(
-                        block_refs[number][r], coeffs, preferred_element_type=jnp.float32
+                        block_refs[number][r], right, preferred_element_type=jnp.float32
                     ).astype(jnp.bfloat16)
             for now in here:
-                copy_in(now).wait()
+                left_copy(now).wait()
         mixed = 0.0
         for along in alongs:
             mixed += jnp.dot(
@@ -331,64 +354,37 @@
                     mixed[(k + 1) * width : (k + 2) * width, columns],
                 )
             )
-        put(out_ref, at, blocks, base_ref, base_at)
-
-
-def near_kernel(work, left_ref, projectors_ref, own_ref, *refs):
-    near_ref, far_ref, lefts, sem = refs[len(work) :]
-    near_ref[:, len(NEAR) :] = own_ref[...]
-    targets = [(NEAR, near_ref, 0, None), (FAR, far_ref, 0, None)]
-    add_up(work, targets, left_ref, projectors_ref, refs[: len(work)], lefts, sem)
-
-
-def far_kernel(work, left_ref, projectors_ref, begun_ref, *refs):
-    out_ref, lefts, sem = refs[len(work) :]
-    targets = [(FAR, out_ref, 0, begun_ref)]
-    add_up(work, targets, left_ref, projectors_ref, refs[: len(work)], lefts, sem)
-
-
-def left_slots(left):
-    return [
-        pltpu.VMEM((2 * BATCH,) + left.shape[1:], left.dtype),
-        pltpu.SemaphoreType.DMA((2 * BATCH,)),
-    ]
-
-
-def near_exchange(work, left, projectors, own, blocks):
-    pieces, own_rows, _, both = own.shape
-    return pl.pallas_call(
-        functools.partial(near_kernel, work),
-        in_specs=[ANY] + [VMEM] * (2 + len(work)),
-        out_specs=[VMEM, VMEM],
+        put(out_ref, at, blocks, old)
+
+
+def exchange(work, before, sets, dtypes, left, blocks, bases):
+    pieces, _, _, both = bases[0].shape
+    own = left.shape[0] // GROUP - len(ENTRIES)
+    wide = GROUP * both // 2
+    return pl.pallas_call(
+        functools.partial(exchange_kernel, work, before, sets, own),
+        in_specs=[ANY] + [VMEM] * (len(work) + len(bases)),
+        out_specs=[VMEM] * len(sets),
         out_shape=[
-            sums_shape(len(NEAR) + own_rows, pieces, both, own.dtype),
-            sums_shape(len(FAR), pieces, both, jnp.float32),
-        ],
-        scratch_shapes=left_slots(left),
+            sums_shape(len(groups) + (own if groups is EARLY else 0), pieces, both, dtype)
+            for groups, dtype in zip(sets, dtypes)
+        ],
+        scratch_shapes=[
+            pltpu.VMEM((2 * BATCH, 2, wide, left.shape[3]), left.dtype),
+            pltpu.VMEM((2 * BATCH, left.shape[2] - wide, left.shape[3]), left.dtype),
+            pltpu.SemaphoreType.DMA((2 * BATCH, 2)),
+        ],
         compiler_params=params(),
-        name="near_exchange",
-    )(left, projectors, own, *blocks)
-
-
-def far_exchange(work, left, projectors, begun, blocks):
-    pieces, _, _, both = begun.shape
-    return pl.pallas_call(
-        functools.partial(far_kernel, work),
-        in_specs=[ANY] + [VMEM] * (2 + len(work)),
-        out_specs=VMEM,
-        out_shape=sums_shape(len(FAR), pieces, both, jnp.bfloat16),
-        scratch_shapes=left_slots(left),
-        compiler_params=params(),
-        name="far_exchange",
-    )(left, projectors, begun, *blocks)
-
-
-def finish_kernel(near_ref, far_ref, denom_ref, out_ref, share_ref, rows_ref):
-    width = near_ref.shape[3] // 2
+        name="exchange",
+    )(left, *blocks, *bases)
+
+
+def finish_kernel(early_ref, late_ref, denom_ref, out_ref, share_ref, rows_ref):
+    width = early_ref.shape[3] // 2
     parts = share_ref.shape[1]
     lane = lax.broadcasted_iota(jnp.int32, (1, 2 * width), 1)
     start = 0
-    for arrived_ref in (near_ref, far_ref):
+    for arrived_ref in (early_ref, late_ref):
         total = arrived_ref[0].astype(jnp.float32)
         for piece in range(1, arrived_ref.shape[0]):
             total += arrived_ref[piece].astype(jnp.float32)
@@ -400,12 +396,11 @@
         columns = pl.ds(part * width, 2 * width)
         rows_ref[0, :, columns] = jnp.where(lane < width, even, pltpu.roll(odd, width, 1))
         rows_ref[1, :, columns] = jnp.where(lane < width, pltpu.roll(even, width, 1), odd)
-    shared = len(NEAR) + len(FAR)
-    own = near_ref.shape[1] - len(NEAR)
+    own = early_ref.shape[1] - len(EARLY)
     place = my_place()
-    groups = [group_of(place, *entry) for entry in NEAR]
-    groups += [shared + n for n in range(own)]
-    groups += [group_of(place, *entry) for entry in FAR]
+    groups = [group_of(place, *entry) for entry in EARLY]
+    groups += [len(ENTRIES) + n for n in range(own)]
+    groups += [group_of(place, *entry) for entry in LATE]
     for n, group in enumerate(groups):
         for k in range(GROUP):
             row = pl.ds(group * GROUP + k, 1)
@@ -414,8 +409,8 @@
             )
 
 
-def finish(near, far, denom):
-    pieces, _, _, both = near.shape
+def finish(early, late, denom):
+    pieces, _, _, both = late.shape
     parts = both // 2 // pieces
     pair_rows = denom.shape[0]
     return pl.pallas_call(
@@ -429,7 +424,7 @@
         ],
         compiler_params=params(),
         name="finish",
-    )(near, far, denom)
+    )(early, late, denom)
 
 
 def denominators_kernel(first_index, second_index, occ_ref, energy_ref, out_ref, base_ref):
@@ -524,24 +519,39 @@
     def work_of(*shifts):
         return tuple((along, shift, core) for shift, core in shifts for along in range(2))
 
-    near_work = work_of((1, 0), (-1, 0), (0, 0), (0, 1), (1, 1), (-1, 1))
-    far_work = work_of((2, 0), (2, 1))
-    chosen = dict(zip(near_work + far_work, choose(near_work + far_work, gathered)))
-    follows = {(1, 1): (1, 0), (-1, 1): (-1, 0), (2, 0): (1, 1), (2, 1): (-1, 1)}
+    def touched(*works):
+        return {entry for work in works for entry, _ in parts_of(work)}
+
+    works = (
+        work_of((1, 0), (-1, 0), (0, 0), (0, 1)),
+        work_of((2, 0), (2, 1)),
+        work_of((1, 1), (-1, 1)),
+    )
+    chosen = dict(zip(sum(works, ()), choose(sum(works, ()), gathered)))
     arrived = {}
-    for along, shift, core in near_work + far_work:
-        one = chosen[along, shift, core]
-        if (shift, core) in follows:
-            one = after(one, arrived[(along, *follows[shift, core])])
-        if (shift, core) != (0, 0):
-            one = step_along(1 - along, one, shift, core)
-        arrived[along, shift, core] = one
-    near, begun = near_exchange(near_work, left, projectors, own, [arrived[one] for one in near_work])
-    near = after(near, arrived[0, 2, 0], arrived[1, 2, 0])
-    near = lax.all_to_all(near, "aux", split_axis=0, concat_axis=0, tiled=True)
-    far = far_exchange(far_work, left, projectors, begun, [arrived[one] for one in far_work])
-    far = lax.all_to_all(after(far, near), "aux", split_axis=0, concat_axis=0, tiled=True)
-    return finish(near, far, denom)
+
+    def send(work, behind):
+        for along, shift, core in work:
+            one = chosen[along, shift, core]
+            if (shift, core) in behind:
+                one = after(one, arrived[(along, *behind[shift, core])])
+            if (shift, core) != (0, 0):
+                one = step_along(1 - along, one, shift, core)
+            arrived[along, shift, core] = one
+        return [arrived[one] for one in work]
+
+    wide, narrow = jnp.float32, jnp.bfloat16
+    blocks = send(works[0], {})
+    sums = exchange(works[0], (), (EARLY, LATE), (wide, wide), left, blocks, [own])
+    blocks = send(works[1], {(2, 0): (1, 0), (2, 1): (-1, 0)})
+    early, late = exchange(
+        works[1], touched(works[0]), (EARLY, LATE), (wide, wide), left, blocks, sums
+    )
+    early = lax.psum_scatter(early, "aux", scatter_dimension=0, tiled=True)
+    blocks = send(works[2], {})
+    (late,) = exchange(works[2], touched(*works[:2]), (LATE,), (narrow,), left, blocks, [late])
+    late = lax.all_to_all(late, "aux", split_axis=0, concat_axis=0, tiled=True)
+    return finish(early, late, denom)
 
 
 def solution(mesh):

time: 169 us -> 163 us (0.964)
  the two profiles are of different devices: /device:TPU:11 before, /device:TPU:1 now
where the time goes in v2:
time: 163 us; the launch traced here: 162 us
  waiting for transfers between devices  52.7 us (32%)
  starting transfers between devices  47 us (29%)
  Pallas kernels  43.4 us (27%)
  between operations  13.6 us (8%)
  local copies, waits for them, and re-layouts  5.77 us (4%)
    ppermute x23, starting transfers between devices, moved(): lax.ppermute(array, 'pair', [(at(x, y, c), at(x + dx, y + dy, c + core))...  42.9 us
    ppermute x23, waiting for transfers between devices, moved(): lax.ppermute(array, 'pair', [(at(x, y, c), at(x + dx, y + dy, c + core))...  38.3 us
    pallas_call x1, Pallas kernels, left_of(): pl.pallas_call(left_kernel, in_specs=[SMEM] * 2 + [VMEM] * 3, out_specs=[...  19.1 us
    pallas_call x3, Pallas kernels, exchange(): pl.pallas_call(functools.partial(exchange_kernel, work, before, sets, own...  18.8 us
    all_to_all x1, waiting for transfers between devices, on_device(): late = lax.all_to_all(late, 'aux', split_axis=0, concat_axis=0, tiled=True)  14.3 us
    unnamed x11, local copies, waits for them, and re-layouts  4.87 us
    all_to_all x1, starting transfers between devices, on_device(): late = lax.all_to_all(late, 'aux', split_axis=0, concat_axis=0, tiled=True)  4.07 us
  transfers between devices with their start and end apart: 25, of which 11 were waited for; matrix products, arithmetic and copies ran while one was open for 0% of the time, Pallas kernels for 21%

profile of v2, /device:TPU:1, one launch (start us, length us, event | category | flops | bytes accessed | tf_op | source)
XLA Modules:
  0.0 162.4 jit_solution(7368943378059302128)
XLA Ops:
  7.5 3.3 %collective-permute-start = (bf16[16,128]{1,0:T(8,128)(2,1)S(1)}, bf16[16,128]{1,0:T(8,128)(2,1)S(1)}, u32[]{:S(2)}, u32[]{:S(2)}) collective-permute-start(bf16[16,128]{1,0:T(8,128)(2,1)S(1)} %broadcast_in_dim.2.wanted_ref), channel_id=1, source_target_pairs={{0,1},{1,0},{2,3},{3,2},{4,5},{5,4},{6,7},{7,6},{8,9},{9,8},{10,11... | collective-permute-start | bytes 12296 | tf_op jit(solution)/shard_map/ppermute | solution.py:484
  14.2 2.7 %collective-permute-start.2 = (bf16[8,528,128]{2,1,0:T(8,128)(2,1)S(1)}, bf16[8,528,128]{2,1,0:T(8,128)(2,1)S(1)}, u32[]{:S(2)}, u32[]{:S(2)}) collective-permute-start(bf16[8,528,128]{2,1,0:T(8,128)(2,1)S(1)} %get-tuple-element.33.first_ref.refs_0_), channel_id=1, source_target_pairs={{0,24},{1,25},{2,26},{3,27},{4,28},{5,29},{6,30},{7,31},{8,0},{9,1... | collective-permute-start | bytes 3244040 | tf_op jit(solution)/shard_map/ppermute | solution.py:484
  16.9 2.7 %collective-permute-start.4 = (bf16[8,528,128]{2,1,0:T(8,128)(2,1)S(1)}, bf16[8,528,128]{2,1,0:T(8,128)(2,1)S(1)}, u32[]{:S(2)}, u32[]{:S(2)}) collective-permute-start(bf16[8,528,128]{2,1,0:T(8,128)(2,1)S(1)} %get-tuple-element.34.second_ref.refs_5_), channel_id=1, source_target_pairs={{0,6},{1,7},{2,0},{3,1},{4,2},{5,3},{6,4},{7,5},{8,14},{9,15},{10,... | collective-permute-start | bytes 3244040 | tf_op jit(solution)/shard_map/ppermute | solution.py:484
  19.6 2.3 %copy-done = bf16[136,128,128]{2,1,0:T(8,128)(2,1)S(1)} copy-done((bf16[136,128,128]{2,1,0:T(8,128)(2,1)S(1)}, bf16[136,128,128]{2,1,0:T(8,128)(2,1)}, u32[]{:S(2)}) %copy-start) | copy-done | bytes 4456472
  21.8 19.1 %left.1 = (bf16[136,2,320,512]{3,2,1,0:T(8,128)(2,1)}, f32[8,2,16,128]{3,2,1,0:T(8,128)S(1)}) custom-call(s32[136]{0:T(256)S(1)} %and_select_fusion.1.left_index, s32[136]{0:T(256)S(1)} %get-tuple-element.62.right_index, bf16[8,528,128]{2,1,0:T(8,128)(2,1)S(1)} %get-tuple-element.33.first_ref.refs_0_, ...), custom_call_target="tpu_custom_call" | custom-call | tf_op jit(solution)/shard_map/left/pallas_call | solution.py:251
  42.8 2.7 %collective-permute-start.6 = (bf16[4,528,128]{2,1,0:T(8,128)(2,1)S(1)}, bf16[4,528,128]{2,1,0:T(8,128)(2,1)S(1)}, u32[]{:S(2)}, u32[]{:S(2)}) collective-permute-start(bf16[4,528,128]{2,1,0:T(8,128)(2,1)S(1)} %get-tuple-element.38), channel_id=1, source_target_pairs={{0,24},{1,25},{2,26},{3,27},{4,28},{5,29},{6,30},{7,31},{8,0},{9,1... | collective-permute-start | bytes 1622024 | tf_op jit(solution)/shard_map/ppermute | solution.py:484
  45.5 2.7 %collective-permute-start.8 = (bf16[4,528,128]{2,1,0:T(8,128)(2,1)S(1)}, bf16[4,528,128]{2,1,0:T(8,128)(2,1)S(1)}, u32[]{:S(2)}, u32[]{:S(2)}) collective-permute-start(bf16[4,528,128]{2,1,0:T(8,128)(2,1)S(1)} %get-tuple-element.40), channel_id=1, source_target_pairs={{0,6},{1,7},{2,0},{3,1},{4,2},{5,3},{6,4},{7,5},{8,14},{9,15},{10,... | collective-permute-start | bytes 1622024 | tf_op jit(solution)/shard_map/ppermute | solution.py:484
  48.1 7.8 %collective-permute-done.5.refs_3_ = bf16[4,528,128]{2,1,0:T(8,128)(2,1)S(1)} collective-permute-done((bf16[4,528,128]{2,1,0:T(8,128)(2,1)S(1)}, bf16[4,528,128]{2,1,0:T(8,128)(2,1)S(1)}, u32[]{:S(2)}, u32[]{:S(2)}) %collective-permute-start.5) | collective-permute-done | bytes 540704 | tf_op jit(solution)/shard_map/ppermute | solution.py:484
  55.9 2.1 %collective-permute-done.7.refs_8_ = bf16[4,528,128]{2,1,0:T(8,128)(2,1)S(1)} collective-permute-done((bf16[4,528,128]{2,1,0:T(8,128)(2,1)S(1)}, bf16[4,528,128]{2,1,0:T(8,128)(2,1)S(1)}, u32[]{:S(2)}, u32[]{:S(2)}) %collective-permute-start.7) | collective-permute-done | bytes 540704 | tf_op jit(solution)/shard_map/ppermute | solution.py:484
  60.3 2.5 %collective-permute-start.13 = (bf16[4,512,128]{2,1,0:T(8,128)(2,1)S(1)}, bf16[4,512,128]{2,1,0:T(8,128)(2,1)S(1)}, u32[]{:S(2)}, u32[]{:S(2)}) collective-permute-start(bf16[4,512,128]{2,1,0:T(8,128)(2,1)S(1)} %get-tuple-element.46), channel_id=1, source_target_pairs={{0,6},{1,7},{2,0},{3,1},{4,2},{5,3},{6,4},{7,5},{8,14},{9,15},{10,... | collective-permute-start | bytes 1572872 | tf_op jit(solution)/shard_map/ppermute | solution.py:484
  62.8 2.6 %collective-permute-start.15 = (bf16[4,512,128]{2,1,0:T(8,128)(2,1)S(1)}, bf16[4,512,128]{2,1,0:T(8,128)(2,1)S(1)}, u32[]{:S(2)}, u32[]{:S(2)}) collective-permute-start(bf16[4,512,128]{2,1,0:T(8,128)(2,1)S(1)} %get-tuple-element.48), channel_id=1, source_target_pairs={{0,24},{1,25},{2,26},{3,27},{4,28},{5,29},{6,30},{7,31},{8,0},{9,1... | collective-permute-start | bytes 1572872 | tf_op jit(solution)/shard_map/ppermute | solution.py:484
  65.4 4.4 %collective-permute-start.17 = (bf16[4,512,128]{2,1,0:T(8,128)(2,1)S(1)}, bf16[4,512,128]{2,1,0:T(8,128)(2,1)S(1)}, u32[]{:S(2)}, u32[]{:S(2)}) collective-permute-start(bf16[4,512,128]{2,1,0:T(8,128)(2,1)S(1)} %get-tuple-element.51), channel_id=1, source_target_pairs={{0,1},{1,0},{2,3},{3,2},{4,5},{5,4},{6,7},{7,6},{8,9},{9,8},{10,11... | collective-permute-start | bytes 1572872 | tf_op jit(solution)/shard_map/ppermute | solution.py:484
  71.4 4.2 %collective-permute-start.18 = (bf16[4,512,128]{2,1,0:T(8,128)(2,1)S(1)}, bf16[4,512,128]{2,1,0:T(8,128)(2,1)S(1)}, u32[]{:S(2)}, u32[]{:S(2)}) collective-permute-start(bf16[4,512,128]{2,1,0:T(8,128)(2,1)S(1)} %get-tuple-element.52), channel_id=1, source_target_pairs={{0,1},{1,0},{2,3},{3,2},{4,5},{5,4},{6,7},{7,6},{8,9},{9,8},{10,11... | collective-permute-start | bytes 1572872 | tf_op jit(solution)/shard_map/ppermute | solution.py:484
  76.2 4.1 %collective-permute-start.14 = (bf16[4,512,128]{2,1,0:T(8,128)(2,1)S(1)}, bf16[4,512,128]{2,1,0:T(8,128)(2,1)S(1)}, u32[]{:S(2)}, u32[]{:S(2)}) collective-permute-start(bf16[4,512,128]{2,1,0:T(8,128)(2,1)S(1)} %after.6), channel_id=1, source_target_pairs={{0,5},{1,4},{2,7},{3,6},{4,1},{5,0},{6,3},{7,2},{8,13},{9,12},{10,... | collective-permute-start | bytes 1572872 | tf_op jit(solution)/shard_map/ppermute | solution.py:484
  80.3 2.4 %collective-permute-start.16 = (bf16[4,512,128]{2,1,0:T(8,128)(2,1)S(1)}, bf16[4,512,128]{2,1,0:T(8,128)(2,1)S(1)}, u32[]{:S(2)}, u32[]{:S(2)}) collective-permute-start(bf16[4,512,128]{2,1,0:T(8,128)(2,1)S(1)} %after.7), channel_id=1, source_target_pairs={{0,17},{1,16},{2,19},{3,18},{4,21},{5,20},{6,23},{7,22},{8,25},{9,... | collective-permute-start | bytes 1572872 | tf_op jit(solution)/shard_map/ppermute | solution.py:484
  82.7 7.9 %exchange.3 = (f32[8,22,16,128]{3,2,1,0:T(8,128)S(1)}, f32[8,12,16,128]{3,2,1,0:T(8,128)S(1)}) custom-call(bf16[136,2,320,512]{3,2,1,0:T(8,128)(2,1)} %get-tuple-element.35.left_ref, bf16[4,512,128]{2,1,0:T(8,128)(2,1)S(1)} %collective-permute-done.9.__1_.refs_0_, bf16[4,512,128]{2,1,0:T(8,128)(2,1)S(1)} %collective-permute-done.11.__1_.refs_1_, ...), custom_call_target="tpu_custom_call" | custom-call | tf_op jit(solution)/shard_map/exchange/pallas_call | solution.py:364
  90.6 11.4 %collective-permute-done.14.refs_2_ = bf16[4,512,128]{2,1,0:T(8,128)(2,1)S(1)} collective-permute-done((bf16[4,512,128]{2,1,0:T(8,128)(2,1)S(1)}, bf16[4,512,128]{2,1,0:T(8,128)(2,1)S(1)}, u32[]{:S(2)}, u32[]{:S(2)}) %collective-permute-start.14) | collective-permute-done | bytes 524320 | tf_op jit(solution)/shard_map/ppermute | solution.py:484
  102.5 5.6 %exchange.4 = (f32[8,22,16,128]{3,2,1,0:T(8,128)}, f32[8,12,16,128]{3,2,1,0:T(8,128)S(1)}) custom-call(bf16[136,2,320,512]{3,2,1,0:T(8,128)(2,1)} %get-tuple-element.35.left_ref, bf16[4,512,128]{2,1,0:T(8,128)(2,1)S(1)} %collective-permute-done.10.refs_0_, bf16[4,512,128]{2,1,0:T(8,128)(2,1)S(1)} %collective-permute-done.12.refs_1_, ...), custom_call_target="tpu_custom_call" | custom-call | tf_op jit(solution)/shard_map/exchange/pallas_call | solution.py:364
  108.5 5.2 %collective-permute-start.21 = (bf16[4,512,128]{2,1,0:T(8,128)(2,1)S(1)}, bf16[4,512,128]{2,1,0:T(8,128)(2,1)S(1)}, u32[]{:S(2)}, u32[]{:S(2)}) collective-permute-start(bf16[4,512,128]{2,1,0:T(8,128)(2,1)S(1)} %get-tuple-element.58), channel_id=1, source_target_pairs={{0,7},{1,6},{2,1},{3,0},{4,3},{5,2},{6,5},{7,4},{8,15},{9,14},{10,... | collective-permute-start | bytes 1572872 | tf_op jit(solution)/shard_map/ppermute | solution.py:484
  115.7 7.2 %collective-permute-done.19.refs_0_ = bf16[4,512,128]{2,1,0:T(8,128)(2,1)S(1)} collective-permute-done((bf16[4,512,128]{2,1,0:T(8,128)(2,1)S(1)}, bf16[4,512,128]{2,1,0:T(8,128)(2,1)S(1)}, u32[]{:S(2)}, u32[]{:S(2)}) %collective-permute-start.19) | collective-permute-done | bytes 524320 | tf_op jit(solution)/shard_map/ppermute | solution.py:484
  124.8 3.4 %collective-permute-done.22.refs_3_ = bf16[4,512,128]{2,1,0:T(8,128)(2,1)S(1)} collective-permute-done((bf16[4,512,128]{2,1,0:T(8,128)(2,1)S(1)}, bf16[4,512,128]{2,1,0:T(8,128)(2,1)S(1)}, u32[]{:S(2)}, u32[]{:S(2)}) %collective-permute-start.22) | collective-permute-done | bytes 524320 | tf_op jit(solution)/shard_map/ppermute | solution.py:484
  128.2 5.4 %exchange.5 = bf16[8,12,16,128]{3,2,1,0:T(8,128)(2,1)} custom-call(bf16[136,2,320,512]{3,2,1,0:T(8,128)(2,1)} %get-tuple-element.35.left_ref, bf16[4,512,128]{2,1,0:T(8,128)(2,1)S(1)} %collective-permute-done.19.refs_0_, bf16[4,512,128]{2,1,0:T(8,128)(2,1)S(1)} %collective-permute-done.20.refs_1_, bf16[4,512,128]{2,1,0:T(8,128)(2,1)S(1)} %collective-permute-done.21.refs_2_, ...), custom_call_target="tpu_custom_call" | custom-call | tf_op jit(solution)/shard_map/exchange/pallas_call | solution.py:364
  133.6 4.1 %all-to-all-start = ((bf16[8,12,16,128]{3,2,1,0:T(8,128)(2,1)}), bf16[8,12,16,128]{3,2,1,0:T(8,128)(2,1)S(1)}, u32[]{:S(2)}, u32[]{:S(2)}) async-start(bf16[8,12,16,128]{3,2,1,0:T(8,128)(2,1)} %exchange.5), calls=%async_computation.1 | async-start | bytes 786432 | tf_op jit(solution)/shard_map/all_to_all | solution.py:553
  139.1 14.3 %all-to-all-done.late_ref = bf16[8,12,16,128]{3,2,1,0:T(8,128)(2,1)S(1)} async-done(((bf16[8,12,16,128]{3,2,1,0:T(8,128)(2,1)}), bf16[8,12,16,128]{3,2,1,0:T(8,128)(2,1)S(1)}, u32[]{:S(2)}, u32[]{:S(2)}) %all-to-all-start) | async-done | bytes 393248 | tf_op jit(solution)/shard_map/all_to_all | solution.py:553
  (57 shorter events, 18.9 us)
Async XLA Ops:
  6.5 146.9 %reduce-scatter.2.cloned.1.call-start = ((), (), s32[]{:S(2)}) async-start(), calls=%async_computation.2 | async-start | bytes 1622016 | tf_op jit(solution)/shard_map/reduce_scatter | solution.py:550
  14.1 26.8 %collective-permute-start.1 = (bf16[8,528,128]{2,1,0:T(8,128)(2,1)S(1)}, bf16[8,528,128]{2,1,0:T(8,128)(2,1)S(1)}, u32[]{:S(2)}, u32[]{:S(2)}) collective-permute-start(bf16[8,528,128]{2,1,0:T(8,128)(2,1)S(1)} %get-tuple-element.33.first_ref.refs_0_), channel_id=1, source_target_pairs={{0,8},{1,9},{2,10},{3,11},{4,12},{5,13},{6,14},{7,15},{8,16},{9,17... | collective-permute-start | bytes 3244040 | tf_op jit(solution)/shard_map/ppermute | solution.py:484
  14.2 26.8 %collective-permute-start.2 = (bf16[8,528,128]{2,1,0:T(8,128)(2,1)S(1)}, bf16[8,528,128]{2,1,0:T(8,128)(2,1)S(1)}, u32[]{:S(2)}, u32[]{:S(2)}) collective-permute-start(bf16[8,528,128]{2,1,0:T(8,128)(2,1)S(1)} %get-tuple-element.33.first_ref.refs_0_), channel_id=1, source_target_pairs={{0,24},{1,25},{2,26},{3,27},{4,28},{5,29},{6,30},{7,31},{8,0},{9,1... | collective-permute-start | bytes 3244040 | tf_op jit(solution)/shard_map/ppermute | solution.py:484
  16.9 25.7 %collective-permute-start.3 = (bf16[8,528,128]{2,1,0:T(8,128)(2,1)S(1)}, bf16[8,528,128]{2,1,0:T(8,128)(2,1)S(1)}, u32[]{:S(2)}, u32[]{:S(2)}) collective-permute-start(bf16[8,528,128]{2,1,0:T(8,128)(2,1)S(1)} %get-tuple-element.34.second_ref.refs_5_), channel_id=1, source_target_pairs={{0,2},{1,3},{2,4},{3,5},{4,6},{5,7},{6,0},{7,1},{8,10},{9,11},{10,... | collective-permute-start | bytes 3244040 | tf_op jit(solution)/shard_map/ppermute | solution.py:484
  16.9 25.7 %collective-permute-start.4 = (bf16[8,528,128]{2,1,0:T(8,128)(2,1)S(1)}, bf16[8,528,128]{2,1,0:T(8,128)(2,1)S(1)}, u32[]{:S(2)}, u32[]{:S(2)}) collective-permute-start(bf16[8,528,128]{2,1,0:T(8,128)(2,1)S(1)} %get-tuple-element.34.second_ref.refs_5_), channel_id=1, source_target_pairs={{0,6},{1,7},{2,0},{3,1},{4,2},{5,3},{6,4},{7,5},{8,14},{9,15},{10,... | collective-permute-start | bytes 3244040 | tf_op jit(solution)/shard_map/ppermute | solution.py:484
  42.7 13.2 %collective-permute-start.5 = (bf16[4,528,128]{2,1,0:T(8,128)(2,1)S(1)}, bf16[4,528,128]{2,1,0:T(8,128)(2,1)S(1)}, u32[]{:S(2)}, u32[]{:S(2)}) collective-permute-start(bf16[4,528,128]{2,1,0:T(8,128)(2,1)S(1)} %get-tuple-element.37), channel_id=1, source_target_pairs={{0,8},{1,9},{2,10},{3,11},{4,12},{5,13},{6,14},{7,15},{8,16},{9,17... | collective-permute-start | bytes 1622024 | tf_op jit(solution)/shard_map/ppermute | solution.py:484
  42.8 13.2 %collective-permute-start.6 = (bf16[4,528,128]{2,1,0:T(8,128)(2,1)S(1)}, bf16[4,528,128]{2,1,0:T(8,128)(2,1)S(1)}, u32[]{:S(2)}, u32[]{:S(2)}) collective-permute-start(bf16[4,528,128]{2,1,0:T(8,128)(2,1)S(1)} %get-tuple-element.38), channel_id=1, source_target_pairs={{0,24},{1,25},{2,26},{3,27},{4,28},{5,29},{6,30},{7,31},{8,0},{9,1... | collective-permute-start | bytes 1622024 | tf_op jit(solution)/shard_map/ppermute | solution.py:484
  45.4 12.6 %collective-permute-start.7 = (bf16[4,528,128]{2,1,0:T(8,128)(2,1)S(1)}, bf16[4,528,128]{2,1,0:T(8,128)(2,1)S(1)}, u32[]{:S(2)}, u32[]{:S(2)}) collective-permute-start(bf16[4,528,128]{2,1,0:T(8,128)(2,1)S(1)} %get-tuple-element.39), channel_id=1, source_target_pairs={{0,2},{1,3},{2,4},{3,5},{4,6},{5,7},{6,0},{7,1},{8,10},{9,11},{10,... | collective-permute-start | bytes 1622024 | tf_op jit(solution)/shard_map/ppermute | solution.py:484
  45.5 12.6 %collective-permute-start.8 = (bf16[4,528,128]{2,1,0:T(8,128)(2,1)S(1)}, bf16[4,528,128]{2,1,0:T(8,128)(2,1)S(1)}, u32[]{:S(2)}, u32[]{:S(2)}) collective-permute-start(bf16[4,528,128]{2,1,0:T(8,128)(2,1)S(1)} %get-tuple-element.40), channel_id=1, source_target_pairs={{0,6},{1,7},{2,0},{3,1},{4,2},{5,3},{6,4},{7,5},{8,14},{9,15},{10,... | collective-permute-start | bytes 1622024 | tf_op jit(solution)/shard_map/ppermute | solution.py:484
  60.0 11.4 %collective-permute-start.9 = (bf16[4,512,128]{2,1,0:T(8,128)(2,1)S(1)}, bf16[4,512,128]{2,1,0:T(8,128)(2,1)S(1)}, u32[]{:S(2)}, u32[]{:S(2)}) collective-permute-start(bf16[4,512,128]{2,1,0:T(8,128)(2,1)S(1)} %get-tuple-element.42), channel_id=1, source_target_pairs={{0,2},{1,3},{2,4},{3,5},{4,6},{5,7},{6,0},{7,1},{8,10},{9,11},{10,... | collective-permute-start | bytes 1572872 | tf_op jit(solution)/shard_map/ppermute | solution.py:484
  60.3 15.3 %collective-permute-start.11 = (bf16[4,512,128]{2,1,0:T(8,128)(2,1)S(1)}, bf16[4,512,128]{2,1,0:T(8,128)(2,1)S(1)}, u32[]{:S(2)}, u32[]{:S(2)}) collective-permute-start(bf16[4,512,128]{2,1,0:T(8,128)(2,1)S(1)} %get-tuple-element.44), channel_id=1, source_target_pairs={{0,8},{1,9},{2,10},{3,11},{4,12},{5,13},{6,14},{7,15},{8,16},{9,17... | collective-permute-start | bytes 1572872 | tf_op jit(solution)/shard_map/ppermute | solution.py:484
  60.3 15.8 %collective-permute-start.13 = (bf16[4,512,128]{2,1,0:T(8,128)(2,1)S(1)}, bf16[4,512,128]{2,1,0:T(8,128)(2,1)S(1)}, u32[]{:S(2)}, u32[]{:S(2)}) collective-permute-start(bf16[4,512,128]{2,1,0:T(8,128)(2,1)S(1)} %get-tuple-element.46), channel_id=1, source_target_pairs={{0,6},{1,7},{2,0},{3,1},{4,2},{5,3},{6,4},{7,5},{8,14},{9,15},{10,... | collective-permute-start | bytes 1572872 | tf_op jit(solution)/shard_map/ppermute | solution.py:484
  62.8 13.4 %collective-permute-start.15 = (bf16[4,512,128]{2,1,0:T(8,128)(2,1)S(1)}, bf16[4,512,128]{2,1,0:T(8,128)(2,1)S(1)}, u32[]{:S(2)}, u32[]{:S(2)}) collective-permute-start(bf16[4,512,128]{2,1,0:T(8,128)(2,1)S(1)} %get-tuple-element.48), channel_id=1, source_target_pairs={{0,24},{1,25},{2,26},{3,27},{4,28},{5,29},{6,30},{7,31},{8,0},{9,1... | collective-permute-start | bytes 1572872 | tf_op jit(solution)/shard_map/ppermute | solution.py:484
  65.4 14.9 %collective-permute-start.17 = (bf16[4,512,128]{2,1,0:T(8,128)(2,1)S(1)}, bf16[4,512,128]{2,1,0:T(8,128)(2,1)S(1)}, u32[]{:S(2)}, u32[]{:S(2)}) collective-permute-start(bf16[4,512,128]{2,1,0:T(8,128)(2,1)S(1)} %get-tuple-element.51), channel_id=1, source_target_pairs={{0,1},{1,0},{2,3},{3,2},{4,5},{5,4},{6,7},{7,6},{8,9},{9,8},{10,11... | collective-permute-start | bytes 1572872 | tf_op jit(solution)/shard_map/ppermute | solution.py:484
  71.4 11.3 %collective-permute-start.18 = (bf16[4,512,128]{2,1,0:T(8,128)(2,1)S(1)}, bf16[4,512,128]{2,1,0:T(8,128)(2,1)S(1)}, u32[]{:S(2)}, u32[]{:S(2)}) collective-permute-start(bf16[4,512,128]{2,1,0:T(8,128)(2,1)S(1)} %get-tuple-element.52), channel_id=1, source_target_pairs={{0,1},{1,0},{2,3},{3,2},{4,5},{5,4},{6,7},{7,6},{8,9},{9,8},{10,11... | collective-permute-start | bytes 1572872 | tf_op jit(solution)/shard_map/ppermute | solution.py:484
  75.6 15.0 %collective-permute-start.10 = (bf16[4,512,128]{2,1,0:T(8,128)(2,1)S(1)}, bf16[4,512,128]{2,1,0:T(8,128)(2,1)S(1)}, u32[]{:S(2)}, u32[]{:S(2)}) collective-permute-start(bf16[4,512,128]{2,1,0:T(8,128)(2,1)S(1)} %after.4), channel_id=1, source_target_pairs={{0,4},{1,5},{2,6},{3,7},{4,0},{5,1},{6,2},{7,3},{8,12},{9,13},{10,... | collective-permute-start | bytes 1572872 | tf_op jit(solution)/shard_map/ppermute | solution.py:484
  76.2 14.4 %collective-permute-start.12 = (bf16[4,512,128]{2,1,0:T(8,128)(2,1)S(1)}, bf16[4,512,128]{2,1,0:T(8,128)(2,1)S(1)}, u32[]{:S(2)}, u32[]{:S(2)}) collective-permute-start(bf16[4,512,128]{2,1,0:T(8,128)(2,1)S(1)} %after.5), channel_id=1, source_target_pairs={{0,16},{1,17},{2,18},{3,19},{4,20},{5,21},{6,22},{7,23},{8,24},{9,... | collective-permute-start | bytes 1572872 | tf_op jit(solution)/shard_map/ppermute | solution.py:484
  76.2 25.8 %collective-permute-start.14 = (bf16[4,512,128]{2,1,0:T(8,128)(2,1)S(1)}, bf16[4,512,128]{2,1,0:T(8,128)(2,1)S(1)}, u32[]{:S(2)}, u32[]{:S(2)}) collective-permute-start(bf16[4,512,128]{2,1,0:T(8,128)(2,1)S(1)} %after.6), channel_id=1, source_target_pairs={{0,5},{1,4},{2,7},{3,6},{4,1},{5,0},{6,3},{7,2},{8,13},{9,12},{10,... | collective-permute-start | bytes 1572872 | tf_op jit(solution)/shard_map/ppermute | solution.py:484
  80.3 22.3 %collective-permute-start.16 = (bf16[4,512,128]{2,1,0:T(8,128)(2,1)S(1)}, bf16[4,512,128]{2,1,0:T(8,128)(2,1)S(1)}, u32[]{:S(2)}, u32[]{:S(2)}) collective-permute-start(bf16[4,512,128]{2,1,0:T(8,128)(2,1)S(1)} %after.7), channel_id=1, source_target_pairs={{0,17},{1,16},{2,19},{3,18},{4,21},{5,20},{6,23},{7,22},{8,25},{9,... | collective-permute-start | bytes 1572872 | tf_op jit(solution)/shard_map/ppermute | solution.py:484
  108.1 14.8 %collective-permute-start.19 = (bf16[4,512,128]{2,1,0:T(8,128)(2,1)S(1)}, bf16[4,512,128]{2,1,0:T(8,128)(2,1)S(1)}, u32[]{:S(2)}, u32[]{:S(2)}) collective-permute-start(bf16[4,512,128]{2,1,0:T(8,128)(2,1)S(1)} %get-tuple-element.56), channel_id=1, source_target_pairs={{0,3},{1,2},{2,5},{3,4},{4,7},{5,6},{6,1},{7,0},{8,11},{9,10},{10,... | collective-permute-start | bytes 1572872 | tf_op jit(solution)/shard_map/ppermute | solution.py:484
  108.5 16.3 %collective-permute-start.20 = (bf16[4,512,128]{2,1,0:T(8,128)(2,1)S(1)}, bf16[4,512,128]{2,1,0:T(8,128)(2,1)S(1)}, u32[]{:S(2)}, u32[]{:S(2)}) collective-permute-start(bf16[4,512,128]{2,1,0:T(8,128)(2,1)S(1)} %get-tuple-element.57), channel_id=1, source_target_pairs={{0,9},{1,8},{2,11},{3,10},{4,13},{5,12},{6,15},{7,14},{8,17},{9,16... | collective-permute-start | bytes 1572872 | tf_op jit(solution)/shard_map/ppermute | solution.py:484
  108.5 16.2 %collective-permute-start.21 = (bf16[4,512,128]{2,1,0:T(8,128)(2,1)S(1)}, bf16[4,512,128]{2,1,0:T(8,128)(2,1)S(1)}, u32[]{:S(2)}, u32[]{:S(2)}) collective-permute-start(bf16[4,512,128]{2,1,0:T(8,128)(2,1)S(1)} %get-tuple-element.58), channel_id=1, source_target_pairs={{0,7},{1,6},{2,1},{3,0},{4,3},{5,2},{6,5},{7,4},{8,15},{9,14},{10,... | collective-permute-start | bytes 1572872 | tf_op jit(solution)/shard_map/ppermute | solution.py:484
  113.7 14.5 %collective-permute-start.22 = (bf16[4,512,128]{2,1,0:T(8,128)(2,1)S(1)}, bf16[4,512,128]{2,1,0:T(8,128)(2,1)S(1)}, u32[]{:S(2)}, u32[]{:S(2)}) collective-permute-start(bf16[4,512,128]{2,1,0:T(8,128)(2,1)S(1)} %get-tuple-element.59), channel_id=1, source_target_pairs={{0,25},{1,24},{2,27},{3,26},{4,29},{5,28},{6,31},{7,30},{8,1},{9,0... | collective-permute-start | bytes 1572872 | tf_op jit(solution)/shard_map/ppermute | solution.py:484
  133.6 19.9 %all-to-all-start = ((bf16[8,12,16,128]{3,2,1,0:T(8,128)(2,1)}), bf16[8,12,16,128]{3,2,1,0:T(8,128)(2,1)S(1)}, u32[]{:S(2)}, u32[]{:S(2)}) async-start(bf16[8,12,16,128]{3,2,1,0:T(8,128)(2,1)} %exchange.5), calls=%async_computation.1 | async-start | bytes 786432 | tf_op jit(solution)/shard_map/all_to_all | solution.py:553
  (6 other events, 28.0 us)
Sparse Core Ops, SparseCore 0:
  108.3 33.9 reduce-scatter.1

commit v3 on v2

--- a/solution.py
+++ b/solution.py
@@ -18,8 +18,8 @@
 VMEM = pl.BlockSpec(memory_space=pltpu.VMEM)
 ANY = pl.BlockSpec(memory_space=pl.ANY)
 ENTRIES = [(dx, dy, c) for c in range(CORES) for dx in RELS for dy in RELS]
-LATE = [entry for entry in ENTRIES if entry[2] == 1 and {1, -1} & set(entry[:2])]
-EARLY = [entry for entry in ENTRIES if entry not in LATE]
+EARLY = [entry for entry in ENTRIES if 2 not in entry and (entry[2] == 0 or entry == (0, 0, 1))]
+LATE = [entry for entry in ENTRIES if entry not in EARLY]
 
 
 def params(mib=20):
@@ -254,7 +254,7 @@
         out_specs=[ANY, VMEM],
         out_shape=[
             jax.ShapeDtypeStruct((pair_rows, 2, rows, half), jnp.bfloat16),
-            sums_shape(own, pieces, both, jnp.float32),
+            sums_shape(own, pieces, both, jnp.bfloat16),
         ],
         scratch_shapes=[
             pltpu.VMEM((2, batch, 2, rows, half), jnp.bfloat16),
@@ -542,12 +542,12 @@
 
     wide, narrow = jnp.float32, jnp.bfloat16
     blocks = send(works[0], {})
-    sums = exchange(works[0], (), (EARLY, LATE), (wide, wide), left, blocks, [own])
+    early, late = exchange(works[0], (), (EARLY, LATE), (narrow, wide), left, blocks, [own])
+    early = lax.all_to_all(early, "aux", split_axis=0, concat_axis=0, tiled=True)
     blocks = send(works[1], {(2, 0): (1, 0), (2, 1): (-1, 0)})
-    early, late = exchange(
-        works[1], touched(works[0]), (EARLY, LATE), (wide, wide), left, blocks, sums
+    (late,) = exchange(
+        works[1], touched(works[0]), (LATE,), (wide,), left, blocks, [after(late, early)]
     )
-    early = lax.psum_scatter(early, "aux", scatter_dimension=0, tiled=True)
     blocks = send(works[2], {})
     (late,) = exchange(works[2], touched(*works[:2]), (LATE,), (narrow,), left, blocks, [late])
     late = lax.all_to_all(late, "aux", split_axis=0, concat_axis=0, tiled=True)

time: 163 us -> 162 us (level)
  between operations: 13.6 us -> 0.27 us
  starting transfers between devices: 47 us -> 54.1 us
  Pallas kernels: 43.4 us -> 47.2 us
  local copies, waits for them, and re-layouts: 5.77 us -> 7.45 us
    ppermute x23, waiting for transfers between devices: 38.3 us -> 27.5 us  [moved(): lax.ppermute(array, 'pair', [(at(x, y, c), at(x + dx, y + dy, c + core))...]
    all_to_all x1, waiting for transfers between devices: 14.3 us -> 20.7 us  [on_device(): late = lax.all_to_all(late, 'aux', split_axis=0, concat_axis=0, tiled=True)]
    all_to_all x0 -> x1, starting transfers between devices: none -> 6.12 us  [on_device(): lax.all_to_all(early, 'aux', split_axis=0, concat_axis=0, tiled=True)]
    all_to_all x0 -> x1, waiting for transfers between devices: none -> 4.51 us  [on_device(): lax.all_to_all(early, 'aux', split_axis=0, concat_axis=0, tiled=True)]
    all_to_all x1, starting transfers between devices: 4.07 us -> 6.78 us  [on_device(): late = lax.all_to_all(late, 'aux', split_axis=0, concat_axis=0, tiled=True)]
    pallas_call x3, Pallas kernels: 18.8 us -> 20.9 us  [exchange(): pl.pallas_call(functools.partial(exchange_kernel, work, before, sets, own...]
    ppermute x23, starting transfers between devices: 42.9 us -> 41.2 us  [moved(): lax.ppermute(array, 'pair', [(at(x, y, c), at(x + dx, y + dy, c + core))...]
    unnamed x11 -> x21, local copies, waits for them, and re-layouts: 4.87 us -> 6.56 us
  transfers between devices with their start and end apart: 25 -> 25, of which waited for: 11 -> 9; matrix products, arithmetic and copies ran while one was open for 0% -> 0% of each run, Pallas kernels for 21% -> 21%
where the time goes in v3:
time: 162 us
  starting transfers between devices  54.1 us (33%)
  waiting for transfers between devices  52.7 us (33%)
  Pallas kernels  47.2 us (29%)
  local copies, waits for them, and re-layouts  7.45 us (5%)
    ppermute x23, starting transfers between devices, moved(): lax.ppermute(array, 'pair', [(at(x, y, c), at(x + dx, y + dy, c + core))...  41.2 us
    ppermute x23, waiting for transfers between devices, moved(): lax.ppermute(array, 'pair', [(at(x, y, c), at(x + dx, y + dy, c + core))...  27.5 us
    pallas_call x3, Pallas kernels, exchange(): pl.pallas_call(functools.partial(exchange_kernel, work, before, sets, own...  20.9 us
    all_to_all x1, waiting for transfers between devices, on_device(): late = lax.all_to_all(late, 'aux', split_axis=0, concat_axis=0, tiled=True)  20.7 us
    pallas_call x1, Pallas kernels, left_of(): pl.pallas_call(left_kernel, in_specs=[SMEM] * 2 + [VMEM] * 3, out_specs=[...  19.2 us
    all_to_all x1, starting transfers between devices, on_device(): late = lax.all_to_all(late, 'aux', split_axis=0, concat_axis=0, tiled=True)  6.78 us
    unnamed x21, local copies, waits for them, and re-layouts  6.56 us
    all_to_all x1, starting transfers between devices, on_device(): lax.all_to_all(early, 'aux', split_axis=0, concat_axis=0, tiled=True)  6.12 us
  transfers between devices with their start and end apart: 25, of which 9 were waited for; matrix products, arithmetic and copies ran while one was open for 0% of the time, Pallas kernels for 21%

profile of v3, /device:TPU:1, one launch (start us, length us, event | category | flops | bytes accessed | tf_op | source)
XLA Modules:
  0.0 161.7 jit_solution(17879574672351482833)
XLA Ops:
  0.9 3.3 %collective-permute-start = (bf16[16,128]{1,0:T(8,128)(2,1)S(1)}, bf16[16,128]{1,0:T(8,128)(2,1)S(1)}, u32[]{:S(2)}, u32[]{:S(2)}) collective-permute-start(bf16[16,128]{1,0:T(8,128)(2,1)S(1)} %broadcast_in_dim.2.wanted_ref), channel_id=1, source_target_pairs={{0,1},{1,0},{2,3},{3,2},{4,5},{5,4},{6,7},{7,6},{8,9},{9,8},{10,11... | collective-permute-start | bytes 12296 | tf_op jit(solution)/shard_map/ppermute | solution.py:484
  7.7 2.7 %collective-permute-start.2 = (bf16[8,528,128]{2,1,0:T(8,128)(2,1)S(1)}, bf16[8,528,128]{2,1,0:T(8,128)(2,1)S(1)}, u32[]{:S(2)}, u32[]{:S(2)}) collective-permute-start(bf16[8,528,128]{2,1,0:T(8,128)(2,1)S(1)} %get-tuple-element.31.first_ref.refs_0_), channel_id=1, source_target_pairs={{0,24},{1,25},{2,26},{3,27},{4,28},{5,29},{6,30},{7,31},{8,0},{9,1... | collective-permute-start | bytes 3244040 | tf_op jit(solution)/shard_map/ppermute | solution.py:484
  10.3 2.7 %collective-permute-start.4 = (bf16[8,528,128]{2,1,0:T(8,128)(2,1)S(1)}, bf16[8,528,128]{2,1,0:T(8,128)(2,1)S(1)}, u32[]{:S(2)}, u32[]{:S(2)}) collective-permute-start(bf16[8,528,128]{2,1,0:T(8,128)(2,1)S(1)} %get-tuple-element.32.second_ref.refs_5_), channel_id=1, source_target_pairs={{0,6},{1,7},{2,0},{3,1},{4,2},{5,3},{6,4},{7,5},{8,14},{9,15},{10,... | collective-permute-start | bytes 3244040 | tf_op jit(solution)/shard_map/ppermute | solution.py:484
  13.0 2.3 %copy-done = bf16[136,128,128]{2,1,0:T(8,128)(2,1)S(1)} copy-done((bf16[136,128,128]{2,1,0:T(8,128)(2,1)S(1)}, bf16[136,128,128]{2,1,0:T(8,128)(2,1)}, u32[]{:S(2)}) %copy-start) | copy-done | bytes 4456472
  15.3 19.2 %left.1 = (bf16[136,2,320,512]{3,2,1,0:T(8,128)(2,1)}, bf16[8,2,16,128]{3,2,1,0:T(8,128)(2,1)S(1)}) custom-call(s32[136]{0:T(256)S(1)} %and_select_fusion.1.left_index, s32[136]{0:T(256)S(1)} %get-tuple-element.58.right_index, bf16[8,528,128]{2,1,0:T(8,128)(2,1)S(1)} %get-tuple-element.31.first_ref.refs_0_, ...), custom_call_target="tpu_custom_call" | custom-call | tf_op jit(solution)/shard_map/left/pallas_call | solution.py:251
  36.2 2.7 %collective-permute-start.6 = (bf16[4,528,128]{2,1,0:T(8,128)(2,1)S(1)}, bf16[4,528,128]{2,1,0:T(8,128)(2,1)S(1)}, u32[]{:S(2)}, u32[]{:S(2)}) collective-permute-start(bf16[4,528,128]{2,1,0:T(8,128)(2,1)S(1)} %get-tuple-element.36), channel_id=1, source_target_pairs={{0,24},{1,25},{2,26},{3,27},{4,28},{5,29},{6,30},{7,31},{8,0},{9,1... | collective-permute-start | bytes 1622024 | tf_op jit(solution)/shard_map/ppermute | solution.py:484
  38.9 2.7 %collective-permute-start.8 = (bf16[4,528,128]{2,1,0:T(8,128)(2,1)S(1)}, bf16[4,528,128]{2,1,0:T(8,128)(2,1)S(1)}, u32[]{:S(2)}, u32[]{:S(2)}) collective-permute-start(bf16[4,528,128]{2,1,0:T(8,128)(2,1)S(1)} %get-tuple-element.38), channel_id=1, source_target_pairs={{0,6},{1,7},{2,0},{3,1},{4,2},{5,3},{6,4},{7,5},{8,14},{9,15},{10,... | collective-permute-start | bytes 1622024 | tf_op jit(solution)/shard_map/ppermute | solution.py:484
  41.6 7.8 %collective-permute-done.5.refs_3_ = bf16[4,528,128]{2,1,0:T(8,128)(2,1)S(1)} collective-permute-done((bf16[4,528,128]{2,1,0:T(8,128)(2,1)S(1)}, bf16[4,528,128]{2,1,0:T(8,128)(2,1)S(1)}, u32[]{:S(2)}, u32[]{:S(2)}) %collective-permute-start.5) | collective-permute-done | bytes 540704 | tf_op jit(solution)/shard_map/ppermute | solution.py:484
  51.5 3.4 %choose.1 = (bf16[4,512,128]{2,1,0:T(8,128)(2,1)S(1)}, bf16[4,512,128]{2,1,0:T(8,128)(2,1)S(1)}, bf16[4,512,128]{2,1,0:T(8,128)(2,1)S(1)}, bf16[4,512,128]{2,1,0...) custom-call(bf16[8,528,128]{2,1,0:T(8,128)(2,1)S(1)} %get-tuple-elem, ...), custom_call_target="tpu_custom_call" | custom-call | tf_op jit(solution)/shard_map/choose/pallas_call | solution.py:138
  55.4 2.5 %collective-permute-start.11 = (bf16[4,512,128]{2,1,0:T(8,128)(2,1)S(1)}, bf16[4,512,128]{2,1,0:T(8,128)(2,1)S(1)}, u32[]{:S(2)}, u32[]{:S(2)}) collective-permute-start(bf16[4,512,128]{2,1,0:T(8,128)(2,1)S(1)} %get-tuple-element.41), channel_id=1, source_target_pairs={{0,6},{1,7},{2,0},{3,1},{4,2},{5,3},{6,4},{7,5},{8,14},{9,15},{10,... | collective-permute-start | bytes 1572872 | tf_op jit(solution)/shard_map/ppermute | solution.py:484
  57.8 2.6 %collective-permute-start.12 = (bf16[4,512,128]{2,1,0:T(8,128)(2,1)S(1)}, bf16[4,512,128]{2,1,0:T(8,128)(2,1)S(1)}, u32[]{:S(2)}, u32[]{:S(2)}) collective-permute-start(bf16[4,512,128]{2,1,0:T(8,128)(2,1)S(1)} %get-tuple-element.42), channel_id=1, source_target_pairs={{0,24},{1,25},{2,26},{3,27},{4,28},{5,29},{6,30},{7,31},{8,0},{9,1... | collective-permute-start | bytes 1572872 | tf_op jit(solution)/shard_map/ppermute | solution.py:484
  60.4 4.4 %collective-permute-start.13 = (bf16[4,512,128]{2,1,0:T(8,128)(2,1)S(1)}, bf16[4,512,128]{2,1,0:T(8,128)(2,1)S(1)}, u32[]{:S(2)}, u32[]{:S(2)}) collective-permute-start(bf16[4,512,128]{2,1,0:T(8,128)(2,1)S(1)} %get-tuple-element.45), channel_id=1, source_target_pairs={{0,1},{1,0},{2,3},{3,2},{4,5},{5,4},{6,7},{7,6},{8,9},{9,8},{10,11... | collective-permute-start | bytes 1572872 | tf_op jit(solution)/shard_map/ppermute | solution.py:484
  66.4 4.2 %collective-permute-start.14 = (bf16[4,512,128]{2,1,0:T(8,128)(2,1)S(1)}, bf16[4,512,128]{2,1,0:T(8,128)(2,1)S(1)}, u32[]{:S(2)}, u32[]{:S(2)}) collective-permute-start(bf16[4,512,128]{2,1,0:T(8,128)(2,1)S(1)} %get-tuple-element.46), channel_id=1, source_target_pairs={{0,1},{1,0},{2,3},{3,2},{4,5},{5,4},{6,7},{7,6},{8,9},{9,8},{10,11... | collective-permute-start | bytes 1572872 | tf_op jit(solution)/shard_map/ppermute | solution.py:484
  71.3 3.7 %collective-permute-start.21 = (bf16[4,512,128]{2,1,0:T(8,128)(2,1)}, bf16[4,512,128]{2,1,0:T(8,128)(2,1)}, u32[]{:S(2)}, u32[]{:S(2)}) collective-permute-start(bf16[4,512,128]{2,1,0:T(8,128)(2,1)} %after.7), channel_id=1, source_target_pairs={{0,5},{1,4},{2,7},{3,6},{4,1},{5,0},{6,3},{7,2},{8,13},{9,12},{10,... | collective-permute-start | bytes 1572872 | tf_op jit(solution)/shard_map/ppermute | solution.py:484
  75.1 7.6 %exchange.3 = (bf16[8,12,16,128]{3,2,1,0:T(8,128)(2,1)S(1)}, f32[8,22,16,128]{3,2,1,0:T(8,128)S(1)}) custom-call(bf16[136,2,320,512]{3,2,1,0:T(8,128)(2,1)} %get-tuple-element.33.left_ref, bf16[4,512,128]{2,1,0:T(8,128)(2,1)S(1)} %collective-permute-done.9.refs_0_.__1_, bf16[4,512,128]{2,1,0:T(8,128)(2,1)S(1)} %collective-permute-done.10.refs_1_.__1_, ...), custom_call_target="tpu_custom_call" | custom-call | tf_op jit(solution)/shard_map/exchange/pallas_call | solution.py:364
  83.5 6.1 %all-to-all-start = ((bf16[8,12,16,128]{3,2,1,0:T(8,128)(2,1)}), bf16[8,12,16,128]{3,2,1,0:T(8,128)(2,1)S(1)}, u32[]{:S(2)}, u32[]{:S(2)}) async-start(bf16[8,12,16,128]{3,2,1,0:T(8,128)(2,1)} %copy-done.5), calls=%async_computation | async-start | bytes 786432 | tf_op jit(solution)/shard_map/all_to_all | solution.py:546
  89.6 3.0 %collective-permute-start.16 = (bf16[4,512,128]{2,1,0:T(8,128)(2,1)}, bf16[4,512,128]{2,1,0:T(8,128)(2,1)}, u32[]{:S(2)}, u32[]{:S(2)}) collective-permute-start(bf16[4,512,128]{2,1,0:T(8,128)(2,1)} %copy-done.7), channel_id=1, source_target_pairs={{0,9},{1,8},{2,11},{3,10},{4,13},{5,12},{6,15},{7,14},{8,17},{9,16... | collective-permute-start | bytes 1572872 | tf_op jit(solution)/shard_map/ppermute | solution.py:484
  95.8 2.3 %collective-permute-start.17 = (bf16[4,512,128]{2,1,0:T(8,128)(2,1)}, bf16[4,512,128]{2,1,0:T(8,128)(2,1)S(1)}, u32[]{:S(2)}, u32[]{:S(2)}) collective-permute-start(bf16[4,512,128]{2,1,0:T(8,128)(2,1)} %get-tuple-element.50), channel_id=1, source_target_pairs={{0,7},{1,6},{2,1},{3,0},{4,3},{5,2},{6,5},{7,4},{8,15},{9,14},{10,... | collective-permute-start | bytes 1572872 | tf_op jit(solution)/shard_map/ppermute | solution.py:484
  100.3 4.5 %all-to-all-done.__1_.early_ref = bf16[8,12,16,128]{3,2,1,0:T(8,128)(2,1)S(1)} async-done(((bf16[8,12,16,128]{3,2,1,0:T(8,128)(2,1)}), bf16[8,12,16,128]{3,2,1,0:T(8,128)(2,1)S(1)}, u32[]{:S(2)}, u32[]{:S(2)}) %all-to-all-start) | async-done | bytes 393248 | tf_op jit(solution)/shard_map/all_to_all | solution.py:546
  104.8 13.3 %collective-permute-done.22.refs_3_ = bf16[4,512,128]{2,1,0:T(8,128)(2,1)} collective-permute-done((bf16[4,512,128]{2,1,0:T(8,128)(2,1)}, bf16[4,512,128]{2,1,0:T(8,128)(2,1)}, u32[]{:S(2)}, u32[]{:S(2)}) %collective-permute-start.22) | collective-permute-done | bytes 524320 | tf_op jit(solution)/shard_map/ppermute | solution.py:484
  118.1 6.4 %exchange.4.refs_4_ = f32[8,22,16,128]{3,2,1,0:T(8,128)S(1)} custom-call(bf16[136,2,320,512]{3,2,1,0:T(8,128)(2,1)} %get-tuple-element.33.left_ref, bf16[4,512,128]{2,1,0:T(8,128)(2,1)S(1)} %collective-permute-done.19.refs_0_, bf16[4,512,128]{2,1,0:T(8,128)(2,1)S(1)} %collective-permute-done.20.refs_1_, ...), custom_call_target="tpu_custom_call" | custom-call | tf_op jit(solution)/shard_map/exchange/pallas_call | solution.py:364
  124.5 6.9 %exchange.5 = bf16[8,22,16,128]{3,2,1,0:T(8,128)(2,1)} custom-call(bf16[136,2,320,512]{3,2,1,0:T(8,128)(2,1)} %get-tuple-element.33.left_ref, bf16[4,512,128]{2,1,0:T(8,128)(2,1)} %collective-permute-done.15.refs_0_, bf16[4,512,128]{2,1,0:T(8,128)(2,1)} %collective-permute-done.16.refs_1_, bf16[4,512,128]{2,1,0:T(8,128)(2,1)S(1)} %collective-permute-done.17.refs_2_, ...), custom_call_target="tpu_custom_call" | custom-call | tf_op jit(solution)/shard_map/exchange/pallas_call | solution.py:364
  131.5 6.8 %all-to-all-start.1 = ((bf16[8,22,16,128]{3,2,1,0:T(8,128)(2,1)}), bf16[8,22,16,128]{3,2,1,0:T(8,128)(2,1)S(1)}, u32[]{:S(2)}, u32[]{:S(2)}) async-start(bf16[8,22,16,128]{3,2,1,0:T(8,128)(2,1)} %exchange.5), calls=%async_computation.1 | async-start | bytes 1441792 | tf_op jit(solution)/shard_map/all_to_all | solution.py:553
  139.7 20.7 %all-to-all-done.1.late_ref = bf16[8,22,16,128]{3,2,1,0:T(8,128)(2,1)S(1)} async-done(((bf16[8,22,16,128]{3,2,1,0:T(8,128)(2,1)}), bf16[8,22,16,128]{3,2,1,0:T(8,128)(2,1)S(1)}, u32[]{:S(2)}, u32[]{:S(2)}) %all-to-all-start.1) | async-done | bytes 720928 | tf_op jit(solution)/shard_map/all_to_all | solution.py:553
  (67 shorter events, 19.6 us)
Async XLA Ops:
  7.6 26.9 %collective-permute-start.1 = (bf16[8,528,128]{2,1,0:T(8,128)(2,1)S(1)}, bf16[8,528,128]{2,1,0:T(8,128)(2,1)S(1)}, u32[]{:S(2)}, u32[]{:S(2)}) collective-permute-start(bf16[8,528,128]{2,1,0:T(8,128)(2,1)S(1)} %get-tuple-element.31.first_ref.refs_0_), channel_id=1, source_target_pairs={{0,8},{1,9},{2,10},{3,11},{4,12},{5,13},{6,14},{7,15},{8,16},{9,17... | collective-permute-start | bytes 3244040 | tf_op jit(solution)/shard_map/ppermute | solution.py:484
  7.7 26.8 %collective-permute-start.2 = (bf16[8,528,128]{2,1,0:T(8,128)(2,1)S(1)}, bf16[8,528,128]{2,1,0:T(8,128)(2,1)S(1)}, u32[]{:S(2)}, u32[]{:S(2)}) collective-permute-start(bf16[8,528,128]{2,1,0:T(8,128)(2,1)S(1)} %get-tuple-element.31.first_ref.refs_0_), channel_id=1, source_target_pairs={{0,24},{1,25},{2,26},{3,27},{4,28},{5,29},{6,30},{7,31},{8,0},{9,1... | collective-permute-start | bytes 3244040 | tf_op jit(solution)/shard_map/ppermute | solution.py:484
  10.3 25.7 %collective-permute-start.3 = (bf16[8,528,128]{2,1,0:T(8,128)(2,1)S(1)}, bf16[8,528,128]{2,1,0:T(8,128)(2,1)S(1)}, u32[]{:S(2)}, u32[]{:S(2)}) collective-permute-start(bf16[8,528,128]{2,1,0:T(8,128)(2,1)S(1)} %get-tuple-element.32.second_ref.refs_5_), channel_id=1, source_target_pairs={{0,2},{1,3},{2,4},{3,5},{4,6},{5,7},{6,0},{7,1},{8,10},{9,11},{10,... | collective-permute-start | bytes 3244040 | tf_op jit(solution)/shard_map/ppermute | solution.py:484
  10.3 25.7 %collective-permute-start.4 = (bf16[8,528,128]{2,1,0:T(8,128)(2,1)S(1)}, bf16[8,528,128]{2,1,0:T(8,128)(2,1)S(1)}, u32[]{:S(2)}, u32[]{:S(2)}) collective-permute-start(bf16[8,528,128]{2,1,0:T(8,128)(2,1)S(1)} %get-tuple-element.32.second_ref.refs_5_), channel_id=1, source_target_pairs={{0,6},{1,7},{2,0},{3,1},{4,2},{5,3},{6,4},{7,5},{8,14},{9,15},{10,... | collective-permute-start | bytes 3244040 | tf_op jit(solution)/shard_map/ppermute | solution.py:484
  36.2 13.2 %collective-permute-start.5 = (bf16[4,528,128]{2,1,0:T(8,128)(2,1)S(1)}, bf16[4,528,128]{2,1,0:T(8,128)(2,1)S(1)}, u32[]{:S(2)}, u32[]{:S(2)}) collective-permute-start(bf16[4,528,128]{2,1,0:T(8,128)(2,1)S(1)} %get-tuple-element.35), channel_id=1, source_target_pairs={{0,8},{1,9},{2,10},{3,11},{4,12},{5,13},{6,14},{7,15},{8,16},{9,17... | collective-permute-start | bytes 1622024 | tf_op jit(solution)/shard_map/ppermute | solution.py:484
  36.2 13.2 %collective-permute-start.6 = (bf16[4,528,128]{2,1,0:T(8,128)(2,1)S(1)}, bf16[4,528,128]{2,1,0:T(8,128)(2,1)S(1)}, u32[]{:S(2)}, u32[]{:S(2)}) collective-permute-start(bf16[4,528,128]{2,1,0:T(8,128)(2,1)S(1)} %get-tuple-element.36), channel_id=1, source_target_pairs={{0,24},{1,25},{2,26},{3,27},{4,28},{5,29},{6,30},{7,31},{8,0},{9,1... | collective-permute-start | bytes 1622024 | tf_op jit(solution)/shard_map/ppermute | solution.py:484
  38.9 12.6 %collective-permute-start.7 = (bf16[4,528,128]{2,1,0:T(8,128)(2,1)S(1)}, bf16[4,528,128]{2,1,0:T(8,128)(2,1)S(1)}, u32[]{:S(2)}, u32[]{:S(2)}) collective-permute-start(bf16[4,528,128]{2,1,0:T(8,128)(2,1)S(1)} %get-tuple-element.37), channel_id=1, source_target_pairs={{0,2},{1,3},{2,4},{3,5},{4,6},{5,7},{6,0},{7,1},{8,10},{9,11},{10,... | collective-permute-start | bytes 1622024 | tf_op jit(solution)/shard_map/ppermute | solution.py:484
  38.9 12.6 %collective-permute-start.8 = (bf16[4,528,128]{2,1,0:T(8,128)(2,1)S(1)}, bf16[4,528,128]{2,1,0:T(8,128)(2,1)S(1)}, u32[]{:S(2)}, u32[]{:S(2)}) collective-permute-start(bf16[4,528,128]{2,1,0:T(8,128)(2,1)S(1)} %get-tuple-element.38), channel_id=1, source_target_pairs={{0,6},{1,7},{2,0},{3,1},{4,2},{5,3},{6,4},{7,5},{8,14},{9,15},{10,... | collective-permute-start | bytes 1622024 | tf_op jit(solution)/shard_map/ppermute | solution.py:484
  55.0 11.4 %collective-permute-start.9 = (bf16[4,512,128]{2,1,0:T(8,128)(2,1)S(1)}, bf16[4,512,128]{2,1,0:T(8,128)(2,1)S(1)}, u32[]{:S(2)}, u32[]{:S(2)}) collective-permute-start(bf16[4,512,128]{2,1,0:T(8,128)(2,1)S(1)} %get-tuple-element.39), channel_id=1, source_target_pairs={{0,2},{1,3},{2,4},{3,5},{4,6},{5,7},{6,0},{7,1},{8,10},{9,11},{10,... | collective-permute-start | bytes 1572872 | tf_op jit(solution)/shard_map/ppermute | solution.py:484
  55.3 15.3 %collective-permute-start.10 = (bf16[4,512,128]{2,1,0:T(8,128)(2,1)S(1)}, bf16[4,512,128]{2,1,0:T(8,128)(2,1)S(1)}, u32[]{:S(2)}, u32[]{:S(2)}) collective-permute-start(bf16[4,512,128]{2,1,0:T(8,128)(2,1)S(1)} %get-tuple-element.40), channel_id=1, source_target_pairs={{0,8},{1,9},{2,10},{3,11},{4,12},{5,13},{6,14},{7,15},{8,16},{9,17... | collective-permute-start | bytes 1572872 | tf_op jit(solution)/shard_map/ppermute | solution.py:484
  55.4 15.8 %collective-permute-start.11 = (bf16[4,512,128]{2,1,0:T(8,128)(2,1)S(1)}, bf16[4,512,128]{2,1,0:T(8,128)(2,1)S(1)}, u32[]{:S(2)}, u32[]{:S(2)}) collective-permute-start(bf16[4,512,128]{2,1,0:T(8,128)(2,1)S(1)} %get-tuple-element.41), channel_id=1, source_target_pairs={{0,6},{1,7},{2,0},{3,1},{4,2},{5,3},{6,4},{7,5},{8,14},{9,15},{10,... | collective-permute-start | bytes 1572872 | tf_op jit(solution)/shard_map/ppermute | solution.py:484
  57.8 13.5 %collective-permute-start.12 = (bf16[4,512,128]{2,1,0:T(8,128)(2,1)S(1)}, bf16[4,512,128]{2,1,0:T(8,128)(2,1)S(1)}, u32[]{:S(2)}, u32[]{:S(2)}) collective-permute-start(bf16[4,512,128]{2,1,0:T(8,128)(2,1)S(1)} %get-tuple-element.42), channel_id=1, source_target_pairs={{0,24},{1,25},{2,26},{3,27},{4,28},{5,29},{6,30},{7,31},{8,0},{9,1... | collective-permute-start | bytes 1572872 | tf_op jit(solution)/shard_map/ppermute | solution.py:484
  60.4 14.7 %collective-permute-start.13 = (bf16[4,512,128]{2,1,0:T(8,128)(2,1)S(1)}, bf16[4,512,128]{2,1,0:T(8,128)(2,1)S(1)}, u32[]{:S(2)}, u32[]{:S(2)}) collective-permute-start(bf16[4,512,128]{2,1,0:T(8,128)(2,1)S(1)} %get-tuple-element.45), channel_id=1, source_target_pairs={{0,1},{1,0},{2,3},{3,2},{4,5},{5,4},{6,7},{7,6},{8,9},{9,8},{10,11... | collective-permute-start | bytes 1572872 | tf_op jit(solution)/shard_map/ppermute | solution.py:484
  66.4 8.7 %collective-permute-start.14 = (bf16[4,512,128]{2,1,0:T(8,128)(2,1)S(1)}, bf16[4,512,128]{2,1,0:T(8,128)(2,1)S(1)}, u32[]{:S(2)}, u32[]{:S(2)}) collective-permute-start(bf16[4,512,128]{2,1,0:T(8,128)(2,1)S(1)} %get-tuple-element.46), channel_id=1, source_target_pairs={{0,1},{1,0},{2,3},{3,2},{4,5},{5,4},{6,7},{7,6},{8,9},{9,8},{10,11... | collective-permute-start | bytes 1572872 | tf_op jit(solution)/shard_map/ppermute | solution.py:484
  70.6 23.9 %collective-permute-start.19 = (bf16[4,512,128]{2,1,0:T(8,128)(2,1)}, bf16[4,512,128]{2,1,0:T(8,128)(2,1)S(1)}, u32[]{:S(2)}, u32[]{:S(2)}) collective-permute-start(bf16[4,512,128]{2,1,0:T(8,128)(2,1)} %after.5), channel_id=1, source_target_pairs={{0,4},{1,5},{2,6},{3,7},{4,0},{5,1},{6,2},{7,3},{8,12},{9,13},{10,... | collective-permute-start | bytes 1572872 | tf_op jit(solution)/shard_map/ppermute | solution.py:484
  71.2 24.6 %collective-permute-start.20 = (bf16[4,512,128]{2,1,0:T(8,128)(2,1)}, bf16[4,512,128]{2,1,0:T(8,128)(2,1)S(1)}, u32[]{:S(2)}, u32[]{:S(2)}) collective-permute-start(bf16[4,512,128]{2,1,0:T(8,128)(2,1)} %after.6), channel_id=1, source_target_pairs={{0,16},{1,17},{2,18},{3,19},{4,20},{5,21},{6,22},{7,23},{8,24},{9,... | collective-permute-start | bytes 1572872 | tf_op jit(solution)/shard_map/ppermute | solution.py:484
  71.3 27.0 %collective-permute-start.21 = (bf16[4,512,128]{2,1,0:T(8,128)(2,1)}, bf16[4,512,128]{2,1,0:T(8,128)(2,1)}, u32[]{:S(2)}, u32[]{:S(2)}) collective-permute-start(bf16[4,512,128]{2,1,0:T(8,128)(2,1)} %after.7), channel_id=1, source_target_pairs={{0,5},{1,4},{2,7},{3,6},{4,1},{5,0},{6,3},{7,2},{8,13},{9,12},{10,... | collective-permute-start | bytes 1572872 | tf_op jit(solution)/shard_map/ppermute | solution.py:484
  83.5 21.3 %all-to-all-start = ((bf16[8,12,16,128]{3,2,1,0:T(8,128)(2,1)}), bf16[8,12,16,128]{3,2,1,0:T(8,128)(2,1)S(1)}, u32[]{:S(2)}, u32[]{:S(2)}) async-start(bf16[8,12,16,128]{3,2,1,0:T(8,128)(2,1)} %copy-done.5), calls=%async_computation | async-start | bytes 786432 | tf_op jit(solution)/shard_map/all_to_all | solution.py:546
  89.6 34.9 %collective-permute-start.15 = (bf16[4,512,128]{2,1,0:T(8,128)(2,1)}, bf16[4,512,128]{2,1,0:T(8,128)(2,1)}, u32[]{:S(2)}, u32[]{:S(2)}) collective-permute-start(bf16[4,512,128]{2,1,0:T(8,128)(2,1)} %copy-done.8), channel_id=1, source_target_pairs={{0,3},{1,2},{2,5},{3,4},{4,7},{5,6},{6,1},{7,0},{8,11},{9,10},{10,... | collective-permute-start | bytes 1572872 | tf_op jit(solution)/shard_map/ppermute | solution.py:484
  89.6 34.9 %collective-permute-start.16 = (bf16[4,512,128]{2,1,0:T(8,128)(2,1)}, bf16[4,512,128]{2,1,0:T(8,128)(2,1)}, u32[]{:S(2)}, u32[]{:S(2)}) collective-permute-start(bf16[4,512,128]{2,1,0:T(8,128)(2,1)} %copy-done.7), channel_id=1, source_target_pairs={{0,9},{1,8},{2,11},{3,10},{4,13},{5,12},{6,15},{7,14},{8,17},{9,16... | collective-permute-start | bytes 1572872 | tf_op jit(solution)/shard_map/ppermute | solution.py:484
  94.5 23.6 %collective-permute-start.22 = (bf16[4,512,128]{2,1,0:T(8,128)(2,1)}, bf16[4,512,128]{2,1,0:T(8,128)(2,1)}, u32[]{:S(2)}, u32[]{:S(2)}) collective-permute-start(bf16[4,512,128]{2,1,0:T(8,128)(2,1)} %copy-done.4), channel_id=1, source_target_pairs={{0,17},{1,16},{2,19},{3,18},{4,21},{5,20},{6,23},{7,22},{8,25},{9,... | collective-permute-start | bytes 1572872 | tf_op jit(solution)/shard_map/ppermute | solution.py:484
  95.8 28.7 %collective-permute-start.17 = (bf16[4,512,128]{2,1,0:T(8,128)(2,1)}, bf16[4,512,128]{2,1,0:T(8,128)(2,1)S(1)}, u32[]{:S(2)}, u32[]{:S(2)}) collective-permute-start(bf16[4,512,128]{2,1,0:T(8,128)(2,1)} %get-tuple-element.50), channel_id=1, source_target_pairs={{0,7},{1,6},{2,1},{3,0},{4,3},{5,2},{6,5},{7,4},{8,15},{9,14},{10,... | collective-permute-start | bytes 1572872 | tf_op jit(solution)/shard_map/ppermute | solution.py:484
  98.3 26.2 %collective-permute-start.18 = (bf16[4,512,128]{2,1,0:T(8,128)(2,1)}, bf16[4,512,128]{2,1,0:T(8,128)(2,1)}, u32[]{:S(2)}, u32[]{:S(2)}) collective-permute-start(bf16[4,512,128]{2,1,0:T(8,128)(2,1)} %get-tuple-element.51), channel_id=1, source_target_pairs={{0,25},{1,24},{2,27},{3,26},{4,29},{5,28},{6,31},{7,30},{8,1},{9,0... | collective-permute-start | bytes 1572872 | tf_op jit(solution)/shard_map/ppermute | solution.py:484
  131.5 28.9 %all-to-all-start.1 = ((bf16[8,22,16,128]{3,2,1,0:T(8,128)(2,1)}), bf16[8,22,16,128]{3,2,1,0:T(8,128)(2,1)S(1)}, u32[]{:S(2)}, u32[]{:S(2)}) async-start(bf16[8,22,16,128]{3,2,1,0:T(8,128)(2,1)} %exchange.5), calls=%async_computation.1 | async-start | bytes 1441792 | tf_op jit(solution)/shard_map/all_to_all | solution.py:553
  (11 other events, 73.0 us)

commit v4 on v3

--- a/solution.py
+++ b/solution.py
@@ -522,33 +522,32 @@
     def touched(*works):
         return {entry for work in works for entry, _ in parts_of(work)}
 
+    far = work_of((2, 0), (2, 1))
     works = (
         work_of((1, 0), (-1, 0), (0, 0), (0, 1)),
-        work_of((2, 0), (2, 1)),
-        work_of((1, 1), (-1, 1)),
+        far[:3],
+        far[3:] + work_of((1, 1), (-1, 1)),
     )
     chosen = dict(zip(sum(works, ()), choose(sum(works, ()), gathered)))
     arrived = {}
 
-    def send(work, behind):
+    def send(work):
         for along, shift, core in work:
             one = chosen[along, shift, core]
-            if (shift, core) in behind:
-                one = after(one, arrived[(along, *behind[shift, core])])
             if (shift, core) != (0, 0):
                 one = step_along(1 - along, one, shift, core)
             arrived[along, shift, core] = one
         return [arrived[one] for one in work]
 
     wide, narrow = jnp.float32, jnp.bfloat16
-    blocks = send(works[0], {})
+    blocks = send(works[0])
     early, late = exchange(works[0], (), (EARLY, LATE), (narrow, wide), left, blocks, [own])
     early = lax.all_to_all(early, "aux", split_axis=0, concat_axis=0, tiled=True)
-    blocks = send(works[1], {(2, 0): (1, 0), (2, 1): (-1, 0)})
+    blocks = send(works[1])
     (late,) = exchange(
         works[1], touched(works[0]), (LATE,), (wide,), left, blocks, [after(late, early)]
     )
-    blocks = send(works[2], {})
+    blocks = send(works[2])
     (late,) = exchange(works[2], touched(*works[:2]), (LATE,), (narrow,), left, blocks, [late])
     late = lax.all_to_all(late, "aux", split_axis=0, concat_axis=0, tiled=True)
     return finish(early, late, denom)

time: 162 us -> 156 us (0.963)
  waiting for transfers between devices: 52.7 us -> 50.1 us
  local copies, waits for them, and re-layouts: 7.45 us -> 5.62 us
    ppermute x23, waiting for transfers between devices: 27.5 us -> 23.7 us  [moved(): lax.ppermute(array, 'pair', [(at(x, y, c), at(x + dx, y + dy, c + core))...]
    unnamed x21, local copies, waits for them, and re-layouts: 6.56 us -> 4.72 us
  transfers between devices with their start and end apart: 25 -> 25, of which waited for: 9 -> 10; matrix products, arithmetic and copies ran while one was open for 0% -> 0% of each run, Pallas kernels for 21% -> 21%
where the time goes in v4:
time: 156 us; the launch traced here: 155 us
  starting transfers between devices  53.6 us (34%)
  waiting for transfers between devices  50.1 us (32%)
  Pallas kernels  45.7 us (29%)
  local copies, waits for them, and re-layouts  5.62 us (4%)
    ppermute x23, starting transfers between devices, moved(): lax.ppermute(array, 'pair', [(at(x, y, c), at(x + dx, y + dy, c + core))...  40.5 us
    ppermute x23, waiting for transfers between devices, moved(): lax.ppermute(array, 'pair', [(at(x, y, c), at(x + dx, y + dy, c + core))...  23.7 us
    all_to_all x1, waiting for transfers between devices, on_device(): late = lax.all_to_all(late, 'aux', split_axis=0, concat_axis=0, tiled=True)  20.7 us
    pallas_call x3, Pallas kernels, exchange(): pl.pallas_call(functools.partial(exchange_kernel, work, before, sets, own...  19.8 us
    pallas_call x1, Pallas kernels, left_of(): pl.pallas_call(left_kernel, in_specs=[SMEM] * 2 + [VMEM] * 3, out_specs=[...  19.2 us
    all_to_all x1, starting transfers between devices, on_device(): late = lax.all_to_all(late, 'aux', split_axis=0, concat_axis=0, tiled=True)  7.07 us
    all_to_all x1, starting transfers between devices, on_device(): lax.all_to_all(early, 'aux', split_axis=0, concat_axis=0, tiled=True)  5.93 us
    all_to_all x1, waiting for transfers between devices, on_device(): lax.all_to_all(early, 'aux', split_axis=0, concat_axis=0, tiled=True)  5.7 us
  transfers between devices with their start and end apart: 25, of which 10 were waited for; matrix products, arithmetic and copies ran while one was open for 0% of the time, Pallas kernels for 21%

profile of v4, /device:TPU:1, one launch (start us, length us, event | category | flops | bytes accessed | tf_op | source)
XLA Modules:
  0.0 155.2 jit_solution(14937541761972312044)
XLA Ops:
  0.9 3.3 %collective-permute-start = (bf16[16,128]{1,0:T(8,128)(2,1)S(1)}, bf16[16,128]{1,0:T(8,128)(2,1)S(1)}, u32[]{:S(2)}, u32[]{:S(2)}) collective-permute-start(bf16[16,128]{1,0:T(8,128)(2,1)S(1)} %broadcast_in_dim.2.wanted_ref), channel_id=1, source_target_pairs={{0,1},{1,0},{2,3},{3,2},{4,5},{5,4},{6,7},{7,6},{8,9},{9,8},{10,11... | collective-permute-start | bytes 12296 | tf_op jit(solution)/shard_map/ppermute | solution.py:484
  7.7 2.7 %collective-permute-start.2 = (bf16[8,528,128]{2,1,0:T(8,128)(2,1)S(1)}, bf16[8,528,128]{2,1,0:T(8,128)(2,1)S(1)}, u32[]{:S(2)}, u32[]{:S(2)}) collective-permute-start(bf16[8,528,128]{2,1,0:T(8,128)(2,1)S(1)} %get-tuple-element.31.first_ref.refs_0_), channel_id=1, source_target_pairs={{0,24},{1,25},{2,26},{3,27},{4,28},{5,29},{6,30},{7,31},{8,0},{9,1... | collective-permute-start | bytes 3244040 | tf_op jit(solution)/shard_map/ppermute | solution.py:484
  10.3 2.7 %collective-permute-start.4 = (bf16[8,528,128]{2,1,0:T(8,128)(2,1)S(1)}, bf16[8,528,128]{2,1,0:T(8,128)(2,1)S(1)}, u32[]{:S(2)}, u32[]{:S(2)}) collective-permute-start(bf16[8,528,128]{2,1,0:T(8,128)(2,1)S(1)} %get-tuple-element.32.second_ref.refs_5_), channel_id=1, source_target_pairs={{0,6},{1,7},{2,0},{3,1},{4,2},{5,3},{6,4},{7,5},{8,14},{9,15},{10,... | collective-permute-start | bytes 3244040 | tf_op jit(solution)/shard_map/ppermute | solution.py:484
  13.0 2.3 %copy-done = bf16[136,128,128]{2,1,0:T(8,128)(2,1)S(1)} copy-done((bf16[136,128,128]{2,1,0:T(8,128)(2,1)S(1)}, bf16[136,128,128]{2,1,0:T(8,128)(2,1)}, u32[]{:S(2)}) %copy-start) | copy-done | bytes 4456472
  15.3 19.2 %left.1 = (bf16[136,2,320,512]{3,2,1,0:T(8,128)(2,1)}, bf16[8,2,16,128]{3,2,1,0:T(8,128)(2,1)S(1)}) custom-call(s32[136]{0:T(256)S(1)} %and_select_fusion.1.left_index, s32[136]{0:T(256)S(1)} %get-tuple-element.58.right_index, bf16[8,528,128]{2,1,0:T(8,128)(2,1)S(1)} %get-tuple-element.31.first_ref.refs_0_, ...), custom_call_target="tpu_custom_call" | custom-call | tf_op jit(solution)/shard_map/left/pallas_call | solution.py:251
  36.2 2.7 %collective-permute-start.6 = (bf16[4,528,128]{2,1,0:T(8,128)(2,1)S(1)}, bf16[4,528,128]{2,1,0:T(8,128)(2,1)S(1)}, u32[]{:S(2)}, u32[]{:S(2)}) collective-permute-start(bf16[4,528,128]{2,1,0:T(8,128)(2,1)S(1)} %get-tuple-element.36), channel_id=1, source_target_pairs={{0,24},{1,25},{2,26},{3,27},{4,28},{5,29},{6,30},{7,31},{8,0},{9,1... | collective-permute-start | bytes 1622024 | tf_op jit(solution)/shard_map/ppermute | solution.py:484
  38.9 2.7 %collective-permute-start.8 = (bf16[4,528,128]{2,1,0:T(8,128)(2,1)S(1)}, bf16[4,528,128]{2,1,0:T(8,128)(2,1)S(1)}, u32[]{:S(2)}, u32[]{:S(2)}) collective-permute-start(bf16[4,528,128]{2,1,0:T(8,128)(2,1)S(1)} %get-tuple-element.38), channel_id=1, source_target_pairs={{0,6},{1,7},{2,0},{3,1},{4,2},{5,3},{6,4},{7,5},{8,14},{9,15},{10,... | collective-permute-start | bytes 1622024 | tf_op jit(solution)/shard_map/ppermute | solution.py:484
  41.6 7.8 %collective-permute-done.5.refs_3_ = bf16[4,528,128]{2,1,0:T(8,128)(2,1)S(1)} collective-permute-done((bf16[4,528,128]{2,1,0:T(8,128)(2,1)S(1)}, bf16[4,528,128]{2,1,0:T(8,128)(2,1)S(1)}, u32[]{:S(2)}, u32[]{:S(2)}) %collective-permute-start.5) | collective-permute-done | bytes 540704 | tf_op jit(solution)/shard_map/ppermute | solution.py:484
  51.5 3.0 %choose.1 = (bf16[4,512,128]{2,1,0:T(8,128)(2,1)S(1)}, bf16[4,512,128]{2,1,0:T(8,128)(2,1)S(1)}, bf16[4,512,128]{2,1,0:T(8,128)(2,1)S(1)}, bf16[4,512,128]{2,1,0...) custom-call(bf16[8,528,128]{2,1,0:T(8,128)(2,1)S(1)} %get-tuple-elem, ...), custom_call_target="tpu_custom_call" | custom-call | tf_op jit(solution)/shard_map/choose/pallas_call | solution.py:138
  55.0 2.5 %collective-permute-start.11 = (bf16[4,512,128]{2,1,0:T(8,128)(2,1)S(1)}, bf16[4,512,128]{2,1,0:T(8,128)(2,1)S(1)}, u32[]{:S(2)}, u32[]{:S(2)}) collective-permute-start(bf16[4,512,128]{2,1,0:T(8,128)(2,1)S(1)} %get-tuple-element.41), channel_id=1, source_target_pairs={{0,6},{1,7},{2,0},{3,1},{4,2},{5,3},{6,4},{7,5},{8,14},{9,15},{10,... | collective-permute-start | bytes 1572872 | tf_op jit(solution)/shard_map/ppermute | solution.py:484
  57.4 2.6 %collective-permute-start.12 = (bf16[4,512,128]{2,1,0:T(8,128)(2,1)S(1)}, bf16[4,512,128]{2,1,0:T(8,128)(2,1)S(1)}, u32[]{:S(2)}, u32[]{:S(2)}) collective-permute-start(bf16[4,512,128]{2,1,0:T(8,128)(2,1)S(1)} %get-tuple-element.42), channel_id=1, source_target_pairs={{0,24},{1,25},{2,26},{3,27},{4,28},{5,29},{6,30},{7,31},{8,0},{9,1... | collective-permute-start | bytes 1572872 | tf_op jit(solution)/shard_map/ppermute | solution.py:484
  60.0 4.4 %collective-permute-start.13 = (bf16[4,512,128]{2,1,0:T(8,128)(2,1)S(1)}, bf16[4,512,128]{2,1,0:T(8,128)(2,1)S(1)}, u32[]{:S(2)}, u32[]{:S(2)}) collective-permute-start(bf16[4,512,128]{2,1,0:T(8,128)(2,1)S(1)} %get-tuple-element.45), channel_id=1, source_target_pairs={{0,1},{1,0},{2,3},{3,2},{4,5},{5,4},{6,7},{7,6},{8,9},{9,8},{10,11... | collective-permute-start | bytes 1572872 | tf_op jit(solution)/shard_map/ppermute | solution.py:484
  66.0 4.2 %collective-permute-start.14 = (bf16[4,512,128]{2,1,0:T(8,128)(2,1)S(1)}, bf16[4,512,128]{2,1,0:T(8,128)(2,1)S(1)}, u32[]{:S(2)}, u32[]{:S(2)}) collective-permute-start(bf16[4,512,128]{2,1,0:T(8,128)(2,1)S(1)} %get-tuple-element.46), channel_id=1, source_target_pairs={{0,1},{1,0},{2,3},{3,2},{4,5},{5,4},{6,7},{7,6},{8,9},{9,8},{10,11... | collective-permute-start | bytes 1572872 | tf_op jit(solution)/shard_map/ppermute | solution.py:484
  70.8 3.9 %collective-permute-start.22 = (bf16[4,512,128]{2,1,0:T(8,128)(2,1)}, bf16[4,512,128]{2,1,0:T(8,128)(2,1)S(1)}, u32[]{:S(2)}, u32[]{:S(2)}) collective-permute-start(bf16[4,512,128]{2,1,0:T(8,128)(2,1)} %get-tuple-element.55), channel_id=1, source_target_pairs={{0,5},{1,4},{2,7},{3,6},{4,1},{5,0},{6,3},{7,2},{8,13},{9,12},{10,... | collective-permute-start | bytes 1572872 | tf_op jit(solution)/shard_map/ppermute | solution.py:484
  74.7 7.7 %exchange.3 = (bf16[8,12,16,128]{3,2,1,0:T(8,128)(2,1)S(1)}, f32[8,22,16,128]{3,2,1,0:T(8,128)S(1)}) custom-call(bf16[136,2,320,512]{3,2,1,0:T(8,128)(2,1)} %get-tuple-element.33.left_ref, bf16[4,512,128]{2,1,0:T(8,128)(2,1)S(1)} %collective-permute-done.9.refs_0_, bf16[4,512,128]{2,1,0:T(8,128)(2,1)S(1)} %collective-permute-done.10.refs_1_, ...), custom_call_target="tpu_custom_call" | custom-call | tf_op jit(solution)/shard_map/exchange/pallas_call | solution.py:364
  83.2 5.9 %all-to-all-start = ((bf16[8,12,16,128]{3,2,1,0:T(8,128)(2,1)}), bf16[8,12,16,128]{3,2,1,0:T(8,128)(2,1)S(1)}, u32[]{:S(2)}, u32[]{:S(2)}) async-start(bf16[8,12,16,128]{3,2,1,0:T(8,128)(2,1)} %copy-done.2), calls=%async_computation | async-start | bytes 786432 | tf_op jit(solution)/shard_map/all_to_all | solution.py:545
  89.1 3.5 %collective-permute-start.15 = (bf16[4,512,128]{2,1,0:T(8,128)(2,1)}, bf16[4,512,128]{2,1,0:T(8,128)(2,1)}, u32[]{:S(2)}, u32[]{:S(2)}) collective-permute-start(bf16[4,512,128]{2,1,0:T(8,128)(2,1)} %copy-done.8), channel_id=1, source_target_pairs={{0,17},{1,16},{2,19},{3,18},{4,21},{5,20},{6,23},{7,22},{8,25},{9,... | collective-permute-start | bytes 1572872 | tf_op jit(solution)/shard_map/ppermute | solution.py:484
  93.5 2.2 %collective-permute-start.18 = (bf16[4,512,128]{2,1,0:T(8,128)(2,1)}, bf16[4,512,128]{2,1,0:T(8,128)(2,1)}, u32[]{:S(2)}, u32[]{:S(2)}) collective-permute-start(bf16[4,512,128]{2,1,0:T(8,128)(2,1)} %copy-done.5), channel_id=1, source_target_pairs={{0,7},{1,6},{2,1},{3,0},{4,3},{5,2},{6,5},{7,4},{8,15},{9,14},{10,... | collective-permute-start | bytes 1572872 | tf_op jit(solution)/shard_map/ppermute | solution.py:484
  98.6 5.7 %all-to-all-done.__1_.early_ref = bf16[8,12,16,128]{3,2,1,0:T(8,128)(2,1)S(1)} async-done(((bf16[8,12,16,128]{3,2,1,0:T(8,128)(2,1)}), bf16[8,12,16,128]{3,2,1,0:T(8,128)(2,1)S(1)}, u32[]{:S(2)}, u32[]{:S(2)}) %all-to-all-start) | async-done | bytes 393248 | tf_op jit(solution)/shard_map/all_to_all | solution.py:545
  104.3 3.9 %exchange.4.refs_5_ = f32[8,22,16,128]{3,2,1,0:T(8,128)S(1)} custom-call(bf16[136,2,320,512]{3,2,1,0:T(8,128)(2,1)} %get-tuple-element.33.left_ref, bf16[4,512,128]{2,1,0:T(8,128)(2,1)S(1)} %collective-permute-done.20.refs_0_, bf16[4,512,128]{2,1,0:T(8,128)(2,1)S(1)} %collective-permute-done.21.refs_1_, ...), custom_call_target="tpu_custom_call" | custom-call | tf_op jit(solution)/shard_map/exchange/pallas_call | solution.py:364
  108.5 7.9 %collective-permute-done.17.refs_2_ = bf16[4,512,128]{2,1,0:T(8,128)(2,1)} collective-permute-done((bf16[4,512,128]{2,1,0:T(8,128)(2,1)}, bf16[4,512,128]{2,1,0:T(8,128)(2,1)}, u32[]{:S(2)}, u32[]{:S(2)}) %collective-permute-start.17) | collective-permute-done | bytes 524320 | tf_op jit(solution)/shard_map/ppermute | solution.py:484
  116.4 8.3 %exchange.5 = bf16[8,22,16,128]{3,2,1,0:T(8,128)(2,1)} custom-call(bf16[136,2,320,512]{3,2,1,0:T(8,128)(2,1)} %get-tuple-element.33.left_ref, bf16[4,512,128]{2,1,0:T(8,128)(2,1)} %collective-permute-done.15.refs_0_, bf16[4,512,128]{2,1,0:T(8,128)(2,1)} %collective-permute-done.16.refs_1_, bf16[4,512,128]{2,1,0:T(8,128)(2,1)} %collective-permute-done.17.refs_2_, ...), custom_call_target="tpu_custom_call" | custom-call | tf_op jit(solution)/shard_map/exchange/pallas_call | solution.py:364
  124.7 7.1 %all-to-all-start.1 = ((bf16[8,22,16,128]{3,2,1,0:T(8,128)(2,1)}), bf16[8,22,16,128]{3,2,1,0:T(8,128)(2,1)S(1)}, u32[]{:S(2)}, u32[]{:S(2)}) async-start(bf16[8,22,16,128]{3,2,1,0:T(8,128)(2,1)} %exchange.5), calls=%async_computation.1 | async-start | bytes 1441792 | tf_op jit(solution)/shard_map/all_to_all | solution.py:552
  133.3 20.7 %all-to-all-done.1.late_ref = bf16[8,22,16,128]{3,2,1,0:T(8,128)(2,1)S(1)} async-done(((bf16[8,22,16,128]{3,2,1,0:T(8,128)(2,1)}), bf16[8,22,16,128]{3,2,1,0:T(8,128)(2,1)S(1)}, u32[]{:S(2)}, u32[]{:S(2)}) %all-to-all-start.1) | async-done | bytes 720928 | tf_op jit(solution)/shard_map/all_to_all | solution.py:552
  (63 shorter events, 18.2 us)
Async XLA Ops:
  7.6 26.9 %collective-permute-start.1 = (bf16[8,528,128]{2,1,0:T(8,128)(2,1)S(1)}, bf16[8,528,128]{2,1,0:T(8,128)(2,1)S(1)}, u32[]{:S(2)}, u32[]{:S(2)}) collective-permute-start(bf16[8,528,128]{2,1,0:T(8,128)(2,1)S(1)} %get-tuple-element.31.first_ref.refs_0_), channel_id=1, source_target_pairs={{0,8},{1,9},{2,10},{3,11},{4,12},{5,13},{6,14},{7,15},{8,16},{9,17... | collective-permute-start | bytes 3244040 | tf_op jit(solution)/shard_map/ppermute | solution.py:484
  7.7 26.8 %collective-permute-start.2 = (bf16[8,528,128]{2,1,0:T(8,128)(2,1)S(1)}, bf16[8,528,128]{2,1,0:T(8,128)(2,1)S(1)}, u32[]{:S(2)}, u32[]{:S(2)}) collective-permute-start(bf16[8,528,128]{2,1,0:T(8,128)(2,1)S(1)} %get-tuple-element.31.first_ref.refs_0_), channel_id=1, source_target_pairs={{0,24},{1,25},{2,26},{3,27},{4,28},{5,29},{6,30},{7,31},{8,0},{9,1... | collective-permute-start | bytes 3244040 | tf_op jit(solution)/shard_map/ppermute | solution.py:484
  10.3 25.7 %collective-permute-start.3 = (bf16[8,528,128]{2,1,0:T(8,128)(2,1)S(1)}, bf16[8,528,128]{2,1,0:T(8,128)(2,1)S(1)}, u32[]{:S(2)}, u32[]{:S(2)}) collective-permute-start(bf16[8,528,128]{2,1,0:T(8,128)(2,1)S(1)} %get-tuple-element.32.second_ref.refs_5_), channel_id=1, source_target_pairs={{0,2},{1,3},{2,4},{3,5},{4,6},{5,7},{6,0},{7,1},{8,10},{9,11},{10,... | collective-permute-start | bytes 3244040 | tf_op jit(solution)/shard_map/ppermute | solution.py:484
  10.3 25.7 %collective-permute-start.4 = (bf16[8,528,128]{2,1,0:T(8,128)(2,1)S(1)}, bf16[8,528,128]{2,1,0:T(8,128)(2,1)S(1)}, u32[]{:S(2)}, u32[]{:S(2)}) collective-permute-start(bf16[8,528,128]{2,1,0:T(8,128)(2,1)S(1)} %get-tuple-element.32.second_ref.refs_5_), channel_id=1, source_target_pairs={{0,6},{1,7},{2,0},{3,1},{4,2},{5,3},{6,4},{7,5},{8,14},{9,15},{10,... | collective-permute-start | bytes 3244040 | tf_op jit(solution)/shard_map/ppermute | solution.py:484
  36.2 13.2 %collective-permute-start.5 = (bf16[4,528,128]{2,1,0:T(8,128)(2,1)S(1)}, bf16[4,528,128]{2,1,0:T(8,128)(2,1)S(1)}, u32[]{:S(2)}, u32[]{:S(2)}) collective-permute-start(bf16[4,528,128]{2,1,0:T(8,128)(2,1)S(1)} %get-tuple-element.35), channel_id=1, source_target_pairs={{0,8},{1,9},{2,10},{3,11},{4,12},{5,13},{6,14},{7,15},{8,16},{9,17... | collective-permute-start | bytes 1622024 | tf_op jit(solution)/shard_map/ppermute | solution.py:484
  36.2 13.2 %collective-permute-start.6 = (bf16[4,528,128]{2,1,0:T(8,128)(2,1)S(1)}, bf16[4,528,128]{2,1,0:T(8,128)(2,1)S(1)}, u32[]{:S(2)}, u32[]{:S(2)}) collective-permute-start(bf16[4,528,128]{2,1,0:T(8,128)(2,1)S(1)} %get-tuple-element.36), channel_id=1, source_target_pairs={{0,24},{1,25},{2,26},{3,27},{4,28},{5,29},{6,30},{7,31},{8,0},{9,1... | collective-permute-start | bytes 1622024 | tf_op jit(solution)/shard_map/ppermute | solution.py:484
  38.9 12.6 %collective-permute-start.7 = (bf16[4,528,128]{2,1,0:T(8,128)(2,1)S(1)}, bf16[4,528,128]{2,1,0:T(8,128)(2,1)S(1)}, u32[]{:S(2)}, u32[]{:S(2)}) collective-permute-start(bf16[4,528,128]{2,1,0:T(8,128)(2,1)S(1)} %get-tuple-element.37), channel_id=1, source_target_pairs={{0,2},{1,3},{2,4},{3,5},{4,6},{5,7},{6,0},{7,1},{8,10},{9,11},{10,... | collective-permute-start | bytes 1622024 | tf_op jit(solution)/shard_map/ppermute | solution.py:484
  38.9 12.6 %collective-permute-start.8 = (bf16[4,528,128]{2,1,0:T(8,128)(2,1)S(1)}, bf16[4,528,128]{2,1,0:T(8,128)(2,1)S(1)}, u32[]{:S(2)}, u32[]{:S(2)}) collective-permute-start(bf16[4,528,128]{2,1,0:T(8,128)(2,1)S(1)} %get-tuple-element.38), channel_id=1, source_target_pairs={{0,6},{1,7},{2,0},{3,1},{4,2},{5,3},{6,4},{7,5},{8,14},{9,15},{10,... | collective-permute-start | bytes 1622024 | tf_op jit(solution)/shard_map/ppermute | solution.py:484
  54.6 11.4 %collective-permute-start.9 = (bf16[4,512,128]{2,1,0:T(8,128)(2,1)S(1)}, bf16[4,512,128]{2,1,0:T(8,128)(2,1)S(1)}, u32[]{:S(2)}, u32[]{:S(2)}) collective-permute-start(bf16[4,512,128]{2,1,0:T(8,128)(2,1)S(1)} %get-tuple-element.39), channel_id=1, source_target_pairs={{0,2},{1,3},{2,4},{3,5},{4,6},{5,7},{6,0},{7,1},{8,10},{9,11},{10,... | collective-permute-start | bytes 1572872 | tf_op jit(solution)/shard_map/ppermute | solution.py:484
  55.0 15.3 %collective-permute-start.10 = (bf16[4,512,128]{2,1,0:T(8,128)(2,1)S(1)}, bf16[4,512,128]{2,1,0:T(8,128)(2,1)S(1)}, u32[]{:S(2)}, u32[]{:S(2)}) collective-permute-start(bf16[4,512,128]{2,1,0:T(8,128)(2,1)S(1)} %get-tuple-element.40), channel_id=1, source_target_pairs={{0,8},{1,9},{2,10},{3,11},{4,12},{5,13},{6,14},{7,15},{8,16},{9,17... | collective-permute-start | bytes 1572872 | tf_op jit(solution)/shard_map/ppermute | solution.py:484
  55.0 15.8 %collective-permute-start.11 = (bf16[4,512,128]{2,1,0:T(8,128)(2,1)S(1)}, bf16[4,512,128]{2,1,0:T(8,128)(2,1)S(1)}, u32[]{:S(2)}, u32[]{:S(2)}) collective-permute-start(bf16[4,512,128]{2,1,0:T(8,128)(2,1)S(1)} %get-tuple-element.41), channel_id=1, source_target_pairs={{0,6},{1,7},{2,0},{3,1},{4,2},{5,3},{6,4},{7,5},{8,14},{9,15},{10,... | collective-permute-start | bytes 1572872 | tf_op jit(solution)/shard_map/ppermute | solution.py:484
  57.4 13.4 %collective-permute-start.12 = (bf16[4,512,128]{2,1,0:T(8,128)(2,1)S(1)}, bf16[4,512,128]{2,1,0:T(8,128)(2,1)S(1)}, u32[]{:S(2)}, u32[]{:S(2)}) collective-permute-start(bf16[4,512,128]{2,1,0:T(8,128)(2,1)S(1)} %get-tuple-element.42), channel_id=1, source_target_pairs={{0,24},{1,25},{2,26},{3,27},{4,28},{5,29},{6,30},{7,31},{8,0},{9,1... | collective-permute-start | bytes 1572872 | tf_op jit(solution)/shard_map/ppermute | solution.py:484
  60.0 14.7 %collective-permute-start.13 = (bf16[4,512,128]{2,1,0:T(8,128)(2,1)S(1)}, bf16[4,512,128]{2,1,0:T(8,128)(2,1)S(1)}, u32[]{:S(2)}, u32[]{:S(2)}) collective-permute-start(bf16[4,512,128]{2,1,0:T(8,128)(2,1)S(1)} %get-tuple-element.45), channel_id=1, source_target_pairs={{0,1},{1,0},{2,3},{3,2},{4,5},{5,4},{6,7},{7,6},{8,9},{9,8},{10,11... | collective-permute-start | bytes 1572872 | tf_op jit(solution)/shard_map/ppermute | solution.py:484
  66.0 8.7 %collective-permute-start.14 = (bf16[4,512,128]{2,1,0:T(8,128)(2,1)S(1)}, bf16[4,512,128]{2,1,0:T(8,128)(2,1)S(1)}, u32[]{:S(2)}, u32[]{:S(2)}) collective-permute-start(bf16[4,512,128]{2,1,0:T(8,128)(2,1)S(1)} %get-tuple-element.46), channel_id=1, source_target_pairs={{0,1},{1,0},{2,3},{3,2},{4,5},{5,4},{6,7},{7,6},{8,9},{9,8},{10,11... | collective-permute-start | bytes 1572872 | tf_op jit(solution)/shard_map/ppermute | solution.py:484
  70.2 23.2 %collective-permute-start.20 = (bf16[4,512,128]{2,1,0:T(8,128)(2,1)}, bf16[4,512,128]{2,1,0:T(8,128)(2,1)S(1)}, u32[]{:S(2)}, u32[]{:S(2)}) collective-permute-start(bf16[4,512,128]{2,1,0:T(8,128)(2,1)} %get-tuple-element.53), channel_id=1, source_target_pairs={{0,4},{1,5},{2,6},{3,7},{4,0},{5,1},{6,2},{7,3},{8,12},{9,13},{10,... | collective-permute-start | bytes 1572872 | tf_op jit(solution)/shard_map/ppermute | solution.py:484
  70.8 22.7 %collective-permute-start.21 = (bf16[4,512,128]{2,1,0:T(8,128)(2,1)}, bf16[4,512,128]{2,1,0:T(8,128)(2,1)S(1)}, u32[]{:S(2)}, u32[]{:S(2)}) collective-permute-start(bf16[4,512,128]{2,1,0:T(8,128)(2,1)} %get-tuple-element.54), channel_id=1, source_target_pairs={{0,16},{1,17},{2,18},{3,19},{4,20},{5,21},{6,22},{7,23},{8,24},{9,... | collective-permute-start | bytes 1572872 | tf_op jit(solution)/shard_map/ppermute | solution.py:484
  70.8 26.4 %collective-permute-start.22 = (bf16[4,512,128]{2,1,0:T(8,128)(2,1)}, bf16[4,512,128]{2,1,0:T(8,128)(2,1)S(1)}, u32[]{:S(2)}, u32[]{:S(2)}) collective-permute-start(bf16[4,512,128]{2,1,0:T(8,128)(2,1)} %get-tuple-element.55), channel_id=1, source_target_pairs={{0,5},{1,4},{2,7},{3,6},{4,1},{5,0},{6,3},{7,2},{8,13},{9,12},{10,... | collective-permute-start | bytes 1572872 | tf_op jit(solution)/shard_map/ppermute | solution.py:484
  83.2 21.1 %all-to-all-start = ((bf16[8,12,16,128]{3,2,1,0:T(8,128)(2,1)}), bf16[8,12,16,128]{3,2,1,0:T(8,128)(2,1)S(1)}, u32[]{:S(2)}, u32[]{:S(2)}) async-start(bf16[8,12,16,128]{3,2,1,0:T(8,128)(2,1)} %copy-done.2), calls=%async_computation | async-start | bytes 786432 | tf_op jit(solution)/shard_map/all_to_all | solution.py:545
  89.1 19.1 %collective-permute-start.15 = (bf16[4,512,128]{2,1,0:T(8,128)(2,1)}, bf16[4,512,128]{2,1,0:T(8,128)(2,1)}, u32[]{:S(2)}, u32[]{:S(2)}) collective-permute-start(bf16[4,512,128]{2,1,0:T(8,128)(2,1)} %copy-done.8), channel_id=1, source_target_pairs={{0,17},{1,16},{2,19},{3,18},{4,21},{5,20},{6,23},{7,22},{8,25},{9,... | collective-permute-start | bytes 1572872 | tf_op jit(solution)/shard_map/ppermute | solution.py:484
  92.6 15.8 %collective-permute-start.16 = (bf16[4,512,128]{2,1,0:T(8,128)(2,1)}, bf16[4,512,128]{2,1,0:T(8,128)(2,1)}, u32[]{:S(2)}, u32[]{:S(2)}) collective-permute-start(bf16[4,512,128]{2,1,0:T(8,128)(2,1)} %copy-done.7), channel_id=1, source_target_pairs={{0,3},{1,2},{2,5},{3,4},{4,7},{5,6},{6,1},{7,0},{8,11},{9,10},{10,... | collective-permute-start | bytes 1572872 | tf_op jit(solution)/shard_map/ppermute | solution.py:484
  93.5 22.9 %collective-permute-start.17 = (bf16[4,512,128]{2,1,0:T(8,128)(2,1)}, bf16[4,512,128]{2,1,0:T(8,128)(2,1)}, u32[]{:S(2)}, u32[]{:S(2)}) collective-permute-start(bf16[4,512,128]{2,1,0:T(8,128)(2,1)} %copy-done.6), channel_id=1, source_target_pairs={{0,9},{1,8},{2,11},{3,10},{4,13},{5,12},{6,15},{7,14},{8,17},{9,16... | collective-permute-start | bytes 1572872 | tf_op jit(solution)/shard_map/ppermute | solution.py:484
  93.5 22.9 %collective-permute-start.18 = (bf16[4,512,128]{2,1,0:T(8,128)(2,1)}, bf16[4,512,128]{2,1,0:T(8,128)(2,1)}, u32[]{:S(2)}, u32[]{:S(2)}) collective-permute-start(bf16[4,512,128]{2,1,0:T(8,128)(2,1)} %copy-done.5), channel_id=1, source_target_pairs={{0,7},{1,6},{2,1},{3,0},{4,3},{5,2},{6,5},{7,4},{8,15},{9,14},{10,... | collective-permute-start | bytes 1572872 | tf_op jit(solution)/shard_map/ppermute | solution.py:484
  97.2 19.2 %collective-permute-start.19 = (bf16[4,512,128]{2,1,0:T(8,128)(2,1)}, bf16[4,512,128]{2,1,0:T(8,128)(2,1)}, u32[]{:S(2)}, u32[]{:S(2)}) collective-permute-start(bf16[4,512,128]{2,1,0:T(8,128)(2,1)} %copy-done.4), channel_id=1, source_target_pairs={{0,25},{1,24},{2,27},{3,26},{4,29},{5,28},{6,31},{7,30},{8,1},{9,0... | collective-permute-start | bytes 1572872 | tf_op jit(solution)/shard_map/ppermute | solution.py:484
  124.7 29.2 %all-to-all-start.1 = ((bf16[8,22,16,128]{3,2,1,0:T(8,128)(2,1)}), bf16[8,22,16,128]{3,2,1,0:T(8,128)(2,1)S(1)}, u32[]{:S(2)}, u32[]{:S(2)}) async-start(bf16[8,22,16,128]{3,2,1,0:T(8,128)(2,1)} %exchange.5), calls=%async_computation.1 | async-start | bytes 1441792 | tf_op jit(solution)/shard_map/all_to_all | solution.py:552
  (11 other events, 162.1 us)

commit v5 on v4

--- a/solution.py
+++ b/solution.py
@@ -18,7 +18,7 @@
 VMEM = pl.BlockSpec(memory_space=pltpu.VMEM)
 ANY = pl.BlockSpec(memory_space=pl.ANY)
 ENTRIES = [(dx, dy, c) for c in range(CORES) for dx in RELS for dy in RELS]
-EARLY = [entry for entry in ENTRIES if 2 not in entry and (entry[2] == 0 or entry == (0, 0, 1))]
+EARLY = [entry for entry in ENTRIES if 2 not in entry and entry[2] == 0]
 LATE = [entry for entry in ENTRIES if entry not in EARLY]
 
 
@@ -110,7 +110,12 @@
     copy = pltpu.make_async_copy(seen_ref, asked_ref, sem)
     copy.start()
     copy.wait()
-    for out_ref, (along, shift, core) in zip(out_refs, work):
+    wanted = [
+        (out_ref, m * len(RELS), *one)
+        for out_ref, unit in zip(out_refs, work)
+        for m, one in enumerate(unit)
+    ]
+    for out_ref, start, along, shift, core in wanted:
         own_ref, less_ref, more_ref, low_ref, high_ref = gathered[along]
         table = along * SIDE + RELS.index(shift)
         for r, rel in enumerate(RELS):
@@ -118,28 +123,31 @@
             asked = asked_ref[table, core, owner]
             if rel != 2:
                 source = {0: own_ref, -1: less_ref, 1: more_ref}[rel]
-                out_ref[r] = source[asked, pl.ds(0, rows), :]
+                out_ref[start + r] = source[asked, pl.ds(0, rows), :]
                 continue
 
             @pl.when(asked < half)
             def _():
-                out_ref[r] = low_ref[jnp.minimum(asked, half - 1), pl.ds(0, rows), :]
+                out_ref[start + r] = low_ref[jnp.minimum(asked, half - 1), pl.ds(0, rows), :]
 
             @pl.when(asked >= half)
             def _():
-                out_ref[r] = high_ref[jnp.maximum(asked - half, 0), pl.ds(0, rows), :]
+                out_ref[start + r] = high_ref[jnp.maximum(asked - half, 0), pl.ds(0, rows), :]
 
 
 def choose(work, gathered):
     own = gathered[0][0]
     _, rows, domain = own.shape
-    shape = jax.ShapeDtypeStruct((len(RELS), rows - EXTRA, domain), own.dtype)
+    shapes = [
+        jax.ShapeDtypeStruct((len(unit) * len(RELS), rows - EXTRA, domain), own.dtype)
+        for unit in work
+    ]
     tables = (2 * SIDE, 8, domain)
     return pl.pallas_call(
         functools.partial(choose_kernel, work),
         in_specs=[VMEM] * 10,
         out_specs=[VMEM] * len(work),
-        out_shape=[shape] * len(work),
+        out_shape=shapes,
         scratch_shapes=[
             pltpu.VMEM(tables, jnp.int32),
             pltpu.SMEM(tables, jnp.int32),
@@ -275,8 +283,9 @@
 
 def parts_of(work):
     return {
-        (entry_of(along, shift, core, rel), along): (n, r)
-        for n, (along, shift, core) in enumerate(work)
+        (entry_of(along, shift, core, rel), along): (n, m * len(RELS) + r)
+        for n, unit in enumerate(work)
+        for m, (along, shift, core) in enumerate(unit)
         for r, rel in enumerate(RELS)
     }
 
@@ -517,27 +526,26 @@
     gathered = list(zip(halves, less, more, low, high))
 
     def work_of(*shifts):
-        return tuple((along, shift, core) for shift, core in shifts for along in range(2))
+        return tuple(((along, shift, core),) for shift, core in shifts for along in range(2))
 
     def touched(*works):
         return {entry for work in works for entry, _ in parts_of(work)}
 
-    far = work_of((2, 0), (2, 1))
     works = (
-        work_of((1, 0), (-1, 0), (0, 0), (0, 1)),
-        far[:3],
-        far[3:] + work_of((1, 1), (-1, 1)),
+        work_of((1, 0), (-1, 0), (0, 0)),
+        work_of((2, 0), (2, 1)) + (((0, 0, 1), (1, 0, 1)),),
+        work_of((1, 1), (-1, 1)),
     )
     chosen = dict(zip(sum(works, ()), choose(sum(works, ()), gathered)))
-    arrived = {}
 
     def send(work):
-        for along, shift, core in work:
-            one = chosen[along, shift, core]
-            if (shift, core) != (0, 0):
-                one = step_along(1 - along, one, shift, core)
-            arrived[along, shift, core] = one
-        return [arrived[one] for one in work]
+        blocks = []
+        for unit in work:
+            along, shift, core = unit[0]
+            one = chosen[unit]
+            at_home = (shift, core) == (0, 0)
+            blocks.append(one if at_home else step_along(1 - along, one, shift, core))
+        return blocks
 
     wide, narrow = jnp.float32, jnp.bfloat16
     blocks = send(works[0])

time: 156 us -> 166 us (1.064)
  starting transfers between devices: 53.6 us -> 66.9 us
  waiting for transfers between devices: 50.1 us -> 45.4 us
  Pallas kernels: 45.7 us -> 47.8 us
    ppermute x23 -> x22, starting transfers between devices: 40.5 us -> 55 us  [moved(): lax.ppermute(array, 'pair', [(at(x, y, c), at(x + dx, y + dy, c + core))...]
    ppermute x23 -> x22, waiting for transfers between devices: 23.7 us -> 17.4 us  [moved(): lax.ppermute(array, 'pair', [(at(x, y, c), at(x + dx, y + dy, c + core))...]
    all_to_all x1, starting transfers between devices: 7.07 us -> 5.29 us  [on_device(): late = lax.all_to_all(late, 'aux', split_axis=0, concat_axis=0, tiled=True)]
    unnamed x21 -> x19, local copies, waits for them, and re-layouts: 4.72 us -> 4.73 us
  transfers between devices with their start and end apart: 25 -> 24, of which waited for: 10 -> 7; matrix products, arithmetic and copies ran while one was open for 0% -> 0% of each run, Pallas kernels for 21% -> 21%
where the time goes in v5:
time: 166 us
  starting transfers between devices  66.9 us (40%)
  Pallas kernels  47.8 us (29%)
  waiting for transfers between devices  45.4 us (27%)
  local copies, waits for them, and re-layouts  5.62 us (3%)
    ppermute x22, starting transfers between devices, moved(): lax.ppermute(array, 'pair', [(at(x, y, c), at(x + dx, y + dy, c + core))...  55 us
    pallas_call x3, Pallas kernels, exchange(): pl.pallas_call(functools.partial(exchange_kernel, work, before, sets, own...  21.5 us
    all_to_all x1, waiting for transfers between devices, on_device(): late = lax.all_to_all(late, 'aux', split_axis=0, concat_axis=0, tiled=True)  21.4 us
    pallas_call x1, Pallas kernels, left_of(): pl.pallas_call(left_kernel, in_specs=[SMEM] * 2 + [VMEM] * 3, out_specs=[...  19.1 us
    ppermute x22, waiting for transfers between devices, moved(): lax.ppermute(array, 'pair', [(at(x, y, c), at(x + dx, y + dy, c + core))...  17.4 us
    all_to_all x1, starting transfers between devices, on_device(): lax.all_to_all(early, 'aux', split_axis=0, concat_axis=0, tiled=True)  6.62 us
    all_to_all x1, waiting for transfers between devices, on_device(): lax.all_to_all(early, 'aux', split_axis=0, concat_axis=0, tiled=True)  6.57 us
    all_to_all x1, starting transfers between devices, on_device(): late = lax.all_to_all(late, 'aux', split_axis=0, concat_axis=0, tiled=True)  5.29 us
  transfers between devices with their start and end apart: 24, of which 7 were waited for; matrix products, arithmetic and copies ran while one was open for 0% of the time, Pallas kernels for 21%

profile of v5, /device:TPU:1, one launch (start us, length us, event | category | flops | bytes accessed | tf_op | source)
XLA Modules:
  0.0 166.1 jit_solution(17237398214932987533)
XLA Ops:
  0.9 3.3 %collective-permute-start = (bf16[16,128]{1,0:T(8,128)(2,1)S(1)}, bf16[16,128]{1,0:T(8,128)(2,1)S(1)}, u32[]{:S(2)}, u32[]{:S(2)}) collective-permute-start(bf16[16,128]{1,0:T(8,128)(2,1)S(1)} %broadcast_in_dim.2.wanted_ref), channel_id=1, source_target_pairs={{0,1},{1,0},{2,3},{3,2},{4,5},{5,4},{6,7},{7,6},{8,9},{9,8},{10,11... | collective-permute-start | bytes 12296 | tf_op jit(solution)/shard_map/ppermute | solution.py:493
  7.7 2.7 %collective-permute-start.2 = (bf16[8,528,128]{2,1,0:T(8,128)(2,1)S(1)}, bf16[8,528,128]{2,1,0:T(8,128)(2,1)S(1)}, u32[]{:S(2)}, u32[]{:S(2)}) collective-permute-start(bf16[8,528,128]{2,1,0:T(8,128)(2,1)S(1)} %get-tuple-element.30.first_ref.refs_0_), channel_id=1, source_target_pairs={{0,24},{1,25},{2,26},{3,27},{4,28},{5,29},{6,30},{7,31},{8,0},{9,1... | collective-permute-start | bytes 3244040 | tf_op jit(solution)/shard_map/ppermute | solution.py:493
  10.3 2.7 %collective-permute-start.4 = (bf16[8,528,128]{2,1,0:T(8,128)(2,1)S(1)}, bf16[8,528,128]{2,1,0:T(8,128)(2,1)S(1)}, u32[]{:S(2)}, u32[]{:S(2)}) collective-permute-start(bf16[8,528,128]{2,1,0:T(8,128)(2,1)S(1)} %get-tuple-element.31.second_ref.refs_5_), channel_id=1, source_target_pairs={{0,6},{1,7},{2,0},{3,1},{4,2},{5,3},{6,4},{7,5},{8,14},{9,15},{10,... | collective-permute-start | bytes 3244040 | tf_op jit(solution)/shard_map/ppermute | solution.py:493
  13.0 2.3 %copy-done = bf16[136,128,128]{2,1,0:T(8,128)(2,1)S(1)} copy-done((bf16[136,128,128]{2,1,0:T(8,128)(2,1)S(1)}, bf16[136,128,128]{2,1,0:T(8,128)(2,1)}, u32[]{:S(2)}) %copy-start) | copy-done | bytes 4456472
  15.3 19.1 %left.1 = (bf16[136,2,320,512]{3,2,1,0:T(8,128)(2,1)}, bf16[8,2,16,128]{3,2,1,0:T(8,128)(2,1)S(1)}) custom-call(s32[136]{0:T(256)S(1)} %and_select_fusion.1.left_index, s32[136]{0:T(256)S(1)} %get-tuple-element.56.right_index, bf16[8,528,128]{2,1,0:T(8,128)(2,1)S(1)} %get-tuple-element.30.first_ref.refs_0_, ...), custom_call_target="tpu_custom_call" | custom-call | tf_op jit(solution)/shard_map/left/pallas_call | solution.py:259
  36.2 2.7 %collective-permute-start.6 = (bf16[4,528,128]{2,1,0:T(8,128)(2,1)S(1)}, bf16[4,528,128]{2,1,0:T(8,128)(2,1)S(1)}, u32[]{:S(2)}, u32[]{:S(2)}) collective-permute-start(bf16[4,528,128]{2,1,0:T(8,128)(2,1)S(1)} %get-tuple-element.35), channel_id=1, source_target_pairs={{0,24},{1,25},{2,26},{3,27},{4,28},{5,29},{6,30},{7,31},{8,0},{9,1... | collective-permute-start | bytes 1622024 | tf_op jit(solution)/shard_map/ppermute | solution.py:493
  38.9 2.7 %collective-permute-start.8 = (bf16[4,528,128]{2,1,0:T(8,128)(2,1)S(1)}, bf16[4,528,128]{2,1,0:T(8,128)(2,1)S(1)}, u32[]{:S(2)}, u32[]{:S(2)}) collective-permute-start(bf16[4,528,128]{2,1,0:T(8,128)(2,1)S(1)} %get-tuple-element.37), channel_id=1, source_target_pairs={{0,6},{1,7},{2,0},{3,1},{4,2},{5,3},{6,4},{7,5},{8,14},{9,15},{10,... | collective-permute-start | bytes 1622024 | tf_op jit(solution)/shard_map/ppermute | solution.py:493
  41.6 7.8 %collective-permute-done.5.refs_3_ = bf16[4,528,128]{2,1,0:T(8,128)(2,1)S(1)} collective-permute-done((bf16[4,528,128]{2,1,0:T(8,128)(2,1)S(1)}, bf16[4,528,128]{2,1,0:T(8,128)(2,1)S(1)}, u32[]{:S(2)}, u32[]{:S(2)}) %collective-permute-start.5) | collective-permute-done | bytes 540704 | tf_op jit(solution)/shard_map/ppermute | solution.py:493
  49.4 2.1 %collective-permute-done.7.refs_8_ = bf16[4,528,128]{2,1,0:T(8,128)(2,1)S(1)} collective-permute-done((bf16[4,528,128]{2,1,0:T(8,128)(2,1)S(1)}, bf16[4,528,128]{2,1,0:T(8,128)(2,1)S(1)}, u32[]{:S(2)}, u32[]{:S(2)}) %collective-permute-start.7) | collective-permute-done | bytes 540704 | tf_op jit(solution)/shard_map/ppermute | solution.py:493
  51.5 3.5 %choose.1 = (bf16[4,512,128]{2,1,0:T(8,128)(2,1)S(1)}, bf16[4,512,128]{2,1,0:T(8,128)(2,1)S(1)}, bf16[4,512,128]{2,1,0:T(8,128)(2,1)S(1)}, bf16[4,512,128]{2,1,0...) custom-call(bf16[8,528,128]{2,1,0:T(8,128)(2,1)S(1)} %get-tuple-elem, ...), custom_call_target="tpu_custom_call" | custom-call | tf_op jit(solution)/shard_map/choose/pallas_call | solution.py:146
  55.5 2.5 %collective-permute-start.11 = (bf16[4,512,128]{2,1,0:T(8,128)(2,1)S(1)}, bf16[4,512,128]{2,1,0:T(8,128)(2,1)S(1)}, u32[]{:S(2)}, u32[]{:S(2)}) collective-permute-start(bf16[4,512,128]{2,1,0:T(8,128)(2,1)S(1)} %get-tuple-element.40), channel_id=1, source_target_pairs={{0,6},{1,7},{2,0},{3,1},{4,2},{5,3},{6,4},{7,5},{8,14},{9,15},{10,... | collective-permute-start | bytes 1572872 | tf_op jit(solution)/shard_map/ppermute | solution.py:493
  57.9 2.6 %collective-permute-start.12 = (bf16[4,512,128]{2,1,0:T(8,128)(2,1)S(1)}, bf16[4,512,128]{2,1,0:T(8,128)(2,1)S(1)}, u32[]{:S(2)}, u32[]{:S(2)}) collective-permute-start(bf16[4,512,128]{2,1,0:T(8,128)(2,1)S(1)} %get-tuple-element.41), channel_id=1, source_target_pairs={{0,24},{1,25},{2,26},{3,27},{4,28},{5,29},{6,30},{7,31},{8,0},{9,1... | collective-permute-start | bytes 1572872 | tf_op jit(solution)/shard_map/ppermute | solution.py:493
  61.4 5.1 %collective-permute-done.9.refs_0_ = bf16[4,512,128]{2,1,0:T(8,128)(2,1)S(1)} collective-permute-done((bf16[4,512,128]{2,1,0:T(8,128)(2,1)S(1)}, bf16[4,512,128]{2,1,0:T(8,128)(2,1)S(1)}, u32[]{:S(2)}, u32[]{:S(2)}) %collective-permute-start.9) | collective-permute-done | bytes 524320 | tf_op jit(solution)/shard_map/ppermute | solution.py:493
  66.5 15.1 %collective-permute-start.19 = (bf16[4,512,128]{2,1,0:T(8,128)(2,1)}, bf16[4,512,128]{2,1,0:T(8,128)(2,1)}, u32[]{:S(2)}, u32[]{:S(2)}) collective-permute-start(bf16[4,512,128]{2,1,0:T(8,128)(2,1)} %get-tuple-element.51), channel_id=1, source_target_pairs={{0,5},{1,4},{2,7},{3,6},{4,1},{5,0},{6,3},{7,2},{8,13},{9,12},{10,... | collective-permute-start | bytes 1572872 | tf_op jit(solution)/shard_map/ppermute | solution.py:493
  81.7 10.9 %collective-permute-start.21 = (bf16[8,512,128]{2,1,0:T(8,128)(2,1)}, bf16[8,512,128]{2,1,0:T(8,128)(2,1)S(1)}, u32[]{:S(2)}, u32[]{:S(2)}) collective-permute-start(bf16[8,512,128]{2,1,0:T(8,128)(2,1)} %get-tuple-element.53), channel_id=1, source_target_pairs={{0,1},{1,0},{2,3},{3,2},{4,5},{5,4},{6,7},{7,6},{8,9},{9,8},{10,11... | collective-permute-start | bytes 3145736 | tf_op jit(solution)/shard_map/ppermute | solution.py:493
  93.9 6.5 %exchange.3 = (bf16[8,11,16,128]{3,2,1,0:T(8,128)(2,1)S(1)}, f32[8,23,16,128]{3,2,1,0:T(8,128)S(1)}) custom-call(bf16[136,2,320,512]{3,2,1,0:T(8,128)(2,1)} %get-tuple-element.32.left_ref, bf16[4,512,128]{2,1,0:T(8,128)(2,1)S(1)} %collective-permute-done.9.refs_0_, bf16[4,512,128]{2,1,0:T(8,128)(2,1)S(1)} %collective-permute-done.10.refs_1_, ...), custom_call_target="tpu_custom_call" | custom-call | tf_op jit(solution)/shard_map/exchange/pallas_call | solution.py:373
  101.1 6.6 %all-to-all-start = ((bf16[8,11,16,128]{3,2,1,0:T(8,128)(2,1)}), bf16[8,11,16,128]{3,2,1,0:T(8,128)(2,1)S(1)}, u32[]{:S(2)}, u32[]{:S(2)}) async-start(bf16[8,11,16,128]{3,2,1,0:T(8,128)(2,1)} %copy-done.2), calls=%async_computation | async-start | bytes 720896 | tf_op jit(solution)/shard_map/all_to_all | solution.py:553
  107.9 2.6 %collective-permute-start.14 = (bf16[4,512,128]{2,1,0:T(8,128)(2,1)}, bf16[4,512,128]{2,1,0:T(8,128)(2,1)}, u32[]{:S(2)}, u32[]{:S(2)}) collective-permute-start(bf16[4,512,128]{2,1,0:T(8,128)(2,1)} %copy-done.6), channel_id=1, source_target_pairs={{0,9},{1,8},{2,11},{3,10},{4,13},{5,12},{6,15},{7,14},{8,17},{9,16... | collective-permute-start | bytes 1572872 | tf_op jit(solution)/shard_map/ppermute | solution.py:493
  110.4 3.0 %collective-permute-start.15 = (bf16[4,512,128]{2,1,0:T(8,128)(2,1)}, bf16[4,512,128]{2,1,0:T(8,128)(2,1)}, u32[]{:S(2)}, u32[]{:S(2)}) collective-permute-start(bf16[4,512,128]{2,1,0:T(8,128)(2,1)} %copy-done.5), channel_id=1, source_target_pairs={{0,7},{1,6},{2,1},{3,0},{4,3},{5,2},{6,5},{7,4},{8,15},{9,14},{10,... | collective-permute-start | bytes 1572872 | tf_op jit(solution)/shard_map/ppermute | solution.py:493
  115.0 6.6 %all-to-all-done.__1_.early_ref = bf16[8,11,16,128]{3,2,1,0:T(8,128)(2,1)S(1)} async-done(((bf16[8,11,16,128]{3,2,1,0:T(8,128)(2,1)}), bf16[8,11,16,128]{3,2,1,0:T(8,128)(2,1)S(1)}, u32[]{:S(2)}, u32[]{:S(2)}) %all-to-all-start) | async-done | bytes 360480 | tf_op jit(solution)/shard_map/all_to_all | solution.py:553
  121.6 8.0 %exchange.4.refs_4_ = f32[8,23,16,128]{3,2,1,0:T(8,128)S(1)} custom-call(bf16[136,2,320,512]{3,2,1,0:T(8,128)(2,1)} %get-tuple-element.32.left_ref, bf16[4,512,128]{2,1,0:T(8,128)(2,1)S(1)} %collective-permute-done.17.refs_0_, bf16[4,512,128]{2,1,0:T(8,128)(2,1)} %collective-permute-done.18.refs_1_, bf16[4,512,128]{2,1,0:T(8,128)(2,1)} %collective-permute-done.19.refs_2_, ...), custom_call_target="tpu_custom_call" | custom-call | tf_op jit(solution)/shard_map/exchange/pallas_call | solution.py:373
  129.6 7.0 %exchange.5 = bf16[8,23,16,128]{3,2,1,0:T(8,128)(2,1)} custom-call(bf16[136,2,320,512]{3,2,1,0:T(8,128)(2,1)} %get-tuple-element.32.left_ref, bf16[4,512,128]{2,1,0:T(8,128)(2,1)} %collective-permute-done.13.refs_0_, bf16[4,512,128]{2,1,0:T(8,128)(2,1)} %collective-permute-done.14.refs_1_, bf16[4,512,128]{2,1,0:T(8,128)(2,1)} %collective-permute-done.15.refs_2_, ...), custom_call_target="tpu_custom_call" | custom-call | tf_op jit(solution)/shard_map/exchange/pallas_call | solution.py:373
  136.6 5.3 %all-to-all-start.1 = ((bf16[8,23,16,128]{3,2,1,0:T(8,128)(2,1)}), bf16[8,23,16,128]{3,2,1,0:T(8,128)(2,1)S(1)}, u32[]{:S(2)}, u32[]{:S(2)}) async-start(bf16[8,23,16,128]{3,2,1,0:T(8,128)(2,1)} %exchange.5), calls=%async_computation.1 | async-start | bytes 1507328 | tf_op jit(solution)/shard_map/all_to_all | solution.py:560
  143.4 21.4 %all-to-all-done.1.late_ref = bf16[8,23,16,128]{3,2,1,0:T(8,128)(2,1)S(1)} async-done(((bf16[8,23,16,128]{3,2,1,0:T(8,128)(2,1)}), bf16[8,23,16,128]{3,2,1,0:T(8,128)(2,1)S(1)}, u32[]{:S(2)}, u32[]{:S(2)}) %all-to-all-start.1) | async-done | bytes 753696 | tf_op jit(solution)/shard_map/all_to_all | solution.py:560
  (59 shorter events, 13.8 us)
Async XLA Ops:
  0.9 4.2 %collective-permute-start = (bf16[16,128]{1,0:T(8,128)(2,1)S(1)}, bf16[16,128]{1,0:T(8,128)(2,1)S(1)}, u32[]{:S(2)}, u32[]{:S(2)}) collective-permute-start(bf16[16,128]{1,0:T(8,128)(2,1)S(1)} %broadcast_in_dim.2.wanted_ref), channel_id=1, source_target_pairs={{0,1},{1,0},{2,3},{3,2},{4,5},{5,4},{6,7},{7,6},{8,9},{9,8},{10,11... | collective-permute-start | bytes 12296 | tf_op jit(solution)/shard_map/ppermute | solution.py:493
  7.6 26.9 %collective-permute-start.1 = (bf16[8,528,128]{2,1,0:T(8,128)(2,1)S(1)}, bf16[8,528,128]{2,1,0:T(8,128)(2,1)S(1)}, u32[]{:S(2)}, u32[]{:S(2)}) collective-permute-start(bf16[8,528,128]{2,1,0:T(8,128)(2,1)S(1)} %get-tuple-element.30.first_ref.refs_0_), channel_id=1, source_target_pairs={{0,8},{1,9},{2,10},{3,11},{4,12},{5,13},{6,14},{7,15},{8,16},{9,17... | collective-permute-start | bytes 3244040 | tf_op jit(solution)/shard_map/ppermute | solution.py:493
  7.7 26.8 %collective-permute-start.2 = (bf16[8,528,128]{2,1,0:T(8,128)(2,1)S(1)}, bf16[8,528,128]{2,1,0:T(8,128)(2,1)S(1)}, u32[]{:S(2)}, u32[]{:S(2)}) collective-permute-start(bf16[8,528,128]{2,1,0:T(8,128)(2,1)S(1)} %get-tuple-element.30.first_ref.refs_0_), channel_id=1, source_target_pairs={{0,24},{1,25},{2,26},{3,27},{4,28},{5,29},{6,30},{7,31},{8,0},{9,1... | collective-permute-start | bytes 3244040 | tf_op jit(solution)/shard_map/ppermute | solution.py:493
  10.3 25.7 %collective-permute-start.3 = (bf16[8,528,128]{2,1,0:T(8,128)(2,1)S(1)}, bf16[8,528,128]{2,1,0:T(8,128)(2,1)S(1)}, u32[]{:S(2)}, u32[]{:S(2)}) collective-permute-start(bf16[8,528,128]{2,1,0:T(8,128)(2,1)S(1)} %get-tuple-element.31.second_ref.refs_5_), channel_id=1, source_target_pairs={{0,2},{1,3},{2,4},{3,5},{4,6},{5,7},{6,0},{7,1},{8,10},{9,11},{10,... | collective-permute-start | bytes 3244040 | tf_op jit(solution)/shard_map/ppermute | solution.py:493
  10.3 25.7 %collective-permute-start.4 = (bf16[8,528,128]{2,1,0:T(8,128)(2,1)S(1)}, bf16[8,528,128]{2,1,0:T(8,128)(2,1)S(1)}, u32[]{:S(2)}, u32[]{:S(2)}) collective-permute-start(bf16[8,528,128]{2,1,0:T(8,128)(2,1)S(1)} %get-tuple-element.31.second_ref.refs_5_), channel_id=1, source_target_pairs={{0,6},{1,7},{2,0},{3,1},{4,2},{5,3},{6,4},{7,5},{8,14},{9,15},{10,... | collective-permute-start | bytes 3244040 | tf_op jit(solution)/shard_map/ppermute | solution.py:493
  36.2 13.2 %collective-permute-start.5 = (bf16[4,528,128]{2,1,0:T(8,128)(2,1)S(1)}, bf16[4,528,128]{2,1,0:T(8,128)(2,1)S(1)}, u32[]{:S(2)}, u32[]{:S(2)}) collective-permute-start(bf16[4,528,128]{2,1,0:T(8,128)(2,1)S(1)} %get-tuple-element.34), channel_id=1, source_target_pairs={{0,8},{1,9},{2,10},{3,11},{4,12},{5,13},{6,14},{7,15},{8,16},{9,17... | collective-permute-start | bytes 1622024 | tf_op jit(solution)/shard_map/ppermute | solution.py:493
  36.2 13.2 %collective-permute-start.6 = (bf16[4,528,128]{2,1,0:T(8,128)(2,1)S(1)}, bf16[4,528,128]{2,1,0:T(8,128)(2,1)S(1)}, u32[]{:S(2)}, u32[]{:S(2)}) collective-permute-start(bf16[4,528,128]{2,1,0:T(8,128)(2,1)S(1)} %get-tuple-element.35), channel_id=1, source_target_pairs={{0,24},{1,25},{2,26},{3,27},{4,28},{5,29},{6,30},{7,31},{8,0},{9,1... | collective-permute-start | bytes 1622024 | tf_op jit(solution)/shard_map/ppermute | solution.py:493
  38.9 12.6 %collective-permute-start.7 = (bf16[4,528,128]{2,1,0:T(8,128)(2,1)S(1)}, bf16[4,528,128]{2,1,0:T(8,128)(2,1)S(1)}, u32[]{:S(2)}, u32[]{:S(2)}) collective-permute-start(bf16[4,528,128]{2,1,0:T(8,128)(2,1)S(1)} %get-tuple-element.36), channel_id=1, source_target_pairs={{0,2},{1,3},{2,4},{3,5},{4,6},{5,7},{6,0},{7,1},{8,10},{9,11},{10,... | collective-permute-start | bytes 1622024 | tf_op jit(solution)/shard_map/ppermute | solution.py:493
  38.9 12.6 %collective-permute-start.8 = (bf16[4,528,128]{2,1,0:T(8,128)(2,1)S(1)}, bf16[4,528,128]{2,1,0:T(8,128)(2,1)S(1)}, u32[]{:S(2)}, u32[]{:S(2)}) collective-permute-start(bf16[4,528,128]{2,1,0:T(8,128)(2,1)S(1)} %get-tuple-element.37), channel_id=1, source_target_pairs={{0,6},{1,7},{2,0},{3,1},{4,2},{5,3},{6,4},{7,5},{8,14},{9,15},{10,... | collective-permute-start | bytes 1622024 | tf_op jit(solution)/shard_map/ppermute | solution.py:493
  55.1 11.4 %collective-permute-start.9 = (bf16[4,512,128]{2,1,0:T(8,128)(2,1)S(1)}, bf16[4,512,128]{2,1,0:T(8,128)(2,1)S(1)}, u32[]{:S(2)}, u32[]{:S(2)}) collective-permute-start(bf16[4,512,128]{2,1,0:T(8,128)(2,1)S(1)} %get-tuple-element.38), channel_id=1, source_target_pairs={{0,2},{1,3},{2,4},{3,5},{4,6},{5,7},{6,0},{7,1},{8,10},{9,11},{10,... | collective-permute-start | bytes 1572872 | tf_op jit(solution)/shard_map/ppermute | solution.py:493
  55.5 11.1 %collective-permute-start.10 = (bf16[4,512,128]{2,1,0:T(8,128)(2,1)S(1)}, bf16[4,512,128]{2,1,0:T(8,128)(2,1)S(1)}, u32[]{:S(2)}, u32[]{:S(2)}) collective-permute-start(bf16[4,512,128]{2,1,0:T(8,128)(2,1)S(1)} %get-tuple-element.39), channel_id=1, source_target_pairs={{0,8},{1,9},{2,10},{3,11},{4,12},{5,13},{6,14},{7,15},{8,16},{9,17... | collective-permute-start | bytes 1572872 | tf_op jit(solution)/shard_map/ppermute | solution.py:493
  55.5 26.2 %collective-permute-start.11 = (bf16[4,512,128]{2,1,0:T(8,128)(2,1)S(1)}, bf16[4,512,128]{2,1,0:T(8,128)(2,1)S(1)}, u32[]{:S(2)}, u32[]{:S(2)}) collective-permute-start(bf16[4,512,128]{2,1,0:T(8,128)(2,1)S(1)} %get-tuple-element.40), channel_id=1, source_target_pairs={{0,6},{1,7},{2,0},{3,1},{4,2},{5,3},{6,4},{7,5},{8,14},{9,15},{10,... | collective-permute-start | bytes 1572872 | tf_op jit(solution)/shard_map/ppermute | solution.py:493
  57.9 34.6 %collective-permute-start.12 = (bf16[4,512,128]{2,1,0:T(8,128)(2,1)S(1)}, bf16[4,512,128]{2,1,0:T(8,128)(2,1)S(1)}, u32[]{:S(2)}, u32[]{:S(2)}) collective-permute-start(bf16[4,512,128]{2,1,0:T(8,128)(2,1)S(1)} %get-tuple-element.41), channel_id=1, source_target_pairs={{0,24},{1,25},{2,26},{3,27},{4,28},{5,29},{6,30},{7,31},{8,0},{9,1... | collective-permute-start | bytes 1572872 | tf_op jit(solution)/shard_map/ppermute | solution.py:493
  60.5 47.2 %collective-permute-start.17 = (bf16[4,512,128]{2,1,0:T(8,128)(2,1)}, bf16[4,512,128]{2,1,0:T(8,128)(2,1)S(1)}, u32[]{:S(2)}, u32[]{:S(2)}) collective-permute-start(bf16[4,512,128]{2,1,0:T(8,128)(2,1)} %get-tuple-element.49), channel_id=1, source_target_pairs={{0,4},{1,5},{2,6},{3,7},{4,0},{5,1},{6,2},{7,3},{8,12},{9,13},{10,... | collective-permute-start | bytes 1572872 | tf_op jit(solution)/shard_map/ppermute | solution.py:493
  66.5 41.4 %collective-permute-start.18 = (bf16[4,512,128]{2,1,0:T(8,128)(2,1)}, bf16[4,512,128]{2,1,0:T(8,128)(2,1)}, u32[]{:S(2)}, u32[]{:S(2)}) collective-permute-start(bf16[4,512,128]{2,1,0:T(8,128)(2,1)} %get-tuple-element.50), channel_id=1, source_target_pairs={{0,16},{1,17},{2,18},{3,19},{4,20},{5,21},{6,22},{7,23},{8,24},{9,... | collective-permute-start | bytes 1572872 | tf_op jit(solution)/shard_map/ppermute | solution.py:493
  66.5 43.9 %collective-permute-start.19 = (bf16[4,512,128]{2,1,0:T(8,128)(2,1)}, bf16[4,512,128]{2,1,0:T(8,128)(2,1)}, u32[]{:S(2)}, u32[]{:S(2)}) collective-permute-start(bf16[4,512,128]{2,1,0:T(8,128)(2,1)} %get-tuple-element.51), channel_id=1, source_target_pairs={{0,5},{1,4},{2,7},{3,6},{4,1},{5,0},{6,3},{7,2},{8,13},{9,12},{10,... | collective-permute-start | bytes 1572872 | tf_op jit(solution)/shard_map/ppermute | solution.py:493
  81.7 39.9 %collective-permute-start.21 = (bf16[8,512,128]{2,1,0:T(8,128)(2,1)}, bf16[8,512,128]{2,1,0:T(8,128)(2,1)S(1)}, u32[]{:S(2)}, u32[]{:S(2)}) collective-permute-start(bf16[8,512,128]{2,1,0:T(8,128)(2,1)} %get-tuple-element.53), channel_id=1, source_target_pairs={{0,1},{1,0},{2,3},{3,2},{4,5},{5,4},{6,7},{7,6},{8,9},{9,8},{10,11... | collective-permute-start | bytes 3145736 | tf_op jit(solution)/shard_map/ppermute | solution.py:493
  92.6 20.8 %collective-permute-start.20 = (bf16[4,512,128]{2,1,0:T(8,128)(2,1)}, bf16[4,512,128]{2,1,0:T(8,128)(2,1)}, u32[]{:S(2)}, u32[]{:S(2)}) collective-permute-start(bf16[4,512,128]{2,1,0:T(8,128)(2,1)} %get-tuple-element.52), channel_id=1, source_target_pairs={{0,17},{1,16},{2,19},{3,18},{4,21},{5,20},{6,23},{7,22},{8,25},{9,... | collective-permute-start | bytes 1572872 | tf_op jit(solution)/shard_map/ppermute | solution.py:493
  101.1 20.4 %all-to-all-start = ((bf16[8,11,16,128]{3,2,1,0:T(8,128)(2,1)}), bf16[8,11,16,128]{3,2,1,0:T(8,128)(2,1)S(1)}, u32[]{:S(2)}, u32[]{:S(2)}) async-start(bf16[8,11,16,128]{3,2,1,0:T(8,128)(2,1)} %copy-done.2), calls=%async_computation | async-start | bytes 720896 | tf_op jit(solution)/shard_map/all_to_all | solution.py:553
  107.8 21.8 %collective-permute-start.13 = (bf16[4,512,128]{2,1,0:T(8,128)(2,1)}, bf16[4,512,128]{2,1,0:T(8,128)(2,1)}, u32[]{:S(2)}, u32[]{:S(2)}) collective-permute-start(bf16[4,512,128]{2,1,0:T(8,128)(2,1)} %copy-done.7), channel_id=1, source_target_pairs={{0,3},{1,2},{2,5},{3,4},{4,7},{5,6},{6,1},{7,0},{8,11},{9,10},{10,... | collective-permute-start | bytes 1572872 | tf_op jit(solution)/shard_map/ppermute | solution.py:493
  107.9 21.7 %collective-permute-start.14 = (bf16[4,512,128]{2,1,0:T(8,128)(2,1)}, bf16[4,512,128]{2,1,0:T(8,128)(2,1)}, u32[]{:S(2)}, u32[]{:S(2)}) collective-permute-start(bf16[4,512,128]{2,1,0:T(8,128)(2,1)} %copy-done.6), channel_id=1, source_target_pairs={{0,9},{1,8},{2,11},{3,10},{4,13},{5,12},{6,15},{7,14},{8,17},{9,16... | collective-permute-start | bytes 1572872 | tf_op jit(solution)/shard_map/ppermute | solution.py:493
  110.4 19.2 %collective-permute-start.15 = (bf16[4,512,128]{2,1,0:T(8,128)(2,1)}, bf16[4,512,128]{2,1,0:T(8,128)(2,1)}, u32[]{:S(2)}, u32[]{:S(2)}) collective-permute-start(bf16[4,512,128]{2,1,0:T(8,128)(2,1)} %copy-done.5), channel_id=1, source_target_pairs={{0,7},{1,6},{2,1},{3,0},{4,3},{5,2},{6,5},{7,4},{8,15},{9,14},{10,... | collective-permute-start | bytes 1572872 | tf_op jit(solution)/shard_map/ppermute | solution.py:493
  113.4 16.2 %collective-permute-start.16 = (bf16[4,512,128]{2,1,0:T(8,128)(2,1)}, bf16[4,512,128]{2,1,0:T(8,128)(2,1)}, u32[]{:S(2)}, u32[]{:S(2)}) collective-permute-start(bf16[4,512,128]{2,1,0:T(8,128)(2,1)} %copy-done.4), channel_id=1, source_target_pairs={{0,25},{1,24},{2,27},{3,26},{4,29},{5,28},{6,31},{7,30},{8,1},{9,0... | collective-permute-start | bytes 1572872 | tf_op jit(solution)/shard_map/ppermute | solution.py:493
  136.6 28.2 %all-to-all-start.1 = ((bf16[8,23,16,128]{3,2,1,0:T(8,128)(2,1)}), bf16[8,23,16,128]{3,2,1,0:T(8,128)(2,1)S(1)}, u32[]{:S(2)}, u32[]{:S(2)}) async-start(bf16[8,23,16,128]{3,2,1,0:T(8,128)(2,1)} %exchange.5), calls=%async_computation.1 | async-start | bytes 1507328 | tf_op jit(solution)/shard_map/all_to_all | solution.py:560
  (9 other events, 196.5 us)

commit v6 on v5

--- a/solution.py
+++ b/solution.py
@@ -18,7 +18,7 @@
 VMEM = pl.BlockSpec(memory_space=pltpu.VMEM)
 ANY = pl.BlockSpec(memory_space=pl.ANY)
 ENTRIES = [(dx, dy, c) for c in range(CORES) for dx in RELS for dy in RELS]
-EARLY = [entry for entry in ENTRIES if 2 not in entry and entry[2] == 0]
+EARLY = [entry for entry in ENTRIES if 2 not in entry and (entry[2] == 0 or entry == (0, 0, 1))]
 LATE = [entry for entry in ENTRIES if entry not in EARLY]
 
 
@@ -531,12 +531,15 @@
     def touched(*works):
         return {entry for work in works for entry, _ in parts_of(work)}
 
+    far = work_of((2, 0), (2, 1))
     works = (
-        work_of((1, 0), (-1, 0), (0, 0)),
-        work_of((2, 0), (2, 1)) + (((0, 0, 1), (1, 0, 1)),),
-        work_of((1, 1), (-1, 1)),
+        work_of((1, 0), (-1, 0), (0, 0)) + (((0, 0, 1), (1, 0, 1)),),
+        far[:3],
+        far[3:] + work_of((1, 1), (-1, 1)),
     )
-    chosen = dict(zip(sum(works, ()), choose(sum(works, ()), gathered)))
+    chosen = {}
+    for work in (works[0], works[1] + works[2]):
+        chosen.update(zip(work, choose(work, gathered)))
 
     def send(work):
         blocks = []

time: 166 us -> 178 us (1.072)
  waiting for transfers between devices: 45.4 us -> 54.4 us
  starting transfers between devices: 66.9 us -> 70.1 us
    ppermute x22, waiting for transfers between devices: 17.4 us -> 33.7 us  [moved(): lax.ppermute(array, 'pair', [(at(x, y, c), at(x + dx, y + dy, c + core))...]
    all_to_all x1, waiting for transfers between devices: 6.57 us -> 0.01 us  [on_device(): lax.all_to_all(early, 'aux', split_axis=0, concat_axis=0, tiled=True)]
    all_to_all x1, starting transfers between devices: 5.29 us -> 7.08 us  [on_device(): late = lax.all_to_all(late, 'aux', split_axis=0, concat_axis=0, tiled=True)]
    pallas_call x1 -> x2, Pallas kernels: 3.54 us -> 4.14 us  [choose(): pl.pallas_call(functools.partial(choose_kernel, work), in_specs=[VMEM] *...]
    unnamed x19 -> x21, local copies, waits for them, and re-layouts: 4.73 us -> 4.72 us
  transfers between devices with their start and end apart: 24 -> 24, of which waited for: 7 -> 10; matrix products, arithmetic and copies ran while one was open for 0% -> 0% of each run, Pallas kernels for 21% -> 20%
where the time goes in v6:
time: 178 us; the launch traced here: 177 us
  starting transfers between devices  70.1 us (39%)
  waiting for transfers between devices  54.4 us (31%)
  Pallas kernels  46.8 us (26%)
  local copies, waits for them, and re-layouts  5.62 us (3%)
    ppermute x22, starting transfers between devices, moved(): lax.ppermute(array, 'pair', [(at(x, y, c), at(x + dx, y + dy, c + core))...  56.5 us
    ppermute x22, waiting for transfers between devices, moved(): lax.ppermute(array, 'pair', [(at(x, y, c), at(x + dx, y + dy, c + core))...  33.7 us
    all_to_all x1, waiting for transfers between devices, on_device(): late = lax.all_to_all(late, 'aux', split_axis=0, concat_axis=0, tiled=True)  20.7 us
    pallas_call x3, Pallas kernels, exchange(): pl.pallas_call(functools.partial(exchange_kernel, work, before, sets, own...  19.8 us
    pallas_call x1, Pallas kernels, left_of(): pl.pallas_call(left_kernel, in_specs=[SMEM] * 2 + [VMEM] * 3, out_specs=[...  19.1 us
    all_to_all x1, starting transfers between devices, on_device(): late = lax.all_to_all(late, 'aux', split_axis=0, concat_axis=0, tiled=True)  7.08 us
    all_to_all x1, starting transfers between devices, on_device(): lax.all_to_all(early, 'aux', split_axis=0, concat_axis=0, tiled=True)  6.58 us
    unnamed x21, local copies, waits for them, and re-layouts  4.72 us
  transfers between devices with their start and end apart: 24, of which 10 were waited for; matrix products, arithmetic and copies ran while one was open for 0% of the time, Pallas kernels for 20%

profile of v6, /device:TPU:1, one launch (start us, length us, event | category | flops | bytes accessed | tf_op | source)
XLA Modules:
  0.0 177.2 jit_solution(16177225774188150670)
XLA Ops:
  0.9 3.3 %collective-permute-start = (bf16[16,128]{1,0:T(8,128)(2,1)S(1)}, bf16[16,128]{1,0:T(8,128)(2,1)S(1)}, u32[]{:S(2)}, u32[]{:S(2)}) collective-permute-start(bf16[16,128]{1,0:T(8,128)(2,1)S(1)} %broadcast_in_dim.2.wanted_ref), channel_id=1, source_target_pairs={{0,1},{1,0},{2,3},{3,2},{4,5},{5,4},{6,7},{7,6},{8,9},{9,8},{10,11... | collective-permute-start | bytes 12296 | tf_op jit(solution)/shard_map/ppermute | solution.py:493
  7.7 2.7 %collective-permute-start.2 = (bf16[8,528,128]{2,1,0:T(8,128)(2,1)S(1)}, bf16[8,528,128]{2,1,0:T(8,128)(2,1)S(1)}, u32[]{:S(2)}, u32[]{:S(2)}) collective-permute-start(bf16[8,528,128]{2,1,0:T(8,128)(2,1)S(1)} %get-tuple-element.30.first_ref.refs_0_), channel_id=1, source_target_pairs={{0,24},{1,25},{2,26},{3,27},{4,28},{5,29},{6,30},{7,31},{8,0},{9,1... | collective-permute-start | bytes 3244040 | tf_op jit(solution)/shard_map/ppermute | solution.py:493
  10.3 2.7 %collective-permute-start.4 = (bf16[8,528,128]{2,1,0:T(8,128)(2,1)S(1)}, bf16[8,528,128]{2,1,0:T(8,128)(2,1)S(1)}, u32[]{:S(2)}, u32[]{:S(2)}) collective-permute-start(bf16[8,528,128]{2,1,0:T(8,128)(2,1)S(1)} %get-tuple-element.31.second_ref.refs_5_), channel_id=1, source_target_pairs={{0,6},{1,7},{2,0},{3,1},{4,2},{5,3},{6,4},{7,5},{8,14},{9,15},{10,... | collective-permute-start | bytes 3244040 | tf_op jit(solution)/shard_map/ppermute | solution.py:493
  15.3 19.1 %left.1 = (bf16[136,2,320,512]{3,2,1,0:T(8,128)(2,1)}, bf16[8,2,16,128]{3,2,1,0:T(8,128)(2,1)S(1)}) custom-call(s32[136]{0:T(256)S(1)} %and_select_fusion.1.left_index, s32[136]{0:T(256)S(1)} %get-tuple-element.56.right_index, bf16[8,528,128]{2,1,0:T(8,128)(2,1)S(1)} %get-tuple-element.30.first_ref.refs_0_, ...), custom_call_target="tpu_custom_call" | custom-call | tf_op jit(solution)/shard_map/left/pallas_call | solution.py:259
  36.2 2.7 %collective-permute-start.6 = (bf16[4,528,128]{2,1,0:T(8,128)(2,1)S(1)}, bf16[4,528,128]{2,1,0:T(8,128)(2,1)S(1)}, u32[]{:S(2)}, u32[]{:S(2)}) collective-permute-start(bf16[4,528,128]{2,1,0:T(8,128)(2,1)S(1)} %get-tuple-element.35), channel_id=1, source_target_pairs={{0,24},{1,25},{2,26},{3,27},{4,28},{5,29},{6,30},{7,31},{8,0},{9,1... | collective-permute-start | bytes 1622024 | tf_op jit(solution)/shard_map/ppermute | solution.py:493
  38.9 2.7 %collective-permute-start.8 = (bf16[4,528,128]{2,1,0:T(8,128)(2,1)S(1)}, bf16[4,528,128]{2,1,0:T(8,128)(2,1)S(1)}, u32[]{:S(2)}, u32[]{:S(2)}) collective-permute-start(bf16[4,528,128]{2,1,0:T(8,128)(2,1)S(1)} %get-tuple-element.37), channel_id=1, source_target_pairs={{0,6},{1,7},{2,0},{3,1},{4,2},{5,3},{6,4},{7,5},{8,14},{9,15},{10,... | collective-permute-start | bytes 1622024 | tf_op jit(solution)/shard_map/ppermute | solution.py:493
  41.6 7.8 %collective-permute-done.5.refs_3_ = bf16[4,528,128]{2,1,0:T(8,128)(2,1)S(1)} collective-permute-done((bf16[4,528,128]{2,1,0:T(8,128)(2,1)S(1)}, bf16[4,528,128]{2,1,0:T(8,128)(2,1)S(1)}, u32[]{:S(2)}, u32[]{:S(2)}) %collective-permute-start.5) | collective-permute-done | bytes 540704 | tf_op jit(solution)/shard_map/ppermute | solution.py:493
  53.0 3.4 %collective-permute-start.13 = (bf16[8,512,128]{2,1,0:T(8,128)(2,1)S(1)}, bf16[8,512,128]{2,1,0:T(8,128)(2,1)S(1)}, u32[]{:S(2)}, u32[]{:S(2)}) collective-permute-start(bf16[8,512,128]{2,1,0:T(8,128)(2,1)S(1)} %get-tuple-element.44), channel_id=1, source_target_pairs={{0,1},{1,0},{2,3},{3,2},{4,5},{5,4},{6,7},{7,6},{8,9},{9,8},{10,11... | collective-permute-start | bytes 3145736 | tf_op jit(solution)/shard_map/ppermute | solution.py:493
  56.4 2.7 %collective-permute-start.11 = (bf16[4,512,128]{2,1,0:T(8,128)(2,1)S(1)}, bf16[4,512,128]{2,1,0:T(8,128)(2,1)S(1)}, u32[]{:S(2)}, u32[]{:S(2)}) collective-permute-start(bf16[4,512,128]{2,1,0:T(8,128)(2,1)S(1)} %get-tuple-element.40), channel_id=1, source_target_pairs={{0,6},{1,7},{2,0},{3,1},{4,2},{5,3},{6,4},{7,5},{8,14},{9,15},{10,... | collective-permute-start | bytes 1572872 | tf_op jit(solution)/shard_map/ppermute | solution.py:493
  59.1 2.7 %collective-permute-start.12 = (bf16[4,512,128]{2,1,0:T(8,128)(2,1)S(1)}, bf16[4,512,128]{2,1,0:T(8,128)(2,1)S(1)}, u32[]{:S(2)}, u32[]{:S(2)}) collective-permute-start(bf16[4,512,128]{2,1,0:T(8,128)(2,1)S(1)} %get-tuple-element.41), channel_id=1, source_target_pairs={{0,24},{1,25},{2,26},{3,27},{4,28},{5,29},{6,30},{7,31},{8,0},{9,1... | collective-permute-start | bytes 1572872 | tf_op jit(solution)/shard_map/ppermute | solution.py:493
  61.8 2.6 %choose.3 = (bf16[4,512,128]{2,1,0:T(8,128)(2,1)}, bf16[4,512,128]{2,1,0:T(8,128)(2,1)}, bf16[4,512,128]{2,1,0:T(8,128)(2,1)}, bf16[4,512,128]{2,1,0:T(8,128)(2,...) custom-call(bf16[8,528,128]{2,1,0:T(8,128)(2,1)S(1)} %get-tuple-elem, ...), custom_call_target="tpu_custom_call" | custom-call | tf_op jit(solution)/shard_map/choose/pallas_call | solution.py:146
  64.5 6.6 %collective-permute-done.10.refs_1_ = bf16[4,512,128]{2,1,0:T(8,128)(2,1)S(1)} collective-permute-done((bf16[4,512,128]{2,1,0:T(8,128)(2,1)S(1)}, bf16[4,512,128]{2,1,0:T(8,128)(2,1)S(1)}, u32[]{:S(2)}, u32[]{:S(2)}) %collective-permute-start.10) | collective-permute-done | bytes 524320 | tf_op jit(solution)/shard_map/ppermute | solution.py:493
  71.1 2.3 %collective-permute-start.19 = (bf16[4,512,128]{2,1,0:T(8,128)(2,1)}, bf16[4,512,128]{2,1,0:T(8,128)(2,1)S(1)}, u32[]{:S(2)}, u32[]{:S(2)}) collective-permute-start(bf16[4,512,128]{2,1,0:T(8,128)(2,1)} %get-tuple-element.51), channel_id=1, source_target_pairs={{0,4},{1,5},{2,6},{3,7},{4,0},{5,1},{6,2},{7,3},{8,12},{9,13},{10,... | collective-permute-start | bytes 1572872 | tf_op jit(solution)/shard_map/ppermute | solution.py:493
  75.5 7.6 %exchange.3 = (bf16[8,12,16,128]{3,2,1,0:T(8,128)(2,1)S(1)}, f32[8,22,16,128]{3,2,1,0:T(8,128)S(1)}) custom-call(bf16[136,2,320,512]{3,2,1,0:T(8,128)(2,1)} %get-tuple-element.32.left_ref, bf16[4,512,128]{2,1,0:T(8,128)(2,1)S(1)} %collective-permute-done.9.refs_0_, bf16[4,512,128]{2,1,0:T(8,128)(2,1)S(1)} %collective-permute-done.10.refs_1_, ...), custom_call_target="tpu_custom_call" | custom-call | tf_op jit(solution)/shard_map/exchange/pallas_call | solution.py:373
  84.0 6.6 %all-to-all-start = ((bf16[8,12,16,128]{3,2,1,0:T(8,128)(2,1)}), bf16[8,12,16,128]{3,2,1,0:T(8,128)(2,1)S(1)}, u32[]{:S(2)}, u32[]{:S(2)}) async-start(bf16[8,12,16,128]{3,2,1,0:T(8,128)(2,1)} %copy-done.2), calls=%async_computation | async-start | bytes 786432 | tf_op jit(solution)/shard_map/all_to_all | solution.py:556
  90.5 23.6 %collective-permute-start.14 = (bf16[4,512,128]{2,1,0:T(8,128)(2,1)}, bf16[4,512,128]{2,1,0:T(8,128)(2,1)}, u32[]{:S(2)}, u32[]{:S(2)}) collective-permute-start(bf16[4,512,128]{2,1,0:T(8,128)(2,1)} %copy-done.8), channel_id=1, source_target_pairs={{0,17},{1,16},{2,19},{3,18},{4,21},{5,20},{6,23},{7,22},{8,25},{9,... | collective-permute-start | bytes 1572872 | tf_op jit(solution)/shard_map/ppermute | solution.py:493
  114.2 3.0 %collective-permute-start.17 = (bf16[4,512,128]{2,1,0:T(8,128)(2,1)}, bf16[4,512,128]{2,1,0:T(8,128)(2,1)}, u32[]{:S(2)}, u32[]{:S(2)}) collective-permute-start(bf16[4,512,128]{2,1,0:T(8,128)(2,1)} %copy-done.5), channel_id=1, source_target_pairs={{0,7},{1,6},{2,1},{3,0},{4,3},{5,2},{6,5},{7,4},{8,15},{9,14},{10,... | collective-permute-start | bytes 1572872 | tf_op jit(solution)/shard_map/ppermute | solution.py:493
  117.2 2.9 %collective-permute-start.18 = (bf16[4,512,128]{2,1,0:T(8,128)(2,1)}, bf16[4,512,128]{2,1,0:T(8,128)(2,1)}, u32[]{:S(2)}, u32[]{:S(2)}) collective-permute-start(bf16[4,512,128]{2,1,0:T(8,128)(2,1)} %copy-done.4), channel_id=1, source_target_pairs={{0,25},{1,24},{2,27},{3,26},{4,29},{5,28},{6,31},{7,30},{8,1},{9,0... | collective-permute-start | bytes 1572872 | tf_op jit(solution)/shard_map/ppermute | solution.py:493
  120.0 3.9 %exchange.4.refs_5_ = f32[8,22,16,128]{3,2,1,0:T(8,128)S(1)} custom-call(bf16[136,2,320,512]{3,2,1,0:T(8,128)(2,1)} %get-tuple-element.32.left_ref, bf16[4,512,128]{2,1,0:T(8,128)(2,1)S(1)} %collective-permute-done.19.refs_0_, bf16[4,512,128]{2,1,0:T(8,128)(2,1)S(1)} %collective-permute-done.20.refs_1_, ...), custom_call_target="tpu_custom_call" | custom-call | tf_op jit(solution)/shard_map/exchange/pallas_call | solution.py:373
  125.0 4.8 %collective-permute-done.15.refs_1_ = bf16[4,512,128]{2,1,0:T(8,128)(2,1)} collective-permute-done((bf16[4,512,128]{2,1,0:T(8,128)(2,1)}, bf16[4,512,128]{2,1,0:T(8,128)(2,1)}, u32[]{:S(2)}, u32[]{:S(2)}) %collective-permute-start.15) | collective-permute-done | bytes 524320 | tf_op jit(solution)/shard_map/ppermute | solution.py:493
  129.8 8.5 %collective-permute-done.16.refs_2_ = bf16[4,512,128]{2,1,0:T(8,128)(2,1)} collective-permute-done((bf16[4,512,128]{2,1,0:T(8,128)(2,1)}, bf16[4,512,128]{2,1,0:T(8,128)(2,1)}, u32[]{:S(2)}, u32[]{:S(2)}) %collective-permute-start.16) | collective-permute-done | bytes 524320 | tf_op jit(solution)/shard_map/ppermute | solution.py:493
  138.4 8.3 %exchange.5 = bf16[8,22,16,128]{3,2,1,0:T(8,128)(2,1)} custom-call(bf16[136,2,320,512]{3,2,1,0:T(8,128)(2,1)} %get-tuple-element.32.left_ref, bf16[4,512,128]{2,1,0:T(8,128)(2,1)} %collective-permute-done.14.refs_0_, bf16[4,512,128]{2,1,0:T(8,128)(2,1)} %collective-permute-done.15.refs_1_, bf16[4,512,128]{2,1,0:T(8,128)(2,1)} %collective-permute-done.16.refs_2_, ...), custom_call_target="tpu_custom_call" | custom-call | tf_op jit(solution)/shard_map/exchange/pallas_call | solution.py:373
  146.7 7.1 %all-to-all-start.1 = ((bf16[8,22,16,128]{3,2,1,0:T(8,128)(2,1)}), bf16[8,22,16,128]{3,2,1,0:T(8,128)(2,1)S(1)}, u32[]{:S(2)}, u32[]{:S(2)}) async-start(bf16[8,22,16,128]{3,2,1,0:T(8,128)(2,1)} %exchange.5), calls=%async_computation.1 | async-start | bytes 1441792 | tf_op jit(solution)/shard_map/all_to_all | solution.py:563
  155.2 20.7 %all-to-all-done.1.late_ref = bf16[8,22,16,128]{3,2,1,0:T(8,128)(2,1)S(1)} async-done(((bf16[8,22,16,128]{3,2,1,0:T(8,128)(2,1)}), bf16[8,22,16,128]{3,2,1,0:T(8,128)(2,1)S(1)}, u32[]{:S(2)}, u32[]{:S(2)}) %all-to-all-start.1) | async-done | bytes 720928 | tf_op jit(solution)/shard_map/all_to_all | solution.py:563
  (62 shorter events, 18.7 us)
Async XLA Ops:
  0.9 4.2 %collective-permute-start = (bf16[16,128]{1,0:T(8,128)(2,1)S(1)}, bf16[16,128]{1,0:T(8,128)(2,1)S(1)}, u32[]{:S(2)}, u32[]{:S(2)}) collective-permute-start(bf16[16,128]{1,0:T(8,128)(2,1)S(1)} %broadcast_in_dim.2.wanted_ref), channel_id=1, source_target_pairs={{0,1},{1,0},{2,3},{3,2},{4,5},{5,4},{6,7},{7,6},{8,9},{9,8},{10,11... | collective-permute-start | bytes 12296 | tf_op jit(solution)/shard_map/ppermute | solution.py:493
  7.6 26.8 %collective-permute-start.1 = (bf16[8,528,128]{2,1,0:T(8,128)(2,1)S(1)}, bf16[8,528,128]{2,1,0:T(8,128)(2,1)S(1)}, u32[]{:S(2)}, u32[]{:S(2)}) collective-permute-start(bf16[8,528,128]{2,1,0:T(8,128)(2,1)S(1)} %get-tuple-element.30.first_ref.refs_0_), channel_id=1, source_target_pairs={{0,8},{1,9},{2,10},{3,11},{4,12},{5,13},{6,14},{7,15},{8,16},{9,17... | collective-permute-start | bytes 3244040 | tf_op jit(solution)/shard_map/ppermute | solution.py:493
  7.7 26.8 %collective-permute-start.2 = (bf16[8,528,128]{2,1,0:T(8,128)(2,1)S(1)}, bf16[8,528,128]{2,1,0:T(8,128)(2,1)S(1)}, u32[]{:S(2)}, u32[]{:S(2)}) collective-permute-start(bf16[8,528,128]{2,1,0:T(8,128)(2,1)S(1)} %get-tuple-element.30.first_ref.refs_0_), channel_id=1, source_target_pairs={{0,24},{1,25},{2,26},{3,27},{4,28},{5,29},{6,30},{7,31},{8,0},{9,1... | collective-permute-start | bytes 3244040 | tf_op jit(solution)/shard_map/ppermute | solution.py:493
  10.3 25.7 %collective-permute-start.3 = (bf16[8,528,128]{2,1,0:T(8,128)(2,1)S(1)}, bf16[8,528,128]{2,1,0:T(8,128)(2,1)S(1)}, u32[]{:S(2)}, u32[]{:S(2)}) collective-permute-start(bf16[8,528,128]{2,1,0:T(8,128)(2,1)S(1)} %get-tuple-element.31.second_ref.refs_5_), channel_id=1, source_target_pairs={{0,2},{1,3},{2,4},{3,5},{4,6},{5,7},{6,0},{7,1},{8,10},{9,11},{10,... | collective-permute-start | bytes 3244040 | tf_op jit(solution)/shard_map/ppermute | solution.py:493
  10.3 25.7 %collective-permute-start.4 = (bf16[8,528,128]{2,1,0:T(8,128)(2,1)S(1)}, bf16[8,528,128]{2,1,0:T(8,128)(2,1)S(1)}, u32[]{:S(2)}, u32[]{:S(2)}) collective-permute-start(bf16[8,528,128]{2,1,0:T(8,128)(2,1)S(1)} %get-tuple-element.31.second_ref.refs_5_), channel_id=1, source_target_pairs={{0,6},{1,7},{2,0},{3,1},{4,2},{5,3},{6,4},{7,5},{8,14},{9,15},{10,... | collective-permute-start | bytes 3244040 | tf_op jit(solution)/shard_map/ppermute | solution.py:493
  36.2 13.2 %collective-permute-start.5 = (bf16[4,528,128]{2,1,0:T(8,128)(2,1)S(1)}, bf16[4,528,128]{2,1,0:T(8,128)(2,1)S(1)}, u32[]{:S(2)}, u32[]{:S(2)}) collective-permute-start(bf16[4,528,128]{2,1,0:T(8,128)(2,1)S(1)} %get-tuple-element.34), channel_id=1, source_target_pairs={{0,8},{1,9},{2,10},{3,11},{4,12},{5,13},{6,14},{7,15},{8,16},{9,17... | collective-permute-start | bytes 1622024 | tf_op jit(solution)/shard_map/ppermute | solution.py:493
  36.2 13.2 %collective-permute-start.6 = (bf16[4,528,128]{2,1,0:T(8,128)(2,1)S(1)}, bf16[4,528,128]{2,1,0:T(8,128)(2,1)S(1)}, u32[]{:S(2)}, u32[]{:S(2)}) collective-permute-start(bf16[4,528,128]{2,1,0:T(8,128)(2,1)S(1)} %get-tuple-element.35), channel_id=1, source_target_pairs={{0,24},{1,25},{2,26},{3,27},{4,28},{5,29},{6,30},{7,31},{8,0},{9,1... | collective-permute-start | bytes 1622024 | tf_op jit(solution)/shard_map/ppermute | solution.py:493
  38.9 12.6 %collective-permute-start.7 = (bf16[4,528,128]{2,1,0:T(8,128)(2,1)S(1)}, bf16[4,528,128]{2,1,0:T(8,128)(2,1)S(1)}, u32[]{:S(2)}, u32[]{:S(2)}) collective-permute-start(bf16[4,528,128]{2,1,0:T(8,128)(2,1)S(1)} %get-tuple-element.36), channel_id=1, source_target_pairs={{0,2},{1,3},{2,4},{3,5},{4,6},{5,7},{6,0},{7,1},{8,10},{9,11},{10,... | collective-permute-start | bytes 1622024 | tf_op jit(solution)/shard_map/ppermute | solution.py:493
  38.9 12.6 %collective-permute-start.8 = (bf16[4,528,128]{2,1,0:T(8,128)(2,1)S(1)}, bf16[4,528,128]{2,1,0:T(8,128)(2,1)S(1)}, u32[]{:S(2)}, u32[]{:S(2)}) collective-permute-start(bf16[4,528,128]{2,1,0:T(8,128)(2,1)S(1)} %get-tuple-element.37), channel_id=1, source_target_pairs={{0,6},{1,7},{2,0},{3,1},{4,2},{5,3},{6,4},{7,5},{8,14},{9,15},{10,... | collective-permute-start | bytes 1622024 | tf_op jit(solution)/shard_map/ppermute | solution.py:493
  53.0 22.5 %collective-permute-start.13 = (bf16[8,512,128]{2,1,0:T(8,128)(2,1)S(1)}, bf16[8,512,128]{2,1,0:T(8,128)(2,1)S(1)}, u32[]{:S(2)}, u32[]{:S(2)}) collective-permute-start(bf16[8,512,128]{2,1,0:T(8,128)(2,1)S(1)} %get-tuple-element.44), channel_id=1, source_target_pairs={{0,1},{1,0},{2,3},{3,2},{4,5},{5,4},{6,7},{7,6},{8,9},{9,8},{10,11... | collective-permute-start | bytes 3145736 | tf_op jit(solution)/shard_map/ppermute | solution.py:493
  56.4 14.7 %collective-permute-start.10 = (bf16[4,512,128]{2,1,0:T(8,128)(2,1)S(1)}, bf16[4,512,128]{2,1,0:T(8,128)(2,1)S(1)}, u32[]{:S(2)}, u32[]{:S(2)}) collective-permute-start(bf16[4,512,128]{2,1,0:T(8,128)(2,1)S(1)} %get-tuple-element.39), channel_id=1, source_target_pairs={{0,8},{1,9},{2,10},{3,11},{4,12},{5,13},{6,14},{7,15},{8,16},{9,17... | collective-permute-start | bytes 1572872 | tf_op jit(solution)/shard_map/ppermute | solution.py:493
  56.4 17.0 %collective-permute-start.11 = (bf16[4,512,128]{2,1,0:T(8,128)(2,1)S(1)}, bf16[4,512,128]{2,1,0:T(8,128)(2,1)S(1)}, u32[]{:S(2)}, u32[]{:S(2)}) collective-permute-start(bf16[4,512,128]{2,1,0:T(8,128)(2,1)S(1)} %get-tuple-element.40), channel_id=1, source_target_pairs={{0,6},{1,7},{2,0},{3,1},{4,2},{5,3},{6,4},{7,5},{8,14},{9,15},{10,... | collective-permute-start | bytes 1572872 | tf_op jit(solution)/shard_map/ppermute | solution.py:493
  59.1 14.4 %collective-permute-start.12 = (bf16[4,512,128]{2,1,0:T(8,128)(2,1)S(1)}, bf16[4,512,128]{2,1,0:T(8,128)(2,1)S(1)}, u32[]{:S(2)}, u32[]{:S(2)}) collective-permute-start(bf16[4,512,128]{2,1,0:T(8,128)(2,1)S(1)} %get-tuple-element.41), channel_id=1, source_target_pairs={{0,24},{1,25},{2,26},{3,27},{4,28},{5,29},{6,30},{7,31},{8,0},{9,1... | collective-permute-start | bytes 1572872 | tf_op jit(solution)/shard_map/ppermute | solution.py:493
  61.8 13.7 %collective-permute-start.9 = (bf16[4,512,128]{2,1,0:T(8,128)(2,1)S(1)}, bf16[4,512,128]{2,1,0:T(8,128)(2,1)S(1)}, u32[]{:S(2)}, u32[]{:S(2)}) collective-permute-start(bf16[4,512,128]{2,1,0:T(8,128)(2,1)S(1)} %get-tuple-element.38), channel_id=1, source_target_pairs={{0,2},{1,3},{2,4},{3,5},{4,6},{5,7},{6,0},{7,1},{8,10},{9,11},{10,... | collective-permute-start | bytes 1572872 | tf_op jit(solution)/shard_map/ppermute | solution.py:493
  71.1 43.0 %collective-permute-start.19 = (bf16[4,512,128]{2,1,0:T(8,128)(2,1)}, bf16[4,512,128]{2,1,0:T(8,128)(2,1)S(1)}, u32[]{:S(2)}, u32[]{:S(2)}) collective-permute-start(bf16[4,512,128]{2,1,0:T(8,128)(2,1)} %get-tuple-element.51), channel_id=1, source_target_pairs={{0,4},{1,5},{2,6},{3,7},{4,0},{5,1},{6,2},{7,3},{8,12},{9,13},{10,... | collective-permute-start | bytes 1572872 | tf_op jit(solution)/shard_map/ppermute | solution.py:493
  73.4 40.8 %collective-permute-start.20 = (bf16[4,512,128]{2,1,0:T(8,128)(2,1)}, bf16[4,512,128]{2,1,0:T(8,128)(2,1)S(1)}, u32[]{:S(2)}, u32[]{:S(2)}) collective-permute-start(bf16[4,512,128]{2,1,0:T(8,128)(2,1)} %get-tuple-element.52), channel_id=1, source_target_pairs={{0,16},{1,17},{2,18},{3,19},{4,20},{5,21},{6,22},{7,23},{8,24},{9,... | collective-permute-start | bytes 1572872 | tf_op jit(solution)/shard_map/ppermute | solution.py:493
  73.4 43.7 %collective-permute-start.21 = (bf16[4,512,128]{2,1,0:T(8,128)(2,1)}, bf16[4,512,128]{2,1,0:T(8,128)(2,1)S(1)}, u32[]{:S(2)}, u32[]{:S(2)}) collective-permute-start(bf16[4,512,128]{2,1,0:T(8,128)(2,1)} %get-tuple-element.53), channel_id=1, source_target_pairs={{0,5},{1,4},{2,7},{3,6},{4,1},{5,0},{6,3},{7,2},{8,13},{9,12},{10,... | collective-permute-start | bytes 1572872 | tf_op jit(solution)/shard_map/ppermute | solution.py:493
  84.0 36.1 %all-to-all-start = ((bf16[8,12,16,128]{3,2,1,0:T(8,128)(2,1)}), bf16[8,12,16,128]{3,2,1,0:T(8,128)(2,1)S(1)}, u32[]{:S(2)}, u32[]{:S(2)}) async-start(bf16[8,12,16,128]{3,2,1,0:T(8,128)(2,1)} %copy-done.2), calls=%async_computation | async-start | bytes 786432 | tf_op jit(solution)/shard_map/all_to_all | solution.py:556
  90.5 34.5 %collective-permute-start.14 = (bf16[4,512,128]{2,1,0:T(8,128)(2,1)}, bf16[4,512,128]{2,1,0:T(8,128)(2,1)}, u32[]{:S(2)}, u32[]{:S(2)}) collective-permute-start(bf16[4,512,128]{2,1,0:T(8,128)(2,1)} %copy-done.8), channel_id=1, source_target_pairs={{0,17},{1,16},{2,19},{3,18},{4,21},{5,20},{6,23},{7,22},{8,25},{9,... | collective-permute-start | bytes 1572872 | tf_op jit(solution)/shard_map/ppermute | solution.py:493
  114.1 15.7 %collective-permute-start.15 = (bf16[4,512,128]{2,1,0:T(8,128)(2,1)}, bf16[4,512,128]{2,1,0:T(8,128)(2,1)}, u32[]{:S(2)}, u32[]{:S(2)}) collective-permute-start(bf16[4,512,128]{2,1,0:T(8,128)(2,1)} %copy-done.7), channel_id=1, source_target_pairs={{0,3},{1,2},{2,5},{3,4},{4,7},{5,6},{6,1},{7,0},{8,11},{9,10},{10,... | collective-permute-start | bytes 1572872 | tf_op jit(solution)/shard_map/ppermute | solution.py:493
  114.1 24.3 %collective-permute-start.16 = (bf16[4,512,128]{2,1,0:T(8,128)(2,1)}, bf16[4,512,128]{2,1,0:T(8,128)(2,1)}, u32[]{:S(2)}, u32[]{:S(2)}) collective-permute-start(bf16[4,512,128]{2,1,0:T(8,128)(2,1)} %copy-done.6), channel_id=1, source_target_pairs={{0,9},{1,8},{2,11},{3,10},{4,13},{5,12},{6,15},{7,14},{8,17},{9,16... | collective-permute-start | bytes 1572872 | tf_op jit(solution)/shard_map/ppermute | solution.py:493
  114.2 24.2 %collective-permute-start.17 = (bf16[4,512,128]{2,1,0:T(8,128)(2,1)}, bf16[4,512,128]{2,1,0:T(8,128)(2,1)}, u32[]{:S(2)}, u32[]{:S(2)}) collective-permute-start(bf16[4,512,128]{2,1,0:T(8,128)(2,1)} %copy-done.5), channel_id=1, source_target_pairs={{0,7},{1,6},{2,1},{3,0},{4,3},{5,2},{6,5},{7,4},{8,15},{9,14},{10,... | collective-permute-start | bytes 1572872 | tf_op jit(solution)/shard_map/ppermute | solution.py:493
  117.2 21.2 %collective-permute-start.18 = (bf16[4,512,128]{2,1,0:T(8,128)(2,1)}, bf16[4,512,128]{2,1,0:T(8,128)(2,1)}, u32[]{:S(2)}, u32[]{:S(2)}) collective-permute-start(bf16[4,512,128]{2,1,0:T(8,128)(2,1)} %copy-done.4), channel_id=1, source_target_pairs={{0,25},{1,24},{2,27},{3,26},{4,29},{5,28},{6,31},{7,30},{8,1},{9,0... | collective-permute-start | bytes 1572872 | tf_op jit(solution)/shard_map/ppermute | solution.py:493
  146.7 29.2 %all-to-all-start.1 = ((bf16[8,22,16,128]{3,2,1,0:T(8,128)(2,1)}), bf16[8,22,16,128]{3,2,1,0:T(8,128)(2,1)S(1)}, u32[]{:S(2)}, u32[]{:S(2)}) async-start(bf16[8,22,16,128]{3,2,1,0:T(8,128)(2,1)} %exchange.5), calls=%async_computation.1 | async-start | bytes 1441792 | tf_op jit(solution)/shard_map/all_to_all | solution.py:563
  (10 other events, 112.6 us)
